TPU v7x, 256 devices: a whole 4x4x8 slice. The times are simulated.
256 devices in a mesh: facet: 16 (over y_lo, x, core), chan: 16 (over z, y_hi).
Axes of the slice: x: 4, y: 4 (y_hi: 2, y_lo: 2; y = y_hi * 2 + y_lo), z: 8, core: 2. Of those that a mesh axis runs over, the one named last changes fastest.
Arguments:
- sky_image: float32 [256, 512, 512], P('chan', 'facet')
- margins: int32 [16], replicated, may hold values from 1 to 7, as said below
- wavelet_dual: float32 [4, 256, 512, 512], P(None, 'chan', 'facet'), may hold values from -2.5 to 2.5
- sparsity_weights: float32 [4, 512, 512], P(None, 'facet'), may hold values from 0.25 to 4
- lowrank_dual: float32 [256, 512, 512], P(None, 'facet', 'chan'), may hold values from -6 to 6
- kernel_weights: bfloat16 [16, 32, 32, 512], P('chan'), may hold values from -0.25 to 0.25
- tile_index: int32 [16, 32], P('chan'), may hold values from 1 to 1023
- data_dual: float32 [256, 2, 1024], P(('chan', 'facet')), may hold values from -6 to 6
- visibilities: float32 [256, 2, 1024], P(('chan', 'facet')), may hold values from -6 to 6
- radius_scale: float32 [256], P(('chan', 'facet')), may hold values from 0.5 to 8
Outputs:
- wavelet_next: float32 [4, 256, 512, 512], P(None, 'chan', 'facet')
- lowrank_next: float32 [256, 512, 512], P(None, 'facet', 'chan')
- data_next: float32 [256, 2, 1024], P(('chan', 'facet'))
Inputs may be any that keep to these rules, and one draw needn't show every extreme that they name: `margins`: some facet other than the first has margin 7.
All inputs are finite; a program needn't handle non-finite values.
Results may differ from a plain program's by a relative error of at most 0.0003.
Values sent between devices are 32-bit elements; how exact they have to be, the bound alone decides.
No kernel may reach another device: no remote copies, remote signals or barrier semaphores. Data moves between devices by JAX's collectives and lax.ppermute only.
A program may use at most 128 MiB of HBM per device.

v0:
```python
import math

import jax
import jax.numpy as jnp
from jax import lax
from jax.sharding import PartitionSpec as P

NSTEP = 5
KT = 16


highest = lax.Precision.HIGHEST
low_taps = (
    -0.010597401784997278,
    0.032883011666982945,
    0.030841381835986965,
    -0.18703481171888114,
    -0.02798376941698385,
    0.6308807679295904,
    0.7148465705525415,
    0.23037781330885523,
)
high_taps = tuple(((-1.0) ** offset * low_taps[7 - offset] for offset in range(8)))


def shifted_2(value, axis, by):
    devices = lax.axis_size(axis)
    pairs = [(i, i + by) for i in range(devices) if 0 <= i + by < devices]
    return lax.ppermute(value, axis, pairs)


def causal_rows(extended, filter_taps, row_count):
    summed = filter_taps[0] * extended[:, 7 : 7 + row_count, :]
    for offset in range(1, 8):
        summed = summed + filter_taps[offset] * extended[:, 7 - offset : 7 - offset + row_count, :]
    return summed


def column_pass(values, filter_taps):
    col_count = values.shape[-1]
    padded = jnp.pad(values, ((0, 0), (0, 0), (7, 0)))
    summed = filter_taps[0] * values
    for offset in range(1, 8):
        summed = summed + filter_taps[offset] * padded[:, :, 7 - offset : 7 - offset + col_count]
    return summed


def inverse_root(gram, pixel_count):
    size_now = gram.shape[0]
    identity = jnp.eye(size_now, dtype=gram.dtype)
    shifted = identity + gram / pixel_count
    frobenius = jnp.sqrt(jnp.sum(shifted * shifted))
    current = shifted / frobenius
    inverse = identity
    for turn in range(NSTEP):
        middle = 1.5 * identity - 0.5 * jnp.dot(inverse, current, precision=highest)
        current = jnp.dot(current, middle, precision=highest)
        inverse = jnp.dot(middle, inverse, precision=highest)
    return inverse / jnp.sqrt(frobenius)


def dft_tables(image_side):
    counter = jnp.arange(image_side, dtype=jnp.int32)
    phase_index = counter[:, None] * counter[None, :] % image_side
    angles = phase_index.astype(jnp.float32) * (2.0 * math.pi / image_side)
    return (jnp.cos(angles), jnp.sin(angles))


def degrid(real_part, imag_part, kernel_block, tile_ids):
    chan_count = real_part.shape[0]
    image_side = real_part.shape[1]
    tiles_side = image_side // KT

    def to_tiles(values):
        shaped = values.reshape(chan_count, tiles_side, KT, tiles_side, KT).transpose(0, 1, 3, 2, 4)
        return shaped.reshape(chan_count, tiles_side * tiles_side, KT * KT)[:, tile_ids, :]

    picked_real = to_tiles(real_part)
    picked_imag = to_tiles(imag_part)
    stacked = jnp.stack(
        [
            jnp.concatenate([picked_real, -picked_imag], axis=-1),
            jnp.concatenate([picked_imag, picked_real], axis=-1),
        ],
        axis=1,
    )
    predicted = jnp.einsum(
        "bvk,ncbk->ncbv", kernel_block.astype(jnp.float32), stacked, precision=highest
    )
    return predicted.reshape(chan_count, 2, -1)


def data_step(data_dual, forward, visibilities, radius_scale):
    moved = data_dual + forward
    residual = 2.0 * moved - visibilities
    distance = jnp.sqrt(jnp.sum(residual * residual, axis=(1, 2)) + 1e-06)
    radius = radius_scale * math.sqrt(2.0 * visibilities.shape[2])
    shrink = jnp.minimum(1.0, radius / distance)
    return moved - 0.5 * (visibilities + residual * shrink[:, None, None])


def per_device(
    sky_image,
    margins,
    wavelet_dual,
    sparsity_weights,
    lowrank_dual,
    kernel_weights,
    tile_index,
    data_dual,
    visibilities,
    radius_scale,
):
    group_size, facet_rows, image_side = sky_image.shape
    channels = lowrank_dual.shape[0]
    upper_rim = shifted_2(sky_image[:, facet_rows - 7 :, :], "facet", 1)
    facet_margin = margins[lax.axis_index("facet")]
    kept_rows = (jnp.arange(7, dtype=jnp.int32) >= 7 - facet_margin).astype(jnp.float32)
    extended = jnp.concatenate([upper_rim * kept_rows[None, :, None], sky_image], axis=1)
    low_rows = causal_rows(extended, low_taps, facet_rows)
    high_rows = causal_rows(extended, high_taps, facet_rows)
    pairs = (
        (low_rows, low_taps),
        (low_rows, high_taps),
        (high_rows, low_taps),
        (high_rows, high_taps),
    )
    coefficients = jnp.stack(
        [column_pass(filtered, column_taps) for filtered, column_taps in pairs]
    )
    blended_w = wavelet_dual + 0.5 * coefficients
    partial_energy = jnp.sum(blended_w * blended_w, axis=1)
    relayed = lax.all_to_all(sky_image, "chan", split_axis=2, concat_axis=0, tiled=True)
    blended_r = lowrank_dual + 0.5 * relayed
    flattened = blended_r.reshape(channels, -1)
    gram_part = jnp.dot(
        flattened, flattened.T, precision=highest, preferred_element_type=jnp.float32
    )
    cosine, sine = dft_tables(image_side)
    piece = lax.all_to_all(sky_image, "facet", split_axis=0, concat_axis=1, tiled=True)
    cos_part = jnp.einsum("yk,nyc->nkc", cosine, piece, precision=highest)
    sin_part = jnp.einsum("yk,nyc->nkc", sine, piece, precision=highest)
    energy, gram = lax.psum((partial_energy, gram_part), "chan")
    factor = jnp.maximum(1.0, jnp.sqrt(energy / channels) / sparsity_weights)
    wavelet_next = blended_w / factor[:, None]
    mixer = inverse_root(gram, facet_rows * image_side)
    lowrank_next = jnp.dot(
        mixer, flattened, precision=highest, preferred_element_type=jnp.float32
    ).reshape(blended_r.shape)
    real_part = jnp.dot(cos_part, cosine, precision=highest) - jnp.dot(
        sin_part, sine, precision=highest
    )
    imag_part = -jnp.dot(sin_part, cosine, precision=highest) - jnp.dot(
        cos_part, sine, precision=highest
    )
    real_part = real_part / image_side
    imag_part = imag_part / image_side
    forward = degrid(real_part, imag_part, kernel_weights[0], tile_index[0])
    data_next = data_step(data_dual, forward, visibilities, radius_scale)
    return (wavelet_next, lowrank_next, data_next)


def solution(mesh):
    in_specs = (
        P("chan", "facet", None),
        P(),
        P(None, "chan", "facet", None),
        P(None, "facet", None),
        P(None, "facet", "chan"),
        P("chan", None, None, None),
        P("chan", None),
        P(("chan", "facet"), None, None),
        P(("chan", "facet"), None, None),
        P(("chan", "facet")),
    )
    out_specs = (
        P(None, "chan", "facet", None),
        P(None, "facet", "chan"),
        P(("chan", "facet"), None, None),
    )
    return jax.shard_map(
        per_device, mesh=mesh, in_specs=in_specs, out_specs=out_specs, check_vma=False
    )
```

profile of v0, /device:TPU:8, one launch (start us, length us, event | category | flops | bytes accessed | tf_op | source)
XLA Modules:
  0.0 352.0 jit_solution(5887408889784134434)
XLA Ops:
  7.2 0.0 copy-start
  7.2 6.4 %all-to-all-start.1 = ((f32[16,32,512]{2,1,0:T(8,128)}), f32[16,32,512]{2,1,0:T(8,128)}, u32[]{:S(2)}, u32[]{:S(2)}) async-start(f32[16,32,512]{2,1,0:T(8,128)} %param.10), calls=%async_computation.1 | async-start | bytes 2097152 | tf_op jit(solution)/shard_map/all_to_all | solution.py:140
  13.6 1.0 slice.87
  14.6 2.1 collective-permute-start
  16.7 0.7 fusion.44
  17.4 4.6 %copy.51 = f32[16,32,512]{1,0,2:T(8,128)} copy(f32[16,32,512]{2,1,0:T(8,128)} %param.10) | data formatting | bytes 2097152 | tf_op args[0]
  22.7 4.7 %reshape.144 = f32[16,1,16384]{2,1,0:T(1,128)} reshape(f32[512,16,32]{2,1,0:T(8,128)} %bitcast.95) | data formatting | bytes 2097152
  27.5 0.6 dynamic_slice.3
  28.7 2.8 collective-permute-done
  31.5 0.1 broadcast_multiply_fusion.1
  31.6 1.7 multiply_add_fusion.1
  33.4 8.7 %add_bitcast_fusion.1 = (f32[1,16,32,512]{3,2,1,0:T(8,128)S(1)}, f32[1,16,32,512]{3,2,1,0:T(8,128)S(1)}, f32[1,16,32,512]{3,2,1,0:T(8,128)}, f32[1,16,32,512]{3,2,1,0:T(8,128)}) fusion(f32[16,32,512]{2,1,0:T(8,128)S(1)} %get-tuple-element.8, f32[16,32,512]{2,1,0:T(8,128)S(1)} %get-tuple-element.7), kind=kLoop, calls=%fused_computation.71 | loop fusion | flops 15728640 | bytes 6291456 | tf_op jit(solution)/shard_map/stack | solution.py:128
  42.1 9.8 %all-to-all-start = ((f32[16,1,16384]{2,1,0:T(1,128)}), f32[16,1,16384]{2,1,0:T(1,128)}, u32[]{:S(2)}, u32[]{:S(2)}) async-start(f32[16,1,16384]{2,1,0:T(1,128)} %reshape.144), calls=%async_computation | async-start | bytes 2097152 | tf_op jit(solution)/shard_map/all_to_all | solution.py:133
  51.9 0.0 all-reduce.5.cloned.1.call-start
  52.0 4.2 %multiply_reduce_fusion = f32[4,32,512]{2,1,0:T(8,128)} fusion(f32[4,16,32,512]{3,2,1,0:T(8,128)} %param.12, f32[1,16,32,512]{3,2,1,0:T(8,128)S(1)} %get-tuple-element.12, f32[1,16,32,512]{3,2,1,0:T(8,128)S(1)} %get-tuple-element.11, f32[1,16,32,512]{3,2,1,0:T(8,128)} %get-tuple-element.15, f32[1,16,32,512]{3,2,1,0:T(8,128)} %get-tuple-element.16), kind=kLoop, calls=%fused_computation.4 | loop fusion | flops 7274496 | bytes 8650752 | tf_op jit(solution)/shard_map/reduce_sum | solution.py:132
  56.2 6.9 %fusion.33 = f32[512,512]{1,0:T(8,128)S(1)} fusion(f32[512,512]{1,0:T(8,128)} %bitcast.13), kind=kOutput, calls=%fused_computation.81 | convolution fusion | flops 1614282752 | bytes 2097152 | tf_op jit(solution)/shard_map/yk,nyc->nkc/dot_general | solution.py:142
  63.1 7.3 %fusion.29 = f32[512,512]{1,0:T(8,128)S(1)} fusion(f32[512,512]{1,0:T(8,128)} %bitcast.13), kind=kOutput, calls=%fused_computation.80 | convolution fusion | flops 1614282752 | bytes 2097152 | tf_op jit(solution)/shard_map/yk,nyc->nkc/dot_general | solution.py:141
  70.4 6.4 %convolution_negate_fusion = f32[512,512]{1,0:T(8,128)S(1)} fusion(f32[512,512]{1,0:T(8,128)S(1)} %fusion.33), kind=kOutput, calls=%fused_computation.38 | convolution fusion | flops 1614544896 | bytes 2097152 | tf_op jit(solution)/shard_map/dot_general | solution.py:153
  76.9 6.7 %fusion.1 = f32[512,512]{1,0:T(8,128)} fusion(f32[512,512]{1,0:T(8,128)S(1)} %convolution_negate_fusion, f32[512,512]{1,0:T(8,128)S(1)} %fusion.29), kind=kOutput, calls=%fused_computation.37 | convolution fusion | flops 1614807040 | bytes 3145728 | tf_op jit(solution)/shard_map/dot_general | solution.py:153
  83.6 6.2 %reshape.115 = f32[1,32,16,32,16]{4,3,2,1,0:T(8,128)} reshape(f32[512,512]{1,0:T(8,128)} %fusion.1) | data formatting | bytes 2097152 | tf_op jit(solution)/shard_map/reshape | solution.py:75
  89.7 7.2 %copy.56 = f32[1,32,32,16,16]{2,1,4,3,0:T(8,128)} copy(f32[1,32,32,16,16]{4,2,3,1,0:T(8,128)} %bitcast.93) | data formatting | bytes 2097152 | tf_op jit(solution)/shard_map/transpose | solution.py:75
  97.0 4.6 %reshape.129 = f32[1024,256]{0,1:T(8,128)} reshape(f32[1,32,32,16,16]{2,1,4,3,0:T(8,128)} %copy.56) | data formatting | bytes 2097152 | tf_op jit(solution)/shard_map/reshape | solution.py:76
  101.5 2.5 copy.57
  104.1 1.8 gather_fusion.1
  105.9 7.8 %fusion.27 = f32[512,512]{1,0:T(8,128)S(1)} fusion(f32[512,512]{1,0:T(8,128)} %copy-done.14), kind=kOutput, calls=%fused_computation.79 | convolution fusion | flops 1614282752 | bytes 2097152 | tf_op jit(solution)/shard_map/dot_general | solution.py:150
  113.8 6.7 %fusion.2 = f32[512,512]{1,0:T(8,128)} fusion(f32[512,512]{1,0:T(8,128)S(1)} %fusion.27, f32[512,512]{1,0:T(8,128)S(1)} %copy-done.13), kind=kOutput, calls=%fused_computation.40 | convolution fusion | flops 1614807040 | bytes 3145728 | tf_op jit(solution)/shard_map/dot_general | solution.py:150
  120.4 6.2 %reshape.113 = f32[1,32,16,32,16]{4,3,2,1,0:T(8,128)} reshape(f32[512,512]{1,0:T(8,128)} %fusion.2) | data formatting | bytes 2097152 | tf_op jit(solution)/shard_map/reshape | solution.py:75
  126.6 7.2 %copy.54 = f32[1,32,32,16,16]{2,1,4,3,0:T(8,128)} copy(f32[1,32,32,16,16]{4,2,3,1,0:T(8,128)} %bitcast.94) | data formatting | bytes 2097152 | tf_op jit(solution)/shard_map/transpose | solution.py:75
  133.8 5.0 %reshape.119 = f32[1024,256]{0,1:T(8,128)} reshape(f32[1,32,32,16,16]{2,1,4,3,0:T(8,128)} %copy.54) | data formatting | bytes 2097152 | tf_op jit(solution)/shard_map/reshape | solution.py:76
  138.9 2.5 copy.55
  141.4 1.8 gather_fusion
  143.3 0.1 maximum_bitcast_fusion.2
  143.4 0.5 broadcast.199
  143.9 5.4 %reduce.1 = f32[16,16384]{1,0:T(8,128)} reduce(f32[16,1,16384]{2,1,0:T(1,128)} %all-to-all-done, f32[]{:T(128)} %broadcast.199), dimensions={1}, to_apply=%all_to_all.4.reduce_sub_computation | reduce | bytes 2097156 | tf_op jit(solution)/shard_map/all_to_all | solution.py:133
  149.3 3.8 %reshape.145 = f32[512,16,32]{2,1,0:T(8,128)} reshape(f32[16,16384]{1,0:T(8,128)} %reduce.1) | data formatting | bytes 2097152
  153.1 4.5 %broadcast_multiply_fusion = f32[16,32,512]{1,0,2:T(8,128)} fusion(f32[512,16,32]{2,1,0:T(8,128)} %reshape.145), kind=kLoop, calls=%fused_computation.11 | loop fusion | flops 262144 | bytes 2097152 | tf_op jit(solution)/shard_map/mul | solution.py:134
  157.5 5.5 %copy.52 = f32[16,32,16,32]{3,1,0,2:T(8,128)} copy(f32[16,32,16,32]{1,0,3,2:T(8,128)} %bitcast.97) | data formatting | bytes 2097152 | tf_op jit(solution)/shard_map/mul | solution.py:134
  163.1 4.5 %copy.53 = f32[256,32,32]{0,2,1:T(8,128)} copy(f32[256,32,32]{2,1,0:T(8,128)} %bitcast.96) | data formatting | bytes 2097152 | tf_op jit(solution)/shard_map/mul | solution.py:134
  167.6 4.8 %convolution_bitcast_fusion = f32[256,256]{1,0:T(8,128)} fusion(f32[256,32,32]{0,2,1:T(8,128)} %param.14, f32[256,32,32]{0,2,1:T(8,128)} %copy.53), kind=kOutput, calls=%fused_computation.53 | convolution fusion | flops 805568512 | bytes 2359296 | tf_op jit(solution)/shard_map/dot_general | solution.py:136
  172.3 0.0 all-reduce.5.cloned.1.call-update
  172.4 0.9 convolution_bitcast_fusion.1
  173.3 0.1 reshape.118
  173.4 0.6 multiply_reduce_fusion.2
  174.7 0.6 multiply_subtract_fusion
  175.4 155.2 %all-reduce.5.cloned.1.call-done = (f32[4,32,512]{2,1,0:T(8,128)}, f32[256,256]{1,0:T(8,128)}) async-done(((f32[4,32,512]{2,1,0:T(8,128)}, f32[256,256]{1,0:T(8,128)}), (f32[4,32,512]{2,1,0:T(8,128)}, f32[256,256]{1,0:T(8,128)})) %all-reduce.5.cloned.1.call-update) | async-done | bytes 524304 | tf_op jit(solution)/shard_map/psum | solution.py:143
  330.6 1.6 multiply_reduce_fusion.1
  332.9 1.3 fusion.8
  334.2 0.0 copy-start.7
  334.3 1.4 fusion.41
  335.7 0.3 fusion.37
  336.0 0.4 fusion.7
  336.4 0.4 fusion.73
  336.8 0.4 fusion.72
  337.1 0.4 fusion.6
  337.5 0.4 fusion.75
  337.9 0.4 fusion.74
  338.3 0.4 fusion.5
  338.7 0.4 fusion.76
  339.1 0.4 fusion.77
  339.5 0.1 divide_maximum_fusion
  339.7 2.6 broadcast_divide_fusion
  342.2 0.4 fusion.4
  342.6 0.4 fusion.3
  343.0 2.0 fusion.18
  (36 shorter events, 0.2 us)
Async XLA Ops:
  7.2 165.2 %copy-start = (bf16[1,32,32,512]{3,2,1,0:T(8,128)(2,1)S(1)}, bf16[1,32,32,512]{3,2,1,0:T(8,128)(2,1)}, u32[]{:S(2)}) copy-start(bf16[1,32,32,512]{3,2,1,0:T(8,128)(2,1)} %param.15) | copy-start | bytes 3145732
  7.2 34.9 %all-to-all-start.1 = ((f32[16,32,512]{2,1,0:T(8,128)}), f32[16,32,512]{2,1,0:T(8,128)}, u32[]{:S(2)}, u32[]{:S(2)}) async-start(f32[16,32,512]{2,1,0:T(8,128)} %param.10), calls=%async_computation.1 | async-start | bytes 2097152 | tf_op jit(solution)/shard_map/all_to_all | solution.py:140
  14.6 16.9 %collective-permute-start = (f32[16,7,512]{2,1,0:T(8,128)S(1)}, f32[16,7,512]{2,1,0:T(8,128)S(1)}, u32[]{:S(2)}, u32[]{:S(2)}) collective-permute-start(f32[16,7,512]{2,1,0:T(8,128)S(1)} %slice.87), channel_id=1, source_target_pairs={{0,16},{16,32},{32,48},{48,64},{64,80},{80,96},{96,112},{112,128},... | collective-permute-start | bytes 688136 | tf_op jit(solution)/shard_map/ppermute | solution.py:29
  17.4 10.1 %copy-start.11 = (s32[16]{0:T(128)S(1)}, s32[16]{0:T(128)}, u32[]{:S(2)}) copy-start(s32[16]{0:T(128)} %param.11) | copy-start | bytes 196
  22.0 9.6 %copy-start.2 = (f32[16,32,512]{2,1,0:T(8,128)S(1)}, f32[16,32,512]{2,1,0:T(8,128)}, u32[]{:S(2)}) copy-start(f32[16,32,512]{2,1,0:T(8,128)} %param.10) | copy-start | bytes 3145732
  42.1 101.3 %all-to-all-start = ((f32[16,1,16384]{2,1,0:T(1,128)}), f32[16,1,16384]{2,1,0:T(1,128)}, u32[]{:S(2)}, u32[]{:S(2)}) async-start(f32[16,1,16384]{2,1,0:T(1,128)} %reshape.144), calls=%async_computation | async-start | bytes 2097152 | tf_op jit(solution)/shard_map/all_to_all | solution.py:133
  51.9 278.6 %all-reduce.5.cloned.1.call-start = ((), (), s32[]{:S(2)}) async-start(), calls=%async_computation.2 | async-start | bytes 1048576 | tf_op jit(solution)/shard_map/psum | solution.py:143
  63.1 13.7 %copy-start.12 = (f32[512,512]{1,0:T(8,128)}, f32[512,512]{1,0:T(8,128)S(1)}, u32[]{:S(2)}) copy-start(f32[512,512]{1,0:T(8,128)S(1)} %fusion.33) | copy-start | bytes 3145732
  70.4 6.5 %copy-start.14 = (f32[512,512]{1,0:T(8,128)}, f32[512,512]{1,0:T(8,128)S(1)}, u32[]{:S(2)}) copy-start(f32[512,512]{1,0:T(8,128)S(1)} %fusion.29) | copy-start | bytes 3145732
  105.9 7.9 %copy-start.13 = (f32[512,512]{1,0:T(8,128)S(1)}, f32[512,512]{1,0:T(8,128)}, u32[]{:S(2)}) copy-start(f32[512,512]{1,0:T(8,128)} %copy-done.12) | copy-start | bytes 3145732
  167.6 5.9 %copy-start.9 = (f32[1,2,1024]{2,1,0:T(2,128)S(1)}, f32[1,2,1024]{2,1,0:T(2,128)}, u32[]{:S(2)}) copy-start(f32[1,2,1024]{2,1,0:T(2,128)} %param.18) | copy-start | bytes 24580
  167.6 5.9 %copy-start.10 = (f32[1,2,1024]{2,1,0:T(2,128)S(1)}, f32[1,2,1024]{2,1,0:T(2,128)}, u32[]{:S(2)}) copy-start(f32[1,2,1024]{2,1,0:T(2,128)} %param.17) | copy-start | bytes 24580
  334.2 5.2 %copy-start.7 = (f32[4,32,512]{2,1,0:T(8,128)S(1)}, f32[4,32,512]{2,1,0:T(8,128)}, u32[]{:S(2)}) copy-start(f32[4,32,512]{2,1,0:T(8,128)} %param.13) | copy-start | bytes 786436
  334.2 5.2 %copy-start.8 = (f32[4,32,512]{2,1,0:T(8,128)S(1)}, f32[4,32,512]{2,1,0:T(8,128)}, u32[]{:S(2)}) copy-start(f32[4,32,512]{2,1,0:T(8,128)} %get-tuple-element.3) | copy-start | bytes 786436
  335.7 3.9 %copy-start.1 = (f32[4,16,32,512]{3,2,1,0:T(8,128)S(1)}, f32[4,16,32,512]{3,2,1,0:T(8,128)}, u32[]{:S(2)}) copy-start(f32[4,16,32,512]{3,2,1,0:T(8,128)} %param.12) | copy-start | bytes 12582916
  335.7 3.9 %copy-start.3 = (f32[1,16,32,512]{3,2,1,0:T(8,128)S(1)}, f32[1,16,32,512]{3,2,1,0:T(8,128)}, u32[]{:S(2)}) copy-start(f32[1,16,32,512]{3,2,1,0:T(8,128)} %get-tuple-element.15) | copy-start | bytes 3145732
  335.7 3.9 %copy-start.4 = (f32[1,16,32,512]{3,2,1,0:T(8,128)S(1)}, f32[1,16,32,512]{3,2,1,0:T(8,128)}, u32[]{:S(2)}) copy-start(f32[1,16,32,512]{3,2,1,0:T(8,128)} %get-tuple-element.16) | copy-start | bytes 3145732
  339.6 3.4 copy-start.5
  339.6 3.4 copy-start.6
Sparse Core Ops, SparseCore 0:
  172.5 158.0 all-reduce.4
where the time goes:
time: 359 us; the launch traced here: 352 us
  waiting for transfers between devices  158 us (44%)
  local copies, waits for them, and re-layouts  70.6 us (20%)
  matrix products  56.6 us (16%)
  other arithmetic  30.9 us (9%)
  starting transfers between devices  18.4 us (5%)
  between operations  17.5 us (5%)
    psum x1, waiting for transfers between devices, per_device(): energy, gram = lax.psum((partial_energy, gram_part), 'chan')  155 us
    reshape x4, local copies, waits for them, and re-layouts, to_tiles(): shaped.reshape(chan_count, tiles_side * tiles_side, KT * KT)[:, tile_ids, :]  14.7 us
    transpose x2, local copies, waits for them, and re-layouts, to_tiles(): values.reshape(chan_count, tiles_side, KT, tiles_side, KT)  14.4 us
    unnamed x33, local copies, waits for them, and re-layouts  13.2 us
    reshape x2, local copies, waits for them, and re-layouts, to_tiles(): values.reshape(chan_count, tiles_side, KT, tiles_side, KT)  12.3 us
    mul x2, local copies, waits for them, and re-layouts, per_device(): blended_r = lowrank_dual + 0.5 * relayed  10 us
    all_to_all x1, starting transfers between devices, per_device(): lax.all_to_all(sky_image, 'chan', split_axis=2, concat_axis=0, tiled=True)  9.85 us
    another operation x1, other arithmetic, per_device(): jnp.stack([column_pass(filtered, column_taps) for filtered, column_taps i...  8.72 us
  transfers between devices with their start and end apart: 4, of which 2 were waited for; matrix products, arithmetic and copies ran while one was open for 33% of the time, Pallas kernels for 0%

commit v1 on v0

v1 whole, which is shorter than its diff:
```python
import math

import jax
import jax.numpy as jnp
import ml_dtypes
import numpy as np
from jax import lax
from jax.experimental import pallas as pl
from jax.experimental.pallas import tpu as pltpu
from jax.sharding import PartitionSpec as P

NSTEP = 5
KT = 16
MIB = 1 << 20

low_taps = (
    -0.010597401784997278,
    0.032883011666982945,
    0.030841381835986965,
    -0.18703481171888114,
    -0.02798376941698385,
    0.6308807679295904,
    0.7148465705525415,
    0.23037781330885523,
)
high_taps = tuple(((-1.0) ** offset * low_taps[7 - offset] for offset in range(8)))
f32 = jnp.float32
bf16 = jnp.bfloat16


def params(mib):
    return pltpu.CompilerParams(vmem_limit_bytes=mib * MIB)


def cost(flops, nbytes):
    return pl.CostEstimate(flops=int(flops), bytes_accessed=int(nbytes), transcendentals=0)


def halves(values):
    upper = values.astype(bf16)
    return upper, (values - upper.astype(f32)).astype(bf16)


def host_halves(values):
    values = values.astype(np.float32)
    upper = values.astype(ml_dtypes.bfloat16)
    return upper, (values - upper.astype(np.float32)).astype(ml_dtypes.bfloat16)


def mm(a, b):
    return jnp.dot(a, b, preferred_element_type=f32)


def mm_t(a, b):
    return lax.dot_general(a, b, (((1,), (1,)), ((), ())), preferred_element_type=f32)


def mm3(a, b):
    ah, al = halves(a)
    bh, bl = halves(b)
    return mm(ah, bh) + (mm(ah, bl) + mm(al, bh))


def swap_chunks(parts, width):
    count = len(parts)
    lane = lax.broadcasted_iota(jnp.int32, parts[0].shape, len(parts[0].shape) - 1)
    axis = len(parts[0].shape) - 1
    step = count // 2
    while step:
        span = step * width
        first = (lane // span) % 2 == 0
        out = list(parts)
        for a in range(count):
            if a & step:
                continue
            b = a | step
            out[a] = jnp.where(first, parts[a], pltpu.roll(parts[b], span, axis))
            out[b] = jnp.where(first, pltpu.roll(parts[a], 128 - span, axis), parts[b])
        parts = out
        step //= 2
    return parts


def pack_kernel(sky_ref, out_ref):
    for quarter in range(4):
        lanes = slice(128 * quarter, 128 * quarter + 128)
        parts = [sky_ref[:, 8 * k : 8 * k + 8, lanes] for k in range(4)]
        for s, done in enumerate(swap_chunks(parts, 32)):
            out_ref[4 * quarter + s] = done


def pack_sky(sky):
    return pl.pallas_call(
        pack_kernel,
        out_shape=jax.ShapeDtypeStruct((16, 16, 8, 128), f32),
        compiler_params=params(16),
        cost_estimate=cost(3e6, 2 * MIB),
        name="pack_sky",
    )(sky)


def gram_kernel(got_ref, dual_ref, y_ref, gram_ref):
    total = jnp.zeros((256, 256), f32)
    for low in range(8):
        seen = got_ref[pl.ds(low, 256, stride=8), :].T
        blocks = []
        for high in range(4):
            rows = pl.ds((8 * high + low) * 32, 32)
            block = dual_ref[rows, :] + 0.5 * seen[32 * high : 32 * high + 32, :]
            y_ref[rows, :] = block
            blocks.append(block)
        right = jnp.concatenate(blocks, axis=0)
        rh, rl = halves(right)
        left = right.T
        lh, ll = halves(left)
        total = total + (mm(lh, rh) + (mm(lh, rl) + mm(ll, rh)))
    gram_ref[...] = total


def gram_part(got, dual):
    return pl.pallas_call(
        gram_kernel,
        out_shape=(
            jax.ShapeDtypeStruct((1024, 256), f32),
            jax.ShapeDtypeStruct((256, 256), f32),
        ),
        compiler_params=params(24),
        cost_estimate=cost(4e8, 3 * MIB),
        name="gram_part",
    )(got, dual)


def mix_kernel(pixels, gram_ref, y_ref, out_ref):
    size = 256
    rows = lax.broadcasted_iota(jnp.int32, (size, size), 0)
    cols = lax.broadcasted_iota(jnp.int32, (size, size), 1)
    identity = (rows == cols).astype(f32)
    shifted = identity + gram_ref[...] * (1.0 / pixels)
    frob = jnp.sqrt(jnp.sum(shifted * shifted, keepdims=True))
    current = shifted / frob
    middle = 1.5 * identity - 0.5 * current
    current = mm3(current, middle)
    inverse = middle
    for turn in range(1, NSTEP):
        middle = 1.5 * identity - 0.5 * mm3(inverse, current)
        if turn < NSTEP - 1:
            current = mm3(current, middle)
        inverse = mm3(middle, inverse)
    mixer = inverse / jnp.sqrt(frob)
    mh, ml = halves(mixer)
    for block in range(4):
        span = pl.ds(256 * block, 256)
        yh, yl = halves(y_ref[span, :])
        out_ref[span, :] = mm_t(yh, mh) + (mm_t(yh, ml) + mm_t(yl, mh))


def mix(gram, y, pixels):
    return pl.pallas_call(
        lambda *refs: mix_kernel(pixels, *refs),
        out_shape=jax.ShapeDtypeStruct((1024, 256), f32),
        compiler_params=params(24),
        cost_estimate=cost(2e9, 3 * MIB),
        name="mix",
    )(gram, y)


def fir(shifted, filter_taps):
    summed = filter_taps[0] * shifted[0]
    for offset in range(1, 8):
        summed = summed + filter_taps[offset] * shifted[offset]
    return summed


def blend_kernel(margin_ref, sky_ref, rim_ref, dual_ref, blend_ref, energy_ref):
    margin = margin_ref[0]
    row = lax.broadcasted_iota(jnp.int32, (8, 512), 0)
    lane = lax.broadcasted_iota(jnp.int32, (32, 512), 1)
    kept = row >= 8 - margin

    @pl.when(pl.program_id(0) == 0)
    def _():
        energy_ref[...] = jnp.zeros_like(energy_ref)

    for c in range(sky_ref.shape[0]):
        ext = jnp.concatenate([jnp.where(kept, rim_ref[c], 0.0), sky_ref[c]], axis=0)
        moved = [ext[8:]] + [pltpu.roll(ext, m, 0)[8:] for m in range(1, 8)]
        for high in range(2):
            value = fir(moved, high_taps if high else low_taps)
            cols = [value] + [
                jnp.where(lane >= m, pltpu.roll(value, m, 1), 0.0) for m in range(1, 8)
            ]
            for band in range(2):
                which = 2 * high + band
                blended = dual_ref[which, c] + 0.5 * fir(cols, high_taps if band else low_taps)
                blend_ref[which, c] = blended
                energy_ref[which] += blended * blended


def blend(margin, sky, rim, dual):
    per = 2
    return pl.pallas_call(
        blend_kernel,
        grid=(16 // per,),
        in_specs=[
            pl.BlockSpec(memory_space=pltpu.SMEM),
            pl.BlockSpec((per, 32, 512), lambda i: (i, 0, 0)),
            pl.BlockSpec((per, 8, 512), lambda i: (i, 0, 0)),
            pl.BlockSpec((4, per, 32, 512), lambda i: (0, i, 0, 0)),
        ],
        out_specs=(
            pl.BlockSpec((4, per, 32, 512), lambda i: (0, i, 0, 0)),
            pl.BlockSpec((4, 32, 512), lambda i: (0, 0, 0)),
        ),
        out_shape=(
            jax.ShapeDtypeStruct((4, 16, 32, 512), f32),
            jax.ShapeDtypeStruct((4, 32, 512), f32),
        ),
        compiler_params=params(16),
        cost_estimate=cost(3e7, 10 * MIB),
        name="blend",
    )(margin, sky, rim, dual)


def shrink_kernel(channels, energy_ref, weight_ref, blend_ref, out_ref):
    ratio = jnp.sqrt(energy_ref[0] * (1.0 / channels)) / weight_ref[0]
    scale = 1.0 / jnp.maximum(1.0, ratio)
    for c in range(blend_ref.shape[1]):
        out_ref[0, c] = blend_ref[0, c] * scale


def shrink(energy, weights, blended, channels):
    return pl.pallas_call(
        lambda *refs: shrink_kernel(channels, *refs),
        grid=(4, 2),
        in_specs=[
            pl.BlockSpec((1, 32, 512), lambda b, i: (b, 0, 0)),
            pl.BlockSpec((1, 32, 512), lambda b, i: (b, 0, 0)),
            pl.BlockSpec((1, 8, 32, 512), lambda b, i: (b, i, 0, 0)),
        ],
        out_specs=pl.BlockSpec((1, 8, 32, 512), lambda b, i: (b, i, 0, 0)),
        out_shape=jax.ShapeDtypeStruct((4, 16, 32, 512), f32),
        input_output_aliases={2: 0},
        compiler_params=params(16),
        cost_estimate=cost(2e6, 9 * MIB),
        name="shrink",
    )(energy, weights, blended)


def degrid_tables(side):
    count = np.arange(side, dtype=np.int64)
    angle = (count[:, None] * count[None, :] % side) * (2.0 * np.pi / side)
    cos_h, cos_l = host_halves(np.cos(angle))
    sin_h, sin_l = host_halves(np.sin(angle))
    ky, row = np.arange(16)[:, None], np.arange(32)[None, :]
    turn = ky * row * (2.0 * np.pi / side)
    whole = np.zeros((16, 4, 2, 2, 4, 32))
    for ch in range(4):
        whole[:, ch, 0, 0, ch, :] = np.cos(turn)
        whole[:, ch, 0, 1, ch, :] = np.sin(turn)
        whole[:, ch, 1, 0, ch, :] = -np.sin(turn)
        whole[:, ch, 1, 1, ch, :] = np.cos(turn)
    row_h, row_l = host_halves(whole.reshape(128, 256))
    return cos_h, cos_l, sin_h, sin_l, row_h, row_l


def degrid_kernel(
    tx_ref,
    turn_ref,
    sky_ref,
    weight_ref,
    pc_ref,
    ps_ref,
    ch_ref,
    cl_ref,
    sh_ref,
    sl_ref,
    rh_ref,
    rl_ref,
    out_ref,
    xh_ref,
    xl_ref,
    table_ref,
    pre_ref,
    pim_ref,
    t_ref,
    u_ref,
):
    for b in range(32):
        start = pl.multiple_of(tx_ref[b] * KT, KT)
        for k, ref in enumerate((ch_ref, cl_ref, sh_ref, sl_ref)):
            table_ref[k, KT * b : KT * b + KT, :] = ref[pl.ds(start, KT), :]
    xh, xl = halves(sky_ref[...].reshape(512, 512))
    xh_ref[...] = xh
    xl_ref[...] = xl
    for half in range(4):
        rows = slice(128 * half, 128 * half + 128)
        xh, xl = xh_ref[rows, :], xl_ref[rows, :]
        gc = mm_t(xh, table_ref[0]) + (mm_t(xl, table_ref[0]) + mm_t(xh, table_ref[1]))
        gs = mm_t(xh, table_ref[2]) + (mm_t(xl, table_ref[2]) + mm_t(xh, table_ref[3]))
        gc, gs = gc.reshape(4, 32, 512), gs.reshape(4, 32, 512)
        pc, ps = pc_ref[...][None], ps_ref[...][None]
        pre = (gc * pc - gs * ps).reshape(128, 512)
        pim = (-(gs * pc + gc * ps)).reshape(128, 512)
        both_h, both_l = halves(jnp.concatenate([pre, pim], axis=0))
        t_ref[half] = mm(rh_ref[...], both_h) + (mm(rl_ref[...], both_h) + mm(rh_ref[...], both_l))
    even = lax.broadcasted_iota(jnp.int32, (8, 128), 0) % 2 == 0
    for quarter in range(4):
        for four in range(4):
            for high in range(2):
                parts = []
                for low in range(8):
                    ky = 8 * high + low
                    part = t_ref[four, 8 * ky : 8 * ky + 8, 128 * quarter : 128 * quarter + 128]
                    other = jnp.where(even, pltpu.roll(part, 7, 0), -pltpu.roll(part, 1, 0))
                    parts.append(part * turn_ref[0, ky] + other * turn_ref[1, ky])
                for b, done in enumerate(swap_chunks(parts, 16)):
                    u_ref[32 * b + 8 * four : 32 * b + 8 * four + 8, 128 * high : 128 * high + 128] = done
        uh, ul = halves(u_ref[...])
        rows = slice(256 * quarter, 256 * quarter + 256)
        sums = []
        for part in range(2):
            weights = weight_ref[rows, 256 * part : 256 * part + 256]
            sums.append(mm_t(uh, weights) + mm_t(ul, weights))
        lane = lax.broadcasted_iota(jnp.int32, (32, 256), 1)
        row = lax.broadcasted_iota(jnp.int32, (32, 256), 0)
        first = jnp.zeros((32, 256), f32)
        second = jnp.zeros((32, 256), f32)
        for b in range(8):
            mine = lane // 32 == b
            first = jnp.where(mine, sums[0][32 * b : 32 * b + 32, :], first)
            second = jnp.where(mine, sums[1][32 * b : 32 * b + 32, :], second)
        other = jnp.where(row % 2 == 0, -pltpu.roll(second, 31, 0), pltpu.roll(second, 1, 0))
        out_ref[:, 256 * quarter : 256 * quarter + 256] = (first + other) * (1.0 / 512.0)


def degrid(sky, weights, tile_ids, facet):
    side = sky.shape[-1]
    tables = [jnp.asarray(t) for t in degrid_tables(side)]
    tx = tile_ids % 32
    ty = tile_ids // 32
    ty_lanes = jnp.repeat(ty, KT)
    row = jnp.arange(32, dtype=jnp.int32)
    angle = (ty_lanes[None, :] * row[:, None] % 32).astype(f32) * (2.0 * math.pi / 32)
    ky = jnp.arange(KT, dtype=jnp.int32)
    facet_angle = (ky * facet % 16).astype(f32) * (2.0 * math.pi / 16)
    turn = jnp.stack([jnp.cos(facet_angle), jnp.sin(facet_angle)])
    smem = pl.BlockSpec(memory_space=pltpu.SMEM)
    vmem = pl.BlockSpec(memory_space=pltpu.VMEM)
    return pl.pallas_call(
        degrid_kernel,
        in_specs=[smem, smem] + [vmem] * 10,
        out_specs=vmem,
        out_shape=jax.ShapeDtypeStruct((32, 1024), f32),
        scratch_shapes=[
            pltpu.VMEM((512, 512), bf16),
            pltpu.VMEM((512, 512), bf16),
            pltpu.VMEM((4, 512, 512), bf16),
            pltpu.VMEM((8, 128), f32),
            pltpu.VMEM((8, 128), f32),
            pltpu.VMEM((4, 128, 512), f32),
            pltpu.VMEM((256, 256), f32),
        ],
        compiler_params=params(40),
        cost_estimate=cost(3e9, 6 * MIB),
        name="degrid",
    )(tx, turn, sky, weights, jnp.cos(angle), jnp.sin(angle), *tables)


def data_step(data_dual, forward, visibilities, radius_scale):
    moved = data_dual + forward
    residual = 2.0 * moved - visibilities
    distance = jnp.sqrt(jnp.sum(residual * residual, axis=(1, 2)) + 1e-06)
    radius = radius_scale * math.sqrt(2.0 * visibilities.shape[2])
    shrunk = jnp.minimum(1.0, radius / distance)
    return moved - 0.5 * (visibilities + residual * shrunk[:, None, None])


def trade(values, axis):
    return lax.all_to_all(values, axis, 0, 0, tiled=True)


def spread(values, axis):
    count = lax.axis_size(axis)
    return trade(jnp.broadcast_to(values[None], (count,) + values.shape), axis)


def per_device(
    sky_image,
    margins,
    wavelet_dual,
    sparsity_weights,
    lowrank_dual,
    kernel_weights,
    tile_index,
    data_dual,
    visibilities,
    radius_scale,
):
    facet_rows, image_side = sky_image.shape[1:]
    channels = lowrank_dual.shape[0]
    facet = lax.axis_index("facet")
    devices = lax.axis_size("facet")

    got = trade(pack_sky(sky_image), "chan").reshape(2048, 128)
    rim = lax.ppermute(
        sky_image[:, facet_rows - 8 :, :], "facet", [(i, i + 1) for i in range(devices - 1)]
    )
    margin = lax.dynamic_slice(margins, (facet,), (1,))
    blended, energy_part = blend(margin, sky_image, rim, wavelet_dual)

    forward_part = degrid(sky_image, kernel_weights.reshape(1024, 512), tile_index[0], facet)
    forward = jnp.sum(trade(forward_part.reshape(16, 2, 1024), "facet"), axis=0, keepdims=True)
    data_next = data_step(data_dual, forward, visibilities, radius_scale)

    energy_own = jnp.sum(trade(energy_part.reshape(16, 8, 512), "chan"), axis=0)
    energy = spread(energy_own, "chan").reshape(4, 32, 512)
    wavelet_next = shrink(energy, sparsity_weights, blended, channels)

    dual = jnp.transpose(lowrank_dual, (1, 2, 0)).reshape(1024, 256)
    y, part = gram_part(got, dual)
    gram_own = jnp.sum(trade(part.reshape(16, 16, 256), "chan"), axis=0)
    gram = spread(gram_own, "chan").reshape(256, 256)
    mixed = mix(gram, y, facet_rows * image_side)
    lowrank_next = jnp.transpose(mixed.reshape(32, 32, 256), (2, 0, 1))
    return (wavelet_next, lowrank_next, data_next)


def solution(mesh):
    in_specs = (
        P("chan", "facet", None),
        P(),
        P(None, "chan", "facet", None),
        P(None, "facet", None),
        P(None, "facet", "chan"),
        P("chan", None, None, None),
        P("chan", None),
        P(("chan", "facet"), None, None),
        P(("chan", "facet"), None, None),
        P(("chan", "facet")),
    )
    out_specs = (
        P(None, "chan", "facet", None),
        P(None, "facet", "chan"),
        P(("chan", "facet"), None, None),
    )
    return jax.shard_map(
        per_device, mesh=mesh, in_specs=in_specs, out_specs=out_specs, check_vma=False
    )
```

time: 359 us -> 142 us (0.40); the launches traced: 352 us -> 140 us
  waiting for transfers between devices: 158 us -> 55.3 us
  matrix products: 56.6 us -> 0 us
  local copies, waits for them, and re-layouts: 70.6 us -> 17.2 us
  Pallas kernels: 0 us -> 29.1 us
  other arithmetic: 30.9 us -> 3.29 us
  between operations: 17.5 us -> 2.15 us
  starting transfers between devices: 18.4 us -> 32.8 us
    psum x1 -> x0, waiting for transfers between devices: 155 us -> none  [per_device(): energy, gram = lax.psum((partial_energy, gram_part), 'chan')]
    dot_general x23 -> x0, matrix products: 56.6 us -> none  [the longest x1 7.82 us: per_device(): jnp.dot(cos_part, cosine, precision=highest)]
    all_to_all x2 -> x6, waiting for transfers between devices: 0.01 us -> 47.5 us  [trade(): return lax.all_to_all(values, axis, 0, 0, tiled=True)]
    pallas_call x0 -> x6, Pallas kernels: none -> 29.1 us  [the longest x1 7.82 us: blend(): pl.pallas_call(blend_kernel, grid=(16 // per,), in_specs=[pl.BlockSpec(me...]
    reshape x7 -> x1, local copies, waits for them, and re-layouts: 27.1 us -> 0.73 us  [per_device(): forward_part.reshape(16, 2, 1024)]
    all_to_all x2 -> x6, starting transfers between devices: 16.3 us -> 30.9 us  [trade(): return lax.all_to_all(values, axis, 0, 0, tiled=True)]
    transpose x3 -> x0, local copies, waits for them, and re-layouts: 14.5 us -> none  [the longest x2 14.4 us: to_tiles(): values.reshape(chan_count, tiles_side, KT, tiles_side, KT)]
    mul x2 -> x1, local copies, waits for them, and re-layouts: 10 us -> 0.08 us  [degrid(): ty_lanes[None, :] * row[:, None] % 32]
  transfers between devices with their start and end apart: 4 -> 7, of which waited for: 2 -> 7; matrix products, arithmetic and copies ran while one was open for 33% -> 3% of each run, Pallas kernels for 0% -> 12%
where the time goes in v1:
time: 142 us; the launch traced here: 140 us
  waiting for transfers between devices  55.3 us (39%)
  starting transfers between devices  32.8 us (23%)
  Pallas kernels  29.1 us (20%)
  local copies, waits for them, and re-layouts  17.2 us (12%)
  other arithmetic  3.29 us (2%)
  between operations  2.15 us (2%)
    all_to_all x6, waiting for transfers between devices, trade(): return lax.all_to_all(values, axis, 0, 0, tiled=True)  47.5 us
    all_to_all x6, starting transfers between devices, trade(): return lax.all_to_all(values, axis, 0, 0, tiled=True)  30.9 us
    unnamed x38, local copies, waits for them, and re-layouts  13.6 us
    ppermute x1, waiting for transfers between devices, per_device(): lax.ppermute(sky_image[:, facet_rows - 8:, :], 'facet', [(i, i + 1) for i...  7.82 us
    pallas_call x1, Pallas kernels, blend(): pl.pallas_call(blend_kernel, grid=(16 // per,), in_specs=[pl.BlockSpec(me...  7.82 us
    pallas_call x1, Pallas kernels, degrid(): pl.pallas_call(degrid_kernel, in_specs=[smem, smem] + [vmem] * 10, out_sp...  7.14 us
    pallas_call x1, Pallas kernels, shrink(): pl.pallas_call(lambda *refs: shrink_kernel(channels, *refs), grid=(4, 2),...  6.67 us
    pallas_call x1, Pallas kernels, mix(): pl.pallas_call(lambda *refs: mix_kernel(pixels, *refs), out_shape=jax.Sha...  4.62 us
  transfers between devices with their start and end apart: 7, of which 7 were waited for; matrix products, arithmetic and copies ran while one was open for 3% of the time, Pallas kernels for 12%

profile of v1, /device:TPU:8, one launch (start us, length us, event | category | flops | bytes accessed | tf_op | source)
XLA Modules:
  0.0 139.8 jit_solution(934296445374331078)
XLA Ops:
  0.6 0.7 and_select_fusion
  1.3 0.1 fusion.11
  1.4 0.1 broadcast_in_dim.10
  1.4 0.1 mul.83
  1.5 0.3 fusion.6
  1.8 0.0 copy-start
  1.8 1.2 copy-done
  3.0 0.0 copy-start.9
  3.0 1.2 copy-done.9
  4.3 0.0 copy-start.10
  4.3 1.0 copy-done.10
  5.3 0.0 copy-start.11
  5.3 1.0 copy-done.11
  6.3 0.0 copy-start.12
  6.3 1.0 copy-done.12
  7.4 0.0 copy-start.13
  7.4 1.0 copy-done.13
  8.4 0.0 copy-start.14
  8.4 0.8 copy-done.14
  9.3 0.0 copy-start.15
  9.3 0.8 copy-done.15
  10.1 0.0 copy-start.1
  10.1 7.1 %degrid.1 = f32[32,1024]{1,0:T(8,128)S(1)} custom-call(s32[32]{0:T(128)S(1)} %get-tuple-element.14.tx_ref, f32[2,16]{1,0:T(2,128)S(1)} %pad_maximum_fusion.turn_ref, f32[16,32,512]{2,1,0:T(8,128)S(1)} %copy-done, bf16[1024,512]{1,0:T(8,128)(2,1)S(1)} %bitcast.41, f32[32,512]{1,0:T(8,128)S(1)} %get-tuple-element.12.pc_ref, ...), custom_call_target="tpu_custom_call" | custom-call | flops 3000000000 | bytes 6291456 | tf_op jit(solution)/shard_map/degrid/pallas_call | solution.py:349
  17.3 0.0 copy-start.18
  17.3 0.7 reshape.104
  18.0 5.8 %all-to-all-start.5 = ((f32[16,2,1024]{2,1,0:T(2,128)}), f32[16,2,1024]{2,1,0:T(2,128)S(1)}, u32[]{:S(2)}, u32[]{:S(2)}) async-start(f32[16,2,1024]{2,1,0:T(2,128)} %reshape.104), calls=%async_computation.5 | async-start | bytes 262144 | tf_op jit(solution)/shard_map/all_to_all | solution.py:379
  23.8 0.0 copy-done.1
  23.8 1.7 %pack_sky.1 = f32[16,16,8,128]{3,2,1,0:T(8,128)} custom-call(f32[16,32,512]{2,1,0:T(8,128)S(1)} %copy-done.1), custom_call_target="tpu_custom_call" | custom-call | flops 3000000 | bytes 2097152 | tf_op jit(solution)/shard_map/pack_sky/pallas_call | solution.py:93
  25.5 3.4 %all-to-all-done.5 = f32[16,2,1024]{2,1,0:T(2,128)S(1)} async-done(((f32[16,2,1024]{2,1,0:T(2,128)}), f32[16,2,1024]{2,1,0:T(2,128)S(1)}, u32[]{:S(2)}, u32[]{:S(2)}) %all-to-all-start.5) | async-done | bytes 131104 | tf_op jit(solution)/shard_map/all_to_all | solution.py:379
  28.9 10.3 %all-to-all-start.2 = ((f32[16,16,8,128]{3,2,1,0:T(8,128)}), f32[16,16,8,128]{3,2,1,0:T(8,128)S(1)}, u32[]{:S(2)}, u32[]{:S(2)}) async-start(f32[16,16,8,128]{3,2,1,0:T(8,128)} %pack_sky.1), calls=%async_computation.2 | async-start | bytes 2097152 | tf_op jit(solution)/shard_map/all_to_all | solution.py:379
  39.2 0.7 slice.3
  39.9 1.9 %collective-permute-start = (f32[16,8,512]{2,1,0:T(8,128)}, f32[16,8,512]{2,1,0:T(8,128)S(1)}, u32[]{:S(2)}, u32[]{:S(2)}) collective-permute-start(f32[16,8,512]{2,1,0:T(8,128)} %slice.3), channel_id=1, source_target_pairs={{0,16},{16,32},{32,48},{48,64},{64,80},{80,96},{96,112},{112,128},... | collective-permute-start | bytes 786440 | tf_op jit(solution)/shard_map/ppermute | solution.py:405
  41.9 0.0 copy-done.18
  41.9 0.6 dynamic_slice.3.margin_ref
  42.5 7.8 %collective-permute-done.rim_ref = f32[16,8,512]{2,1,0:T(8,128)S(1)} collective-permute-done((f32[16,8,512]{2,1,0:T(8,128)}, f32[16,8,512]{2,1,0:T(8,128)S(1)}, u32[]{:S(2)}, u32[]{:S(2)}) %collective-permute-start) | collective-permute-done | bytes 262176 | tf_op jit(solution)/shard_map/ppermute | solution.py:405
  50.3 0.7 copy-done.5
  51.0 2.2 %copy-done.2 = f32[4,16,32,512]{3,2,1,0:T(8,128)S(1)} copy-done((f32[4,16,32,512]{3,2,1,0:T(8,128)S(1)}, f32[4,16,32,512]{3,2,1,0:T(8,128)}, u32[]{:S(2)}) %copy-start.2) | copy-done | bytes 4194328
  53.2 0.9 copy-done.6
  54.1 7.8 %blend.1 = (f32[4,16,32,512]{3,2,1,0:T(8,128)}, f32[4,32,512]{2,1,0:T(8,128)S(1)}) custom-call(s32[1]{0:T(128)} %dynamic_slice.3.margin_ref, f32[16,32,512]{2,1,0:T(8,128)S(1)} %copy-done.1, f32[16,8,512]{2,1,0:T(8,128)S(1)} %copy-done.6, f32[4,16,32,512]{3,2,1,0:T(8,128)S(1)} %copy-done.2), custom_call_target="tpu_custom_call" | custom-call | flops 30000000 | bytes 10485760 | tf_op jit(solution)/shard_map/blend/pallas_call | solution.py:201
  61.9 0.7 copy-done.7
  62.6 7.1 %all-to-all-done.2 = f32[16,16,8,128]{3,2,1,0:T(8,128)S(1)} async-done(((f32[16,16,8,128]{3,2,1,0:T(8,128)}), f32[16,16,8,128]{3,2,1,0:T(8,128)S(1)}, u32[]{:S(2)}, u32[]{:S(2)}) %all-to-all-start.2) | async-done | bytes 1048608 | tf_op jit(solution)/shard_map/all_to_all | solution.py:379
  69.8 4.2 %all-to-all-start = ((f32[16,8,512]{2,1,0:T(8,128)}), f32[16,8,512]{2,1,0:T(8,128)}, u32[]{:S(2)}, u32[]{:S(2)}) async-start(f32[16,8,512]{2,1,0:T(8,128)} %bitcast.39), calls=%async_computation | async-start | bytes 524288 | tf_op jit(solution)/shard_map/all_to_all | solution.py:379
  74.0 0.0 copy-done.3
  74.0 1.1 gram_part.1
  75.1 0.0 copy-start.8
  75.1 0.7 copy-done.8
  75.8 10.7 %all-to-all-done = f32[16,8,512]{2,1,0:T(8,128)} async-done(((f32[16,8,512]{2,1,0:T(8,128)}), f32[16,8,512]{2,1,0:T(8,128)}, u32[]{:S(2)}, u32[]{:S(2)}) %all-to-all-start) | async-done | bytes 262176 | tf_op jit(solution)/shard_map/all_to_all | solution.py:379
  86.5 3.5 %all-to-all-start.3 = ((f32[16,16,256]{2,1,0:T(8,128)}), f32[16,16,256]{2,1,0:T(8,128)S(1)}, u32[]{:S(2)}, u32[]{:S(2)}) async-start(f32[16,16,256]{2,1,0:T(8,128)} %bitcast.40), calls=%async_computation.3 | async-start | bytes 524288 | tf_op jit(solution)/shard_map/all_to_all | solution.py:379
  90.0 1.0 reduce_sum.36
  91.0 11.2 %all-to-all-done.3 = f32[16,16,256]{2,1,0:T(8,128)S(1)} async-done(((f32[16,16,256]{2,1,0:T(8,128)}), f32[16,16,256]{2,1,0:T(8,128)S(1)}, u32[]{:S(2)}, u32[]{:S(2)}) %all-to-all-start.3) | async-done | bytes 262176 | tf_op jit(solution)/shard_map/all_to_all | solution.py:379
  102.2 0.7 broadcast_in_dim.8
  103.0 3.5 %all-to-all-start.1 = ((f32[16,8,512]{2,1,0:T(8,128)}), f32[16,8,512]{2,1,0:T(8,128)S(1)}, u32[]{:S(2)}, u32[]{:S(2)}) async-start(f32[16,8,512]{2,1,0:T(8,128)} %broadcast_in_dim.8), calls=%async_computation.1 | async-start | bytes 524288 | tf_op jit(solution)/shard_map/all_to_all | solution.py:379
  106.5 12.2 %all-to-all-done.1 = f32[16,8,512]{2,1,0:T(8,128)S(1)} async-done(((f32[16,8,512]{2,1,0:T(8,128)}), f32[16,8,512]{2,1,0:T(8,128)S(1)}, u32[]{:S(2)}, u32[]{:S(2)}) %all-to-all-start.1) | async-done | bytes 262176 | tf_op jit(solution)/shard_map/all_to_all | solution.py:379
  118.7 0.7 broadcast_in_dim.9
  119.5 3.5 %all-to-all-start.4 = ((f32[16,16,256]{2,1,0:T(8,128)}), f32[16,16,256]{2,1,0:T(8,128)S(1)}, u32[]{:S(2)}, u32[]{:S(2)}) async-start(f32[16,16,256]{2,1,0:T(8,128)} %broadcast_in_dim.9), calls=%async_computation.4 | async-start | bytes 524288 | tf_op jit(solution)/shard_map/all_to_all | solution.py:379
  123.6 0.1 reduce_sum.38
  123.7 0.0 copy-done.16
  123.7 0.0 copy-done.17
  123.7 0.6 multiply_reduce_fusion
  125.0 0.6 multiply_subtract_fusion
  125.6 0.0 copy-done.4
  125.6 6.7 %shrink.1 = f32[4,16,32,512]{3,2,1,0:T(8,128)} custom-call(f32[4,32,512]{2,1,0:T(8,128)S(1)} %bitcast.36, f32[4,32,512]{2,1,0:T(8,128)S(1)} %copy-done.4, f32[4,16,32,512]{3,2,1,0:T(8,128)} %get-tuple-element.8.refs_2_), custom_call_target="tpu_custom_call", output_to_operand_aliasing={{}: (2, {})} | custom-call | flops 2000000 | bytes 9437184 | tf_op jit(solution)/shard_map/shrink/pallas_call | solution.py:232
  132.3 2.9 %all-to-all-done.4 = f32[16,16,256]{2,1,0:T(8,128)S(1)} async-done(((f32[16,16,256]{2,1,0:T(8,128)}), f32[16,16,256]{2,1,0:T(8,128)S(1)}, u32[]{:S(2)}, u32[]{:S(2)}) %all-to-all-start.4) | async-done | bytes 262176 | tf_op jit(solution)/shard_map/all_to_all | solution.py:379
  135.2 4.6 %mix.1 = f32[1024,256]{1,0:T(8,128)} custom-call(f32[256,256]{1,0:T(8,128)S(1)} %bitcast.38, f32[1024,256]{1,0:T(8,128)S(1)} %get-tuple-element.10.refs_1_), custom_call_target="tpu_custom_call" | custom-call | flops 2000000000 | bytes 3145728 | tf_op jit(solution)/shard_map/mix/pallas_call | solution.py:158
  (10 shorter events, 0.0 us)
Async XLA Ops:
  1.8 1.2 copy-start
  3.0 1.2 copy-start.9
  4.3 1.0 copy-start.10
  5.3 1.0 copy-start.11
  6.3 1.0 copy-start.12
  7.4 1.0 copy-start.13
  8.4 0.8 copy-start.14
  9.3 0.8 copy-start.15
  10.1 13.7 %copy-start.1 = (f32[16,32,512]{2,1,0:T(8,128)S(1)}, f32[16,32,512]{2,1,0:T(8,128)}, u32[]{:S(2)}) copy-start(f32[16,32,512]{2,1,0:T(8,128)} %sky_ref.5) | copy-start | bytes 3145732
  17.3 24.6 %copy-start.18 = (s32[16]{0:T(128)S(1)}, s32[16]{0:T(128)}, u32[]{:S(2)}) copy-start(s32[16]{0:T(128)} %param.17) | copy-start | bytes 196
  18.0 10.9 %all-to-all-start.5 = ((f32[16,2,1024]{2,1,0:T(2,128)}), f32[16,2,1024]{2,1,0:T(2,128)S(1)}, u32[]{:S(2)}, u32[]{:S(2)}) async-start(f32[16,2,1024]{2,1,0:T(2,128)} %reshape.104), calls=%async_computation.5 | async-start | bytes 262144 | tf_op jit(solution)/shard_map/all_to_all | solution.py:379
  25.5 48.5 %copy-start.3 = (f32[256,32,32]{0,2,1:T(8,128)S(1)}, f32[256,32,32]{0,2,1:T(8,128)}, u32[]{:S(2)}) copy-start(f32[256,32,32]{0,2,1:T(8,128)} %param.20) | copy-start | bytes 3145732
  28.9 40.9 %all-to-all-start.2 = ((f32[16,16,8,128]{3,2,1,0:T(8,128)}), f32[16,16,8,128]{3,2,1,0:T(8,128)S(1)}, u32[]{:S(2)}, u32[]{:S(2)}) async-start(f32[16,16,8,128]{3,2,1,0:T(8,128)} %pack_sky.1), calls=%async_computation.2 | async-start | bytes 2097152 | tf_op jit(solution)/shard_map/all_to_all | solution.py:379
  39.9 10.3 %collective-permute-start = (f32[16,8,512]{2,1,0:T(8,128)}, f32[16,8,512]{2,1,0:T(8,128)S(1)}, u32[]{:S(2)}, u32[]{:S(2)}) collective-permute-start(f32[16,8,512]{2,1,0:T(8,128)} %slice.3), channel_id=1, source_target_pairs={{0,16},{16,32},{32,48},{48,64},{64,80},{80,96},{96,112},{112,128},... | collective-permute-start | bytes 786440 | tf_op jit(solution)/shard_map/ppermute | solution.py:405
  50.3 0.7 copy-start.5
  51.0 2.2 %copy-start.2 = (f32[4,16,32,512]{3,2,1,0:T(8,128)S(1)}, f32[4,16,32,512]{3,2,1,0:T(8,128)}, u32[]{:S(2)}) copy-start(f32[4,16,32,512]{3,2,1,0:T(8,128)} %dual_ref.1) | copy-start | bytes 12582916
  53.2 0.9 copy-start.6
  54.1 69.6 %copy-start.16 = (f32[1,2,1024]{2,1,0:T(2,128)S(1)}, f32[1,2,1024]{2,1,0:T(2,128)}, u32[]{:S(2)}) copy-start(f32[1,2,1024]{2,1,0:T(2,128)} %param.24) | copy-start | bytes 24580
  54.1 69.6 %copy-start.17 = (f32[1,2,1024]{2,1,0:T(2,128)S(1)}, f32[1,2,1024]{2,1,0:T(2,128)}, u32[]{:S(2)}) copy-start(f32[1,2,1024]{2,1,0:T(2,128)} %param.23) | copy-start | bytes 24580
  54.1 71.5 %copy-start.4 = (f32[4,32,512]{2,1,0:T(8,128)S(1)}, f32[4,32,512]{2,1,0:T(8,128)}, u32[]{:S(2)}) copy-start(f32[4,32,512]{2,1,0:T(8,128)} %refs_1_.1) | copy-start | bytes 786436
  61.9 0.7 copy-start.7
  69.8 16.7 %all-to-all-start = ((f32[16,8,512]{2,1,0:T(8,128)}), f32[16,8,512]{2,1,0:T(8,128)}, u32[]{:S(2)}, u32[]{:S(2)}) async-start(f32[16,8,512]{2,1,0:T(8,128)} %bitcast.39), calls=%async_computation | async-start | bytes 524288 | tf_op jit(solution)/shard_map/all_to_all | solution.py:379
  75.1 0.7 copy-start.8
  86.5 15.8 %all-to-all-start.3 = ((f32[16,16,256]{2,1,0:T(8,128)}), f32[16,16,256]{2,1,0:T(8,128)S(1)}, u32[]{:S(2)}, u32[]{:S(2)}) async-start(f32[16,16,256]{2,1,0:T(8,128)} %bitcast.40), calls=%async_computation.3 | async-start | bytes 524288 | tf_op jit(solution)/shard_map/all_to_all | solution.py:379
  103.0 15.8 %all-to-all-start.1 = ((f32[16,8,512]{2,1,0:T(8,128)}), f32[16,8,512]{2,1,0:T(8,128)S(1)}, u32[]{:S(2)}, u32[]{:S(2)}) async-start(f32[16,8,512]{2,1,0:T(8,128)} %broadcast_in_dim.8), calls=%async_computation.1 | async-start | bytes 524288 | tf_op jit(solution)/shard_map/all_to_all | solution.py:379
  119.5 15.8 %all-to-all-start.4 = ((f32[16,16,256]{2,1,0:T(8,128)}), f32[16,16,256]{2,1,0:T(8,128)S(1)}, u32[]{:S(2)}, u32[]{:S(2)}) async-start(f32[16,16,256]{2,1,0:T(8,128)} %broadcast_in_dim.9), calls=%async_computation.4 | async-start | bytes 524288 | tf_op jit(solution)/shard_map/all_to_all | solution.py:379

commit v2 on v1

v2 whole, which is shorter than its diff:
```python
import math

import jax
import jax.numpy as jnp
import ml_dtypes
import numpy as np
from jax import lax
from jax.experimental import pallas as pl
from jax.experimental.pallas import tpu as pltpu
from jax.sharding import PartitionSpec as P

NSTEP = 5
KT = 16
MIB = 1 << 20
BIG = 56

low_taps = (
    -0.010597401784997278,
    0.032883011666982945,
    0.030841381835986965,
    -0.18703481171888114,
    -0.02798376941698385,
    0.6308807679295904,
    0.7148465705525415,
    0.23037781330885523,
)
high_taps = tuple(((-1.0) ** offset * low_taps[7 - offset] for offset in range(8)))
f32 = jnp.float32
bf16 = jnp.bfloat16


def params(mib):
    return pltpu.CompilerParams(vmem_limit_bytes=int(mib * MIB))


def cost(flops, nbytes):
    return pl.CostEstimate(flops=int(flops), bytes_accessed=int(nbytes), transcendentals=0)


def halves(values):
    upper = values.astype(bf16)
    return upper, (values - upper.astype(f32)).astype(bf16)


def host_halves(values):
    values = values.astype(np.float32)
    upper = values.astype(ml_dtypes.bfloat16)
    return upper, (values - upper.astype(np.float32)).astype(ml_dtypes.bfloat16)


def mm(a, b):
    return jnp.dot(a, b, preferred_element_type=f32)


def mm_t(a, b):
    return lax.dot_general(a, b, (((1,), (1,)), ((), ())), preferred_element_type=f32)


def mm3(a, b):
    ah, al = halves(a)
    bh, bl = halves(b)
    return mm(ah, bh) + (mm(ah, bl) + mm(al, bh))


def swap_chunks(parts, width):
    count = len(parts)
    lane = lax.broadcasted_iota(jnp.int32, parts[0].shape, len(parts[0].shape) - 1)
    axis = len(parts[0].shape) - 1
    step = count // 2
    while step:
        span = step * width
        first = (lane // span) % 2 == 0
        out = list(parts)
        for a in range(count):
            if a & step:
                continue
            b = a | step
            out[a] = jnp.where(first, parts[a], pltpu.roll(parts[b], span, axis))
            out[b] = jnp.where(first, pltpu.roll(parts[a], 128 - span, axis), parts[b])
        parts = out
        step //= 2
    return parts


def pack_kernel(sky_in, packed_out, sky_ref, packed_ref, in_sems, out_sems):
    fours = [slice(4 * k, 4 * k + 4) for k in range(4)]
    coming = [
        pltpu.make_async_copy(sky_in.at[four], sky_ref.at[four], in_sems.at[k])
        for k, four in enumerate(fours)
    ]
    going = [
        pltpu.make_async_copy(packed_ref.at[:, four], packed_out.at[:, four], out_sems.at[k])
        for k, four in enumerate(fours)
    ]
    for copy in coming:
        copy.start()
    for k, four in enumerate(fours):
        coming[k].wait()
        for quarter in range(4):
            lanes = slice(128 * quarter, 128 * quarter + 128)
            parts = [sky_ref[four, 8 * j : 8 * j + 8, lanes] for j in range(4)]
            for s, done in enumerate(swap_chunks(parts, 32)):
                packed_ref[4 * quarter + s, four] = done
        going[k].start()
    for copy in going:
        copy.wait()


def pack_sky(sky):
    hbm = pl.BlockSpec(memory_space=pl.ANY)
    return pl.pallas_call(
        pack_kernel,
        in_specs=[hbm],
        out_specs=hbm,
        out_shape=jax.ShapeDtypeStruct((16, 16, 8, 128), f32),
        scratch_shapes=[
            pltpu.VMEM((16, 32, 512), f32),
            pltpu.VMEM((16, 16, 8, 128), f32),
            pltpu.SemaphoreType.DMA((4,)),
            pltpu.SemaphoreType.DMA((4,)),
        ],
        compiler_params=params(59.9),
        cost_estimate=cost(3e6, 2 * MIB),
        name="pack_sky",
    )(sky)


def gram_kernel(got_ref, dual_ref, energy_ref, y_out, part_out, y_ref, gram_ref, sems):
    copies = [pltpu.make_async_copy(energy_ref, part_out.at[:, :32], sems.at[8])]
    copies[0].start()
    total = jnp.zeros((256, 256), f32)
    for low in range(8):
        seen = got_ref[pl.ds(low, 256, stride=8), :].T
        right = dual_ref[:, low].reshape(128, 256) + 0.5 * seen
        y_ref[:, low] = right.reshape(4, 32, 256)
        copies.append(pltpu.make_async_copy(y_ref.at[:, low], y_out.at[:, low], sems.at[low]))
        copies[-1].start()
        rh, rl = halves(right)
        left = right.T
        lh, ll = halves(left)
        total = total + (mm(lh, rh) + (mm(lh, rl) + mm(ll, rh)))
    for peer in range(16):
        for h in range(2):
            gram_ref[peer, 16 * h : 16 * h + 16, :] = total[
                16 * peer : 16 * peer + 16, 128 * h : 128 * h + 128
            ]
    copies.append(pltpu.make_async_copy(gram_ref, part_out.at[:, 32:], sems.at[9]))
    copies[-1].start()
    for copy in copies:
        copy.wait()


def gram_part(got, dual, energy):
    vmem = pl.BlockSpec(memory_space=pltpu.VMEM)
    hbm = pl.BlockSpec(memory_space=pl.ANY)
    return pl.pallas_call(
        gram_kernel,
        in_specs=[vmem] * 3,
        out_specs=(hbm, hbm),
        out_shape=(
            jax.ShapeDtypeStruct((4, 8, 32, 256), f32),
            jax.ShapeDtypeStruct((16, 64, 128), f32),
        ),
        scratch_shapes=[
            pltpu.VMEM((4, 8, 32, 256), f32),
            pltpu.VMEM((16, 32, 128), f32),
            pltpu.SemaphoreType.DMA((10,)),
        ],
        compiler_params=params(58),
        cost_estimate=cost(4e8, 3 * MIB),
        name="gram_part",
    )(got, dual, energy)


def sum_kernel(got_ref, out_ref):
    total = got_ref[0]
    for peer in range(1, 16):
        total = total + got_ref[peer]
    for peer in range(16):
        out_ref[peer] = total


def sum_copies(got):
    return pl.pallas_call(
        sum_kernel,
        out_shape=jax.ShapeDtypeStruct(got.shape, f32),
        compiler_params=params(16),
        cost_estimate=cost(1e6, MIB),
        name="sum_copies",
    )(got)


def finish_kernel(
    pixels,
    channels,
    got_ref,
    weight_in,
    blend_in,
    y_in,
    wave_out,
    mixed_out,
    weight_ref,
    blend_ref,
    wave_ref,
    y_ref,
    mixed_ref,
    in_sems,
    out_sems,
):
    coming = [pltpu.make_async_copy(weight_in, weight_ref, in_sems.at[5])]
    coming += [
        pltpu.make_async_copy(blend_in.at[band], blend_ref.at[band], in_sems.at[band])
        for band in range(4)
    ]
    coming.append(pltpu.make_async_copy(y_in, y_ref, in_sems.at[4]))
    for copy in coming:
        copy.start()
    going = []

    def wave():
        for copy in coming:
            copy.wait()
        for band in range(4):
            for part in range(4):
                rows = slice(8 * part, 8 * part + 8)
                for q in range(4):
                    lanes = slice(128 * q, 128 * q + 128)
                    energy = got_ref[4 * band + part, 8 * q : 8 * q + 8, :]
                    ratio = jnp.sqrt(energy * (1.0 / channels)) / weight_ref[band, rows, lanes]
                    scale = 1.0 / jnp.maximum(1.0, ratio)
                    wave_ref[band, :, rows, lanes] = blend_ref[band, :, rows, lanes] * scale[None]
            copy = pltpu.make_async_copy(wave_ref.at[band], wave_out.at[band], out_sems.at[band])
            copy.start()
            going.append(copy)

    size = 256
    rows = lax.broadcasted_iota(jnp.int32, (size, size), 0)
    cols = lax.broadcasted_iota(jnp.int32, (size, size), 1)
    identity = (rows == cols).astype(f32)
    sides = [got_ref[:, 32 + 16 * h : 48 + 16 * h, :].reshape(size, 128) for h in range(2)]
    shifted = identity + jnp.concatenate(sides, axis=1) * (1.0 / pixels)
    frob = jnp.sqrt(jnp.sum(shifted * shifted, keepdims=True))
    current = shifted / frob
    middle = 1.5 * identity - 0.5 * current
    current = mm3(current, middle)
    inverse = middle
    for turn in range(1, NSTEP):
        middle = 1.5 * identity - 0.5 * mm3(inverse, current)
        if turn < NSTEP - 1:
            both = mm3(jnp.concatenate([current, inverse], axis=0), middle)
            current, inverse = both[:size], both[size:]
        else:
            inverse = mm3(inverse, middle)
        if turn == 2:
            wave()
    mixer = inverse / jnp.sqrt(frob)
    mh, ml = halves(mixer)
    for block in range(4):
        span = pl.ds(256 * block, 256)
        yh, yl = halves(y_ref[span, :])
        mixed_ref[span, :] = mm_t(yh, mh) + (mm_t(yh, ml) + mm_t(yl, mh))
        copy = pltpu.make_async_copy(mixed_ref.at[span], mixed_out.at[span], out_sems.at[4 + block])
        copy.start()
        going.append(copy)
    for copy in going:
        copy.wait()


def finish(got, weights, blended, y, pixels, channels):
    hbm = pl.BlockSpec(memory_space=pl.ANY)
    return pl.pallas_call(
        lambda *refs: finish_kernel(pixels, channels, *refs),
        in_specs=[pl.BlockSpec(memory_space=pltpu.VMEM), hbm, hbm, hbm],
        out_specs=(hbm, hbm),
        out_shape=(
            jax.ShapeDtypeStruct(blended.shape, f32),
            jax.ShapeDtypeStruct((1024, 256), f32),
        ),
        scratch_shapes=[
            pltpu.VMEM(weights.shape, f32),
            pltpu.VMEM(blended.shape, f32),
            pltpu.VMEM(blended.shape, f32),
            pltpu.VMEM((1024, 256), f32),
            pltpu.VMEM((1024, 256), f32),
            pltpu.SemaphoreType.DMA((6,)),
            pltpu.SemaphoreType.DMA((8,)),
        ],
        compiler_params=params(59.8),
        cost_estimate=cost(2e9, 8 * MIB),
        name="finish",
    )(got, weights, blended, y)


def filter_tables():
    both = (low_taps, high_taps)
    down = np.zeros((2, 4, 32, 4, 40))
    across = np.zeros((256, 2, 128))
    for which, taps in enumerate(both):
        for m, tap in enumerate(taps):
            for row in range(32):
                for ch in range(4):
                    down[which, ch, row, ch, 8 + row - m] = tap
            for col in range(128):
                across[128 + col - m, which, col] = 0.5 * tap
    down = np.concatenate(host_halves(down.reshape(256, 160)))
    return down, np.concatenate(host_halves(across.reshape(256, 256)))


def blend_kernel(margin_ref, sky_ref, rim_ref, dual_ref, down_ref, across_ref, blend_ref, energy_ref):
    row = lax.broadcasted_iota(jnp.int32, (8, 512), 0)
    kept = row >= 8 - margin_ref[0]

    @pl.when(pl.program_id(0) == 0)
    def _():
        energy_ref[...] = jnp.zeros_like(energy_ref)

    pieces = []
    for c in range(4):
        pieces += [jnp.where(kept, rim_ref[c], 0.0), sky_ref[c]]
    eh, el = halves(jnp.concatenate(pieces, axis=0))
    dh, dl = down_ref[:256, :], down_ref[256:, :]
    filtered = mm(dh, eh) + (mm(dh, el) + mm(dl, eh))
    vh, vl = halves(filtered)
    for j in range(4):
        if j:
            lanes = slice(128 * j - 128, 128 * j + 128)
            ah, al = across_ref[:256, :], across_ref[256:, :]
        else:
            lanes = slice(0, 128)
            ah, al = across_ref[128:256, :], across_ref[384:, :]
        done = mm(vh[:, lanes], ah) + (mm(vl[:, lanes], ah) + mm(vh[:, lanes], al))
        here = slice(128 * j, 128 * j + 128)
        for band in range(4):
            part = done[128 * (band // 2) : 128 * (band // 2) + 128]
            part = part[:, 128 * (band % 2) : 128 * (band % 2) + 128].reshape(4, 32, 128)
            blended = dual_ref[band, :, :, here] + part
            blend_ref[band, :, :, here] = blended
            squares = jnp.sum(blended * blended, axis=0)
            for strip in range(4):
                energy_ref[4 * band + strip, 8 * j : 8 * j + 8, :] += squares[8 * strip : 8 * strip + 8]


def blend(margin, sky, rim, dual):
    down, across = (jnp.asarray(t) for t in filter_tables())
    return pl.pallas_call(
        blend_kernel,
        grid=(4,),
        in_specs=[
            pl.BlockSpec(memory_space=pltpu.SMEM),
            pl.BlockSpec((4, 32, 512), lambda i: (i, 0, 0)),
            pl.BlockSpec((4, 8, 512), lambda i: (i, 0, 0)),
            pl.BlockSpec((4, 4, 32, 512), lambda i: (0, i, 0, 0)),
            pl.BlockSpec((512, 160), lambda i: (0, 0)),
            pl.BlockSpec((512, 256), lambda i: (0, 0)),
        ],
        out_specs=(
            pl.BlockSpec((4, 4, 32, 512), lambda i: (0, i, 0, 0)),
            pl.BlockSpec((16, 32, 128), lambda i: (0, 0, 0)),
        ),
        out_shape=(
            jax.ShapeDtypeStruct((4, 16, 32, 512), f32),
            jax.ShapeDtypeStruct((16, 32, 128), f32),
        ),
        compiler_params=params(57),
        cost_estimate=cost(3e9, 10 * MIB),
        name="blend",
    )(margin, sky, rim, dual, down, across)


def degrid_tables(side):
    column = np.arange(side, dtype=np.int64)[None, :]
    kx = np.arange(KT, dtype=np.int64)[:, None]
    tile = np.arange(side // KT, dtype=np.int64)[:, None]
    inner = (kx * column % side) * (2.0 * np.pi / side)
    outer = (KT * tile * column % side) * (2.0 * np.pi / side)
    columns = np.concatenate([np.cos(inner), np.sin(inner), np.cos(outer), np.sin(outer)])
    ky, row = np.arange(16)[:, None], np.arange(32)[None, :]
    turn = ky * row * (2.0 * np.pi / side)
    whole = np.zeros((16, 4, 2, 2, 4, 32))
    for ch in range(4):
        whole[:, ch, 0, 0, ch, :] = np.cos(turn)
        whole[:, ch, 0, 1, ch, :] = np.sin(turn)
        whole[:, ch, 1, 0, ch, :] = -np.sin(turn)
        whole[:, ch, 1, 1, ch, :] = np.cos(turn)
    rows = np.concatenate(host_halves(whole.reshape(128, 256)))
    return columns.astype(np.float32), rows


def channel_at(place):
    b0, b3, b1, b2 = ((place >> k) & 1 for k in (3, 2, 1, 0))
    return b0 + 2 * b1 + 4 * b2 + 8 * b3


def degrid_kernel(
    tx_ref,
    turn_ref,
    sky_ref,
    phase_ref,
    column_ref,
    row_ref,
    weight_in,
    out_ref,
    xh_ref,
    xl_ref,
    table_ref,
    t_ref,
    u_ref,
    weight_ref,
    sem,
):
    coming = pltpu.make_async_copy(weight_in, weight_ref, sem.at[0])
    coming.start()
    inner_cos, inner_sin = column_ref[:KT, :], column_ref[KT : 2 * KT, :]
    for b in range(32):
        outer_cos = column_ref[pl.ds(2 * KT + tx_ref[b], 1), :]
        outer_sin = column_ref[pl.ds(2 * KT + 32 + tx_ref[b], 1), :]
        rows = slice(KT * b, KT * b + KT)
        both = (
            inner_cos * outer_cos - inner_sin * outer_sin,
            inner_sin * outer_cos + inner_cos * outer_sin,
        )
        for k, values in enumerate(both):
            upper, lower = halves(values)
            table_ref[2 * k, rows, :] = upper
            table_ref[2 * k + 1, rows, :] = lower
    for place in range(16):
        xh, xl = halves(sky_ref[channel_at(place)])
        xh_ref[32 * place : 32 * place + 32, :] = xh
        xl_ref[32 * place : 32 * place + 32, :] = xl
    cos_h, cos_l, sin_h, sin_l = (table_ref[k] for k in range(4))
    row_h, row_l = row_ref[:128, :], row_ref[128:, :]
    for half in range(4):
        rows = slice(128 * half, 128 * half + 128)
        xh, xl = xh_ref[rows, :], xl_ref[rows, :]
        gc = mm_t(xh, cos_h) + (mm_t(xl, cos_h) + mm_t(xh, cos_l))
        gs = mm_t(xh, sin_h) + (mm_t(xl, sin_h) + mm_t(xh, sin_l))
        gc, gs = gc.reshape(4, 32, 512), gs.reshape(4, 32, 512)
        pc, ps = phase_ref[0][None], phase_ref[1][None]
        pre = (gc * pc - gs * ps).reshape(128, 512)
        pim = (-(gs * pc + gc * ps)).reshape(128, 512)
        both_h, both_l = halves(jnp.concatenate([pre, pim], axis=0))
        t_ref[half] = mm(row_h, both_h) + (mm(row_l, both_h) + mm(row_h, both_l))
    even = lax.broadcasted_iota(jnp.int32, (8, 128), 0) % 2 == 0
    coming.wait()
    for quarter in range(4):
        for four in range(4):
            for high in range(2):
                parts = []
                for low in range(8):
                    ky = 8 * high + low
                    part = t_ref[four, 8 * ky : 8 * ky + 8, 128 * quarter : 128 * quarter + 128]
                    other = jnp.where(even, pltpu.roll(part, 7, 0), -pltpu.roll(part, 1, 0))
                    parts.append(part * turn_ref[0, ky] + other * turn_ref[1, ky])
                for b, done in enumerate(swap_chunks(parts, 16)):
                    u_ref[32 * b + 8 * four : 32 * b + 8 * four + 8, 128 * high : 128 * high + 128] = done
        uh, ul = halves(u_ref[...])
        rows = slice(256 * quarter, 256 * quarter + 256)
        sums = []
        for part in range(2):
            weights = weight_ref[rows, 256 * part : 256 * part + 256]
            sums.append(mm_t(uh, weights) + mm_t(ul, weights))
        lane = lax.broadcasted_iota(jnp.int32, (32, 256), 1)
        row = lax.broadcasted_iota(jnp.int32, (32, 256), 0)
        first = jnp.zeros((32, 256), f32)
        second = jnp.zeros((32, 256), f32)
        for b in range(8):
            mine = lane // 32 == b
            first = jnp.where(mine, sums[0][32 * b : 32 * b + 32, :], first)
            second = jnp.where(mine, sums[1][32 * b : 32 * b + 32, :], second)
        other = jnp.where(row % 2 == 0, -pltpu.roll(second, 31, 0), pltpu.roll(second, 1, 0))
        out_ref[:, 256 * quarter : 256 * quarter + 256] = (first + other) * (1.0 / 512.0)


def degrid(sky, weights, tile_ids, facet):
    side = sky.shape[-1]
    columns, rows = (jnp.asarray(t) for t in degrid_tables(side))
    ty_lanes = jnp.repeat(tile_ids // 32, KT)
    row = jnp.arange(32, dtype=jnp.int32)
    angle = (ty_lanes[None, :] * row[:, None] % 32).astype(f32) * (2.0 * math.pi / 32)
    phase = jnp.stack([jnp.cos(angle), jnp.sin(angle)])
    ky = jnp.arange(KT, dtype=jnp.int32)
    facet_angle = (ky * facet % 16).astype(f32) * (2.0 * math.pi / 16)
    turn = jnp.stack([jnp.cos(facet_angle), jnp.sin(facet_angle)])
    smem = pl.BlockSpec(memory_space=pltpu.SMEM)
    vmem = pl.BlockSpec(memory_space=pltpu.VMEM)
    return pl.pallas_call(
        degrid_kernel,
        in_specs=[smem, smem] + [vmem] * 4 + [pl.BlockSpec(memory_space=pl.ANY)],
        out_specs=vmem,
        out_shape=jax.ShapeDtypeStruct((32, 1024), f32),
        scratch_shapes=[
            pltpu.VMEM((512, 512), bf16),
            pltpu.VMEM((512, 512), bf16),
            pltpu.VMEM((4, 512, 512), bf16),
            pltpu.VMEM((4, 128, 512), f32),
            pltpu.VMEM((256, 256), f32),
            pltpu.VMEM((1024, 512), bf16),
            pltpu.SemaphoreType.DMA((1,)),
        ],
        compiler_params=params(24),
        cost_estimate=cost(3e9, 6 * MIB),
        name="degrid",
    )(tile_ids % 32, turn, sky, phase, columns, rows, weights)


def data_step(data_dual, forward, visibilities, radius_scale):
    moved = data_dual + forward
    residual = 2.0 * moved - visibilities
    distance = jnp.sqrt(jnp.sum(residual * residual, axis=(1, 2)) + 1e-06)
    radius = radius_scale * math.sqrt(2.0 * visibilities.shape[2])
    shrunk = jnp.minimum(1.0, radius / distance)
    return moved - 0.5 * (visibilities + residual * shrunk[:, None, None])


def trade(values, axis):
    return lax.all_to_all(values, axis, 0, 0, tiled=True)


def halving_sum(values, axis, bits):
    me = lax.axis_index(axis)
    count = lax.axis_size(axis)
    for bit in bits:
        values = values.reshape((2, values.shape[0] // 2) + values.shape[1:])
        mine = (me >> bit) & 1
        sent = lax.dynamic_index_in_dim(values, 1 - mine, 0, keepdims=False)
        kept = lax.dynamic_index_in_dim(values, mine, 0, keepdims=False)
        pairs = [(i, i ^ (1 << bit)) for i in range(count)]
        values = kept + lax.ppermute(sent, axis, pairs)
    return values[0]


def per_device(
    sky_image,
    margins,
    wavelet_dual,
    sparsity_weights,
    lowrank_dual,
    kernel_weights,
    tile_index,
    data_dual,
    visibilities,
    radius_scale,
):
    facet_rows, image_side = sky_image.shape[1:]
    channels = lowrank_dual.shape[0]
    facet = lax.axis_index("facet")
    devices = lax.axis_size("facet")

    packed, sky = lax.optimization_barrier((pack_sky(sky_image), sky_image))
    got = trade(packed, "chan").reshape(2048, 128)
    rim = lax.ppermute(
        sky[:, facet_rows - 8 :, :], "facet", [(i, i + 1) for i in range(devices - 1)]
    )
    forward_part = degrid(sky, kernel_weights.reshape(1024, 512), tile_index[0], facet)
    margin = lax.dynamic_slice(margins, (facet,), (1,))
    margin, forward_part = lax.optimization_barrier((margin, forward_part))
    blended, energy_part = blend(margin, sky, rim, wavelet_dual)
    energy_part, forward_part = lax.optimization_barrier((energy_part, forward_part))
    forward = halving_sum(forward_part.reshape(16, 2, 1024), "facet", (0, 3, 1, 2))[None]

    dual = jnp.transpose(lowrank_dual, (1, 2, 0)).reshape(4, 8, 32, 256)
    y, part = gram_part(got, dual, energy_part)
    reduced, forward = lax.optimization_barrier((trade(part, "chan"), forward))
    data_next = data_step(data_dual, forward, visibilities, radius_scale)
    total = trade(sum_copies(reduced), "chan")
    wavelet_next, mixed = finish(
        total, sparsity_weights, blended, y.reshape(1024, 256), facet_rows * image_side, channels
    )
    lowrank_next = jnp.transpose(mixed.reshape(32, 32, 256), (2, 0, 1))
    return (wavelet_next, lowrank_next, data_next)


def solution(mesh):
    in_specs = (
        P("chan", "facet", None),
        P(),
        P(None, "chan", "facet", None),
        P(None, "facet", None),
        P(None, "facet", "chan"),
        P("chan", None, None, None),
        P("chan", None),
        P(("chan", "facet"), None, None),
        P(("chan", "facet"), None, None),
        P(("chan", "facet")),
    )
    out_specs = (
        P(None, "chan", "facet", None),
        P(None, "facet", "chan"),
        P(("chan", "facet"), None, None),
    )
    return jax.shard_map(
        per_device, mesh=mesh, in_specs=in_specs, out_specs=out_specs, check_vma=False
    )
```

time: 142 us -> 102 us (0.72)
  waiting for transfers between devices: 55.3 us -> 34.9 us
  local copies, waits for them, and re-layouts: 17.2 us -> 2.41 us
  starting transfers between devices: 32.8 us -> 28.5 us
  other arithmetic: 3.29 us -> 1.66 us
  Pallas kernels: 29.1 us -> 30.6 us
    all_to_all x6 -> x3, waiting for transfers between devices: 47.5 us -> 27.1 us  [trade(): return lax.all_to_all(values, axis, 0, 0, tiled=True)]
    all_to_all x6 -> x3, starting transfers between devices: 30.9 us -> 18.8 us  [trade(): return lax.all_to_all(values, axis, 0, 0, tiled=True)]
    unnamed x38 -> x20, local copies, waits for them, and re-layouts: 13.6 us -> 1.53 us
    ppermute x1 -> x5, starting transfers between devices: 1.91 us -> 9.77 us  [the longest x4 7.85 us: halving_sum(): values = kept + lax.ppermute(sent, axis, pairs)]
    pallas_call x6, Pallas kernels: 29.1 us -> 30.6 us  [the longest x1 7.94 us: finish(): pl.pallas_call(lambda *refs: finish_kernel(pixels, channels, *refs), in_s...]
    broadcast_in_dim x3 -> x1, local copies, waits for them, and re-layouts: 1.53 us -> 0.07 us  [degrid(): ty_lanes = jnp.repeat(tile_ids // 32, KT)]
    ppermute x1 -> x5, waiting for transfers between devices: 7.82 us -> 7.8 us  [the longest x4 7.8 us: halving_sum(): values = kept + lax.ppermute(sent, axis, pairs)]
  transfers between devices with their start and end apart: 7 -> 8, of which waited for: 7 -> 7; matrix products, arithmetic and copies ran while one was open for 3% -> 3% of each run, Pallas kernels for 12% -> 15%
where the time goes in v2:
time: 102 us; the launch traced here: 101 us
  waiting for transfers between devices  34.9 us (34%)
  Pallas kernels  30.6 us (30%)
  starting transfers between devices  28.5 us (28%)
  between operations  2.42 us (2%)
  local copies, waits for them, and re-layouts  2.41 us (2%)
  other arithmetic  1.66 us (2%)
    all_to_all x3, waiting for transfers between devices, trade(): return lax.all_to_all(values, axis, 0, 0, tiled=True)  27.1 us
    all_to_all x3, starting transfers between devices, trade(): return lax.all_to_all(values, axis, 0, 0, tiled=True)  18.8 us
    pallas_call x1, Pallas kernels, finish(): pl.pallas_call(lambda *refs: finish_kernel(pixels, channels, *refs), in_s...  7.94 us
    ppermute x4, starting transfers between devices, halving_sum(): values = kept + lax.ppermute(sent, axis, pairs)  7.85 us
    ppermute x4, waiting for transfers between devices, halving_sum(): values = kept + lax.ppermute(sent, axis, pairs)  7.8 us
    pallas_call x1, Pallas kernels, blend(): pl.pallas_call(blend_kernel, grid=(4,), in_specs=[pl.BlockSpec(memory_spa...  7.68 us
    pallas_call x1, Pallas kernels, degrid(): pl.pallas_call(degrid_kernel, in_specs=[smem, smem] + [vmem] * 4 + [pl.Bl...  7.64 us
    pallas_call x1, Pallas kernels, gram_part(): pl.pallas_call(gram_kernel, in_specs=[vmem] * 3, out_specs=(hbm, hbm), ou...  3.53 us
  transfers between devices with their start and end apart: 8, of which 7 were waited for; matrix products, arithmetic and copies ran while one was open for 3% of the time, Pallas kernels for 15%

profile of v2, /device:TPU:8, one launch (start us, length us, event | category | flops | bytes accessed | tf_op | source)
XLA Modules:
  0.0 100.6 jit_solution(14348971113504713147)
XLA Ops:
  0.6 0.0 copy-start.2
  0.6 0.0 copy-start.3
  0.7 0.0 copy-start
  0.7 0.0 copy-start.8
  0.7 0.0 copy-start.9
  0.7 0.0 copy-start.1
  0.7 3.0 %pack_sky.1 = f32[16,16,8,128]{3,2,1,0:T(8,128)} custom-call(f32[16,32,512]{2,1,0:T(8,128)} %sky_ref.1), custom_call_target="tpu_custom_call" | custom-call | flops 3000000 | bytes 2097152 | tf_op jit(solution)/shard_map/pack_sky/pallas_call | solution.py:111
  3.7 10.4 %all-to-all-start = ((f32[16,16,8,128]{3,2,1,0:T(8,128)}), f32[16,16,8,128]{3,2,1,0:T(8,128)}, u32[]{:S(2)}, u32[]{:S(2)}) async-start(f32[16,16,8,128]{3,2,1,0:T(8,128)} %pack_sky.1), calls=%async_computation | async-start | bytes 2097152 | tf_op jit(solution)/shard_map/all_to_all | solution.py:516
  14.1 0.0 copy-done
  14.1 1.9 %collective-permute-start = (f32[16,8,512]{2,1,0:T(8,128)S(1)}, f32[16,8,512]{2,1,0:T(8,128)S(1)}, u32[]{:S(2)}, u32[]{:S(2)}) collective-permute-start(f32[16,8,512]{2,1,0:T(8,128)S(1)} %slice.3), channel_id=1, source_target_pairs={{0,16},{16,32},{32,48},{48,64},{64,80},{80,96},{96,112},{112,128},... | collective-permute-start | bytes 786440 | tf_op jit(solution)/shard_map/ppermute | solution.py:551
  16.0 0.0 copy-done.8
  16.1 0.1 broadcast_in_dim.2
  16.1 0.1 mul.105
  16.2 0.0 copy-done.9
  16.2 0.6 dynamic_slice.27.margin_ref
  16.8 0.1 fusion.11
  16.9 0.3 fusion.7
  17.2 0.0 copy-done.2
  17.2 0.0 copy-done.3
  17.2 0.0 copy-done.1
  17.2 7.6 %degrid.1 = f32[32,1024]{1,0:T(8,128)S(1)} custom-call(s32[32]{0:T(128)S(1)} %get-tuple-element.36.tx_ref, f32[2,16]{1,0:T(2,128)S(1)} %pad_maximum_fusion.1.turn_ref, f32[16,32,512]{2,1,0:T(8,128)S(1)} %copy-done, f32[2,32,512]{2,1,0:T(8,128)S(1)} %pad_maximum_fusion.phase_ref, f32[96,512]{1,0:T(8,128)S(1)} %copy-done.2, bf16[256,256]{1,0:T(8,128)(2,1)S(1)} %copy-done.3, ...), custom_call_target="tpu_custom_call" | custom-call | flops 3000000000 | bytes 6291456 | tf_op jit(solution)/shard_map/degrid/pallas_call | solution.py:486
  24.9 0.0 collective-permute-done.rim_ref
  24.9 0.0 copy-start.7
  24.9 0.7 copy-done.7
  25.6 7.7 %blend.1 = (f32[4,16,32,512]{3,2,1,0:T(8,128)}, f32[16,32,128]{2,1,0:T(8,128)}) custom-call(s32[1]{0:T(128)} %dynamic_slice.27.margin_ref, f32[16,32,512]{2,1,0:T(8,128)} %sky_ref.1, f32[16,8,512]{2,1,0:T(8,128)} %copy-done.7, f32[4,16,32,512]{3,2,1,0:T(8,128)} %dual_ref.1, bf16[512,160]{1,0:T(8,128)(2,1)} %constant.116.clone.down_ref, ...), custom_call_target="tpu_custom_call" | custom-call | flops 3000000000 | bytes 10485760 | tf_op jit(solution)/shard_map/blend/pallas_call | solution.py:345
  33.3 0.0 copy-start.5
  33.3 0.0 copy-start.6
  33.3 0.1 reshape_reshape.3
  33.4 1.7 %collective-permute-start.1 = (f32[8,2,1024]{2,1,0:T(2,128)S(1)}, f32[8,2,1024]{2,1,0:T(2,128)S(1)}, u32[]{:S(2)}, u32[]{:S(2)}) collective-permute-start(f32[8,2,1024]{2,1,0:T(2,128)S(1)} %dynamic-slice_bitcast_fusion), channel_id=1, source_target_pairs={{0,16},{16,0},{32,48},{48,32},{64,80},{80,64},{96,112},{112,96},{1... | collective-permute-start | bytes 196616 | tf_op jit(solution)/shard_map/ppermute | solution.py:528
  35.1 0.9 collective-permute-done.1
  36.0 8.3 %all-to-all-done = f32[16,16,8,128]{3,2,1,0:T(8,128)} async-done(((f32[16,16,8,128]{3,2,1,0:T(8,128)}), f32[16,16,8,128]{3,2,1,0:T(8,128)}, u32[]{:S(2)}, u32[]{:S(2)}) %all-to-all-start) | async-done | bytes 1048608 | tf_op jit(solution)/shard_map/all_to_all | solution.py:516
  44.3 3.5 %gram_part.1 = (f32[4,8,32,256]{3,2,1,0:T(8,128)}, f32[16,64,128]{2,1,0:T(8,128)}) custom-call(f32[2048,128]{1,0:T(8,128)} %bitcast.got_ref, f32[4,8,32,256]{3,2,1,0:T(8,128)} %bitcast.41, f32[16,32,128]{2,1,0:T(8,128)} %get-tuple-element.22.energy_ref), custom_call_target="tpu_custom_call" | custom-call | flops 400000000 | bytes 3145728 | tf_op jit(solution)/shard_map/gram_part/pallas_call | solution.py:156
  47.8 3.6 %all-to-all-start.1 = ((f32[16,64,128]{2,1,0:T(8,128)}), f32[16,64,128]{2,1,0:T(8,128)S(1)}, u32[]{:S(2)}, u32[]{:S(2)}) async-start(f32[16,64,128]{2,1,0:T(8,128)} %get-tuple-element.23), calls=%async_computation.1 | async-start | bytes 1048576 | tf_op jit(solution)/shard_map/all_to_all | solution.py:516
  51.4 1.4 %collective-permute-start.2 = (f32[4,2,1024]{2,1,0:T(2,128)S(1)}, f32[4,2,1024]{2,1,0:T(2,128)S(1)}, u32[]{:S(2)}, u32[]{:S(2)}) collective-permute-start(f32[4,2,1024]{2,1,0:T(2,128)S(1)} %dynamic-slice_bitcast_fusion.1), channel_id=1, source_target_pairs={{0,128},{16,144},{32,160},{48,176},{64,192},{80,208},{96,224},{112... | collective-permute-start | bytes 98312 | tf_op jit(solution)/shard_map/ppermute | solution.py:528
  52.9 2.6 %collective-permute-done.2 = f32[4,2,1024]{2,1,0:T(2,128)S(1)} collective-permute-done((f32[4,2,1024]{2,1,0:T(2,128)S(1)}, f32[4,2,1024]{2,1,0:T(2,128)S(1)}, u32[]{:S(2)}, u32[]{:S(2)}) %collective-permute-start.2) | collective-permute-done | bytes 32800 | tf_op jit(solution)/shard_map/ppermute | solution.py:528
  55.5 1.6 %collective-permute-start.3 = (f32[2,2,1024]{2,1,0:T(2,128)S(1)}, f32[2,2,1024]{2,1,0:T(2,128)S(1)}, u32[]{:S(2)}, u32[]{:S(2)}) collective-permute-start(f32[2,2,1024]{2,1,0:T(2,128)S(1)} %dynamic-slice_bitcast_fusion.2), channel_id=1, source_target_pairs={{0,32},{16,48},{32,0},{48,16},{64,96},{80,112},{96,64},{112,80},{1... | collective-permute-start | bytes 49160 | tf_op jit(solution)/shard_map/ppermute | solution.py:528
  57.1 2.2 %collective-permute-done.3 = f32[2,2,1024]{2,1,0:T(2,128)S(1)} collective-permute-done((f32[2,2,1024]{2,1,0:T(2,128)S(1)}, f32[2,2,1024]{2,1,0:T(2,128)S(1)}, u32[]{:S(2)}, u32[]{:S(2)}) %collective-permute-start.3) | collective-permute-done | bytes 16416 | tf_op jit(solution)/shard_map/ppermute | solution.py:528
  59.4 3.2 %collective-permute-start.4 = (f32[1,2,1024]{2,1,0:T(2,128)S(1)}, f32[1,2,1024]{2,1,0:T(2,128)S(1)}, u32[]{:S(2)}, u32[]{:S(2)}) collective-permute-start(f32[1,2,1024]{2,1,0:T(2,128)S(1)} %constant_dynamic-slice_fusion), channel_id=1, source_target_pairs={{0,64},{16,80},{32,96},{48,112},{64,0},{80,16},{96,32},{112,48},{1... | collective-permute-start | bytes 24584 | tf_op jit(solution)/shard_map/ppermute | solution.py:528
  62.5 2.1 %collective-permute-done.4 = f32[1,2,1024]{2,1,0:T(2,128)S(1)} collective-permute-done((f32[1,2,1024]{2,1,0:T(2,128)S(1)}, f32[1,2,1024]{2,1,0:T(2,128)S(1)}, u32[]{:S(2)}, u32[]{:S(2)}) %collective-permute-start.4) | collective-permute-done | bytes 8224 | tf_op jit(solution)/shard_map/ppermute | solution.py:528
  64.6 5.0 %all-to-all-done.1.got_ref = f32[16,64,128]{2,1,0:T(8,128)S(1)} async-done(((f32[16,64,128]{2,1,0:T(8,128)}), f32[16,64,128]{2,1,0:T(8,128)S(1)}, u32[]{:S(2)}, u32[]{:S(2)}) %all-to-all-start.1) | async-done | bytes 524320 | tf_op jit(solution)/shard_map/all_to_all | solution.py:516
  69.6 0.9 sum_copies.1
  70.4 4.8 %all-to-all-start.2 = ((f32[16,64,128]{2,1,0:T(8,128)}), f32[16,64,128]{2,1,0:T(8,128)S(1)}, u32[]{:S(2)}, u32[]{:S(2)}) async-start(f32[16,64,128]{2,1,0:T(8,128)} %sum_copies.1), calls=%async_computation.2 | async-start | bytes 1048576 | tf_op jit(solution)/shard_map/all_to_all | solution.py:516
  75.9 0.0 copy-done.5
  75.9 0.0 copy-done.6
  75.9 0.6 multiply_reduce_fusion
  77.2 0.6 multiply_subtract_fusion
  77.8 13.8 %all-to-all-done.2.refs_0_ = f32[16,64,128]{2,1,0:T(8,128)S(1)} async-done(((f32[16,64,128]{2,1,0:T(8,128)}), f32[16,64,128]{2,1,0:T(8,128)S(1)}, u32[]{:S(2)}, u32[]{:S(2)}) %all-to-all-start.2) | async-done | bytes 524320 | tf_op jit(solution)/shard_map/all_to_all | solution.py:516
  91.7 0.0 copy-start.4
  91.7 0.8 copy-done.4
  92.4 7.9 %finish.1 = (f32[4,16,32,512]{3,2,1,0:T(8,128)}, f32[1024,256]{1,0:T(8,128)}) custom-call(f32[16,64,128]{2,1,0:T(8,128)} %copy-done.4, f32[4,32,512]{2,1,0:T(8,128)} %refs_1_.1, f32[4,16,32,512]{3,2,1,0:T(8,128)} %get-tuple-element.26.refs_2_, f32[1024,256]{1,0:T(8,128)} %bitcast.46), custom_call_target="tpu_custom_call" | custom-call | flops 2000000000 | bytes 8388608 | tf_op jit(solution)/shard_map/finish/pallas_call | solution.py:271
  (12 shorter events, 0.2 us)
Async XLA Ops:
  0.6 16.5 %copy-start.2 = (f32[96,512]{1,0:T(8,128)S(1)}, f32[96,512]{1,0:T(8,128)}, u32[]{:S(2)}) copy-start(f32[96,512]{1,0:T(8,128)} %constant.114.clone.column_ref) | copy-start | bytes 589828
  0.6 16.5 %copy-start.3 = (bf16[256,256]{1,0:T(8,128)(2,1)S(1)}, bf16[256,256]{1,0:T(8,128)(2,1)}, u32[]{:S(2)}) copy-start(bf16[256,256]{1,0:T(8,128)(2,1)} %constant.115.clone.row_ref) | copy-start | bytes 393220
  0.7 13.4 %copy-start = (f32[16,32,512]{2,1,0:T(8,128)S(1)}, f32[16,32,512]{2,1,0:T(8,128)}, u32[]{:S(2)}) copy-start(f32[16,32,512]{2,1,0:T(8,128)} %sky_ref.1) | copy-start | bytes 3145732
  0.7 15.4 %copy-start.8 = (s32[1,32]{1,0:T(1,128)S(1)}, s32[1,32]{1,0:T(1,128)}, u32[]{:S(2)}) copy-start(s32[1,32]{1,0:T(1,128)} %param.20) | copy-start | bytes 388
  0.7 15.5 %copy-start.9 = (s32[16]{0:T(128)S(1)}, s32[16]{0:T(128)}, u32[]{:S(2)}) copy-start(s32[16]{0:T(128)} %param.15) | copy-start | bytes 196
  0.7 16.5 %copy-start.1 = (bf16[1,32,32,512]{3,2,1,0:T(8,128)(2,1)S(1)}, bf16[1,32,32,512]{3,2,1,0:T(8,128)(2,1)}, u32[]{:S(2)}) copy-start(bf16[1,32,32,512]{3,2,1,0:T(8,128)(2,1)} %param.19) | copy-start | bytes 3145732
  3.7 40.6 %all-to-all-start = ((f32[16,16,8,128]{3,2,1,0:T(8,128)}), f32[16,16,8,128]{3,2,1,0:T(8,128)}, u32[]{:S(2)}, u32[]{:S(2)}) async-start(f32[16,16,8,128]{3,2,1,0:T(8,128)} %pack_sky.1), calls=%async_computation | async-start | bytes 2097152 | tf_op jit(solution)/shard_map/all_to_all | solution.py:516
  14.1 10.8 %collective-permute-start = (f32[16,8,512]{2,1,0:T(8,128)S(1)}, f32[16,8,512]{2,1,0:T(8,128)S(1)}, u32[]{:S(2)}, u32[]{:S(2)}) collective-permute-start(f32[16,8,512]{2,1,0:T(8,128)S(1)} %slice.3), channel_id=1, source_target_pairs={{0,16},{16,32},{32,48},{48,64},{64,80},{80,96},{96,112},{112,128},... | collective-permute-start | bytes 786440 | tf_op jit(solution)/shard_map/ppermute | solution.py:551
  24.9 0.7 copy-start.7
  33.3 42.6 %copy-start.5 = (f32[1,2,1024]{2,1,0:T(2,128)S(1)}, f32[1,2,1024]{2,1,0:T(2,128)}, u32[]{:S(2)}) copy-start(f32[1,2,1024]{2,1,0:T(2,128)} %param.22) | copy-start | bytes 24580
  33.3 42.7 %copy-start.6 = (f32[1,2,1024]{2,1,0:T(2,128)S(1)}, f32[1,2,1024]{2,1,0:T(2,128)}, u32[]{:S(2)}) copy-start(f32[1,2,1024]{2,1,0:T(2,128)} %param.21) | copy-start | bytes 24580
  33.4 2.6 %collective-permute-start.1 = (f32[8,2,1024]{2,1,0:T(2,128)S(1)}, f32[8,2,1024]{2,1,0:T(2,128)S(1)}, u32[]{:S(2)}, u32[]{:S(2)}) collective-permute-start(f32[8,2,1024]{2,1,0:T(2,128)S(1)} %dynamic-slice_bitcast_fusion), channel_id=1, source_target_pairs={{0,16},{16,0},{32,48},{48,32},{64,80},{80,64},{96,112},{112,96},{1... | collective-permute-start | bytes 196616 | tf_op jit(solution)/shard_map/ppermute | solution.py:528
  47.8 21.7 %all-to-all-start.1 = ((f32[16,64,128]{2,1,0:T(8,128)}), f32[16,64,128]{2,1,0:T(8,128)S(1)}, u32[]{:S(2)}, u32[]{:S(2)}) async-start(f32[16,64,128]{2,1,0:T(8,128)} %get-tuple-element.23), calls=%async_computation.1 | async-start | bytes 1048576 | tf_op jit(solution)/shard_map/all_to_all | solution.py:516
  51.4 4.0 %collective-permute-start.2 = (f32[4,2,1024]{2,1,0:T(2,128)S(1)}, f32[4,2,1024]{2,1,0:T(2,128)S(1)}, u32[]{:S(2)}, u32[]{:S(2)}) collective-permute-start(f32[4,2,1024]{2,1,0:T(2,128)S(1)} %dynamic-slice_bitcast_fusion.1), channel_id=1, source_target_pairs={{0,128},{16,144},{32,160},{48,176},{64,192},{80,208},{96,224},{112... | collective-permute-start | bytes 98312 | tf_op jit(solution)/shard_map/ppermute | solution.py:528
  55.5 3.8 %collective-permute-start.3 = (f32[2,2,1024]{2,1,0:T(2,128)S(1)}, f32[2,2,1024]{2,1,0:T(2,128)S(1)}, u32[]{:S(2)}, u32[]{:S(2)}) collective-permute-start(f32[2,2,1024]{2,1,0:T(2,128)S(1)} %dynamic-slice_bitcast_fusion.2), channel_id=1, source_target_pairs={{0,32},{16,48},{32,0},{48,16},{64,96},{80,112},{96,64},{112,80},{1... | collective-permute-start | bytes 49160 | tf_op jit(solution)/shard_map/ppermute | solution.py:528
  59.4 5.2 %collective-permute-start.4 = (f32[1,2,1024]{2,1,0:T(2,128)S(1)}, f32[1,2,1024]{2,1,0:T(2,128)S(1)}, u32[]{:S(2)}, u32[]{:S(2)}) collective-permute-start(f32[1,2,1024]{2,1,0:T(2,128)S(1)} %constant_dynamic-slice_fusion), channel_id=1, source_target_pairs={{0,64},{16,80},{32,96},{48,112},{64,0},{80,16},{96,32},{112,48},{1... | collective-permute-start | bytes 24584 | tf_op jit(solution)/shard_map/ppermute | solution.py:528
  70.4 21.2 %all-to-all-start.2 = ((f32[16,64,128]{2,1,0:T(8,128)}), f32[16,64,128]{2,1,0:T(8,128)S(1)}, u32[]{:S(2)}, u32[]{:S(2)}) async-start(f32[16,64,128]{2,1,0:T(8,128)} %sum_copies.1), calls=%async_computation.2 | async-start | bytes 1048576 | tf_op jit(solution)/shard_map/all_to_all | solution.py:516
  91.7 0.8 copy-start.4

commit v3 on v2

v3 whole, which is shorter than its diff:
```python
import math

import jax
import jax.numpy as jnp
import ml_dtypes
import numpy as np
from jax import lax
from jax.experimental import pallas as pl
from jax.experimental.pallas import tpu as pltpu
from jax.sharding import PartitionSpec as P

NSTEP = 5
KT = 16
MIB = 1 << 20
ROOM = 24

low_taps = (
    -0.010597401784997278,
    0.032883011666982945,
    0.030841381835986965,
    -0.18703481171888114,
    -0.02798376941698385,
    0.6308807679295904,
    0.7148465705525415,
    0.23037781330885523,
)
high_taps = tuple(((-1.0) ** offset * low_taps[7 - offset] for offset in range(8)))
f32 = jnp.float32
bf16 = jnp.bfloat16


def params(mib):
    return pltpu.CompilerParams(vmem_limit_bytes=int(mib * MIB))


def cost(flops, nbytes):
    return pl.CostEstimate(flops=int(flops), bytes_accessed=int(nbytes), transcendentals=0)


def halves(values):
    upper = values.astype(bf16)
    return upper, (values - upper.astype(f32)).astype(bf16)


def host_halves(values):
    values = values.astype(np.float32)
    upper = values.astype(ml_dtypes.bfloat16)
    return upper, (values - upper.astype(np.float32)).astype(ml_dtypes.bfloat16)


def mm(a, b):
    return jnp.dot(a, b, preferred_element_type=f32)


def mm_t(a, b):
    return lax.dot_general(a, b, (((1,), (1,)), ((), ())), preferred_element_type=f32)


def mm3_right(a, bh, bl):
    ah, al = halves(a)
    return mm(ah, bh) + (mm(ah, bl) + mm(al, bh))


def swap_chunks(parts, width):
    count = len(parts)
    lane = lax.broadcasted_iota(jnp.int32, parts[0].shape, len(parts[0].shape) - 1)
    axis = len(parts[0].shape) - 1
    step = count // 2
    while step:
        span = step * width
        first = (lane // span) % 2 == 0
        out = list(parts)
        for a in range(count):
            if a & step:
                continue
            b = a | step
            out[a] = jnp.where(first, parts[a], pltpu.roll(parts[b], span, axis))
            out[b] = jnp.where(first, pltpu.roll(parts[a], 128 - span, axis), parts[b])
        parts = out
        step //= 2
    return parts


def pack_kernel(sky_in, packed_out, rim_out, sky_ref, packed_ref, in_sems, out_sems):
    fours = [slice(4 * k, 4 * k + 4) for k in range(4)]
    coming = [
        pltpu.make_async_copy(sky_in.at[four], sky_ref.at[four], in_sems.at[k])
        for k, four in enumerate(fours)
    ]
    going = [
        pltpu.make_async_copy(packed_ref.at[:, four], packed_out.at[:, four], out_sems.at[k])
        for k, four in enumerate(fours)
    ]
    going.append(pltpu.make_async_copy(sky_ref.at[:, 24:, :], rim_out, out_sems.at[4]))
    for copy in coming:
        copy.start()
    for k, four in enumerate(fours):
        coming[k].wait()
        for quarter in range(4):
            lanes = slice(128 * quarter, 128 * quarter + 128)
            parts = [sky_ref[four, 8 * j : 8 * j + 8, lanes] for j in range(4)]
            for s, done in enumerate(swap_chunks(parts, 32)):
                packed_ref[4 * quarter + s, four] = done
        going[k].start()
    going[4].start()
    for copy in going:
        copy.wait()


def pack_sky(sky):
    hbm = pl.BlockSpec(memory_space=pl.ANY)
    return pl.pallas_call(
        pack_kernel,
        in_specs=[hbm],
        out_specs=(hbm, hbm),
        out_shape=(
            jax.ShapeDtypeStruct((16, 16, 8, 128), f32),
            jax.ShapeDtypeStruct((16, 8, 512), f32),
        ),
        scratch_shapes=[
            pltpu.VMEM((16, 32, 512), f32),
            pltpu.VMEM((16, 16, 8, 128), f32),
            pltpu.SemaphoreType.DMA((4,)),
            pltpu.SemaphoreType.DMA((5,)),
        ],
        compiler_params=params(60),
        cost_estimate=cost(3e6, 2 * MIB),
        name="pack_sky",
    )(sky)


def gram_kernel(
    got_ref, dual_ref, kept_ref, other_ref, y_out, part_out, y_ref, sum_ref, gram_ref, sems
):
    sum_ref[...] = kept_ref[...] + other_ref[...]
    copies = [pltpu.make_async_copy(sum_ref, part_out.at[:, :16], sems.at[8])]
    copies[0].start()
    total = jnp.zeros((256, 256), f32)
    cross = jnp.zeros((256, 256), f32)
    held = []
    for low in range(8):
        seen = got_ref[pl.ds(low, 256, stride=8), :].T
        right = dual_ref[:, low].reshape(128, 256) + 0.5 * seen
        rh, rl = halves(right)
        y_ref[0, :, low] = rh.reshape(4, 32, 256)
        y_ref[1, :, low] = rl.reshape(4, 32, 256)
        copies.append(pltpu.make_async_copy(y_ref.at[:, :, low], y_out.at[:2, :, low], sems.at[low]))
        copies[-1].start()
        held.append((rh, rl))
        if low % 4 == 3:
            rh = jnp.concatenate([upper for upper, _ in held], axis=0)
            rl = jnp.concatenate([lower for _, lower in held], axis=0)
            held = []
            lh = rh.T
            total = total + mm(lh, rh)
            cross = cross + mm(lh, rl)
    total = total + (cross + cross.T)
    gram_ref[:, 16:, :] = jnp.zeros((16, 8, 128), f32)
    for peer in range(16):
        turned = total[16 * peer : 16 * peer + 16, :]
        if peer:
            turned = pltpu.roll(turned, 256 - 16 * peer, 1)
        gram_ref[peer, :16, :] = turned[:, :128]
        gram_ref[peer, 16:, :16] = turned[:8, 128:144]
        gram_ref[peer, 16:, 16:32] = turned[8:, 128:144]
    copies.append(pltpu.make_async_copy(gram_ref, part_out.at[:, 16:], sems.at[9]))
    copies[-1].start()
    for copy in copies:
        copy.wait()


def gram_part(got, dual, kept, other):
    vmem = pl.BlockSpec(memory_space=pltpu.VMEM)
    hbm = pl.BlockSpec(memory_space=pl.ANY)
    return pl.pallas_call(
        gram_kernel,
        in_specs=[vmem] * 4,
        out_specs=(hbm, hbm),
        out_shape=(
            jax.ShapeDtypeStruct((2 * ROOM, 4, 8, 32, 256), bf16),
            jax.ShapeDtypeStruct((16, 40, 128), f32),
        ),
        scratch_shapes=[
            pltpu.VMEM((2, 4, 8, 32, 256), bf16),
            pltpu.VMEM((16, 16, 128), f32),
            pltpu.VMEM((16, 24, 128), f32),
            pltpu.SemaphoreType.DMA((10,)),
        ],
        compiler_params=params(40),
        cost_estimate=cost(4e8, 3 * MIB),
        name="gram_part",
    )(got, dual, kept, other)


def sum_kernel(got_ref, out_ref):
    halves_of = [got_ref[0, :16], got_ref[1, :16]]
    gram = got_ref[0, 16:]
    for peer in range(1, 16):
        gram = gram + got_ref[peer, 16:]
        if peer > 1:
            halves_of[peer % 2] = halves_of[peer % 2] + got_ref[peer, :16]
    for peer in range(16):
        out_ref[peer, :16] = halves_of[0]
        out_ref[peer, 16:32] = halves_of[1]
        out_ref[peer, 32:] = gram


def sum_copies(got):
    return pl.pallas_call(
        sum_kernel,
        out_shape=jax.ShapeDtypeStruct((16, 56, 128), f32),
        compiler_params=params(16),
        cost_estimate=cost(1e6, MIB),
        name="sum_copies",
    )(got)


def finish_kernel(
    pixels,
    channels,
    got_ref,
    weight_in,
    blend_in,
    y_in,
    wave_out,
    mixed_out,
    weight_ref,
    blend_ref,
    wave_ref,
    y_ref,
    mixed_ref,
    in_sems,
    out_sems,
):
    coming = [
        pltpu.make_async_copy(weight_in, weight_ref, in_sems.at[5]),
        pltpu.make_async_copy(y_in.at[:2], y_ref, in_sems.at[4]),
    ]
    arrived = [
        pltpu.make_async_copy(blend_in.at[band], blend_ref.at[band], in_sems.at[band])
        for band in range(4)
    ]
    for copy in coming + arrived:
        copy.start()
    going = []

    def wave(band):
        if band == 0:
            coming[0].wait()
        arrived[band].wait()
        for part in range(4):
            rows = slice(8 * part, 8 * part + 8)
            for q in range(4):
                lanes = slice(128 * q, 128 * q + 128)
                energy = got_ref[4 * band + part, 8 * q : 8 * q + 8, :]
                ratio = jnp.sqrt(energy * (1.0 / channels)) / weight_ref[band, rows, lanes]
                scale = 1.0 / jnp.maximum(1.0, ratio)
                wave_ref[band, :, rows, lanes] = blend_ref[band, :, rows, lanes] * scale[None]
        copy = pltpu.make_async_copy(wave_ref.at[band], wave_out.at[band], out_sems.at[band])
        copy.start()
        going.append(copy)

    size = 256
    rows = lax.broadcasted_iota(jnp.int32, (size, size), 0)
    cols = lax.broadcasted_iota(jnp.int32, (size, size), 1)
    blocks = []
    for peer in range(16):
        ninth = jnp.concatenate([got_ref[peer, 48:, :], jnp.zeros((8, 128), f32)], axis=0)
        second = jnp.concatenate([jnp.zeros((8, 128), f32), pltpu.roll(got_ref[peer, 48:, :], 112, 1)], axis=0)
        ninth = ninth + second
        block = jnp.concatenate([got_ref[peer, 32:48, :], ninth], axis=1)
        blocks.append(pltpu.roll(block, 16 * peer, 1) if peer else block)
    half = jnp.concatenate(blocks, axis=0)
    known = (cols // 16 - rows // 16) % 16 < 9
    gram = jnp.where(known, half, half.T)
    shifted = (rows == cols).astype(f32) + gram * (1.0 / pixels)
    frob = jnp.sqrt(jnp.sum(shifted * shifted, keepdims=True))

    def middle_of(product):
        return jnp.where(rows == cols, 1.5, 0.0) - 0.5 * product

    product = shifted / frob
    middle = middle_of(product)
    inverse = middle
    for turn in range(1, NSTEP):
        mh, ml = halves(middle)
        if turn == 1:
            first = mm3_right(product, mh, ml)
        else:
            both = mm3_right(jnp.concatenate([product, inverse], axis=0), mh, ml)
            first, inverse = both[:size], both[size:]
        if turn > 2:
            wave(2 * turn - 6)
            wave(2 * turn - 5)
        product = mm3_right(first, mh, ml)
        middle = middle_of(product)
    mh, ml = halves(middle)
    mh, ml = halves(mm3_right(inverse, mh, ml) * lax.rsqrt(frob))
    coming[1].wait()
    for block in range(4):
        span = pl.ds(256 * block, 256)
        yh = y_ref[0, span, :]
        mixed_ref[span, :] = mm(yh, mh) + (mm(yh, ml) + mm(y_ref[1, span, :], mh))
        copy = pltpu.make_async_copy(mixed_ref.at[span], mixed_out.at[span], out_sems.at[4 + block])
        copy.start()
        going.append(copy)
    for copy in going:
        copy.wait()


def finish(got, weights, blended, y, pixels, channels):
    shape = (4, 16, 32, 512)
    hbm = pl.BlockSpec(memory_space=pl.ANY)
    return pl.pallas_call(
        lambda *refs: finish_kernel(pixels, channels, *refs),
        in_specs=[pl.BlockSpec(memory_space=pltpu.VMEM)] + [hbm] * 3,
        out_specs=(hbm, hbm),
        out_shape=(
            jax.ShapeDtypeStruct(shape, f32),
            jax.ShapeDtypeStruct((1024, 256), f32),
        ),
        scratch_shapes=[
            pltpu.VMEM(weights.shape, f32),
            pltpu.VMEM(shape, f32),
            pltpu.VMEM(shape, f32),
            pltpu.VMEM((2, 1024, 256), bf16),
            pltpu.VMEM((1024, 256), f32),
            pltpu.SemaphoreType.DMA((6,)),
            pltpu.SemaphoreType.DMA((8,)),
        ],
        compiler_params=params(40),
        cost_estimate=cost(2e9, 8 * MIB),
        name="finish",
    )(got, weights, blended, y)


def filter_tables(first, last):
    both = (low_taps, high_taps)
    count = last - first
    down = np.zeros((2, 4, count, 4, count + 8))
    across = np.zeros((256, 2, 128))
    for which, taps in enumerate(both):
        for m, tap in enumerate(taps):
            for row in range(count):
                for ch in range(4):
                    down[which, ch, row, ch, 8 + row - m] = tap
            for col in range(128):
                across[128 + col - m, which, col] = 0.5 * tap
    down = np.stack(host_halves(down.reshape(8 * count, 4 * count + 32)))
    return down, np.concatenate(host_halves(across.reshape(256, 256)))


def copy_in(source, target, sem):
    copy = pltpu.make_async_copy(source, target, sem)
    copy.start()
    return copy


def blend_group(pieces, four, first, down_ref, across_ref, dual_ref, blend_ref, energy_ref):
    count = dual_ref.shape[2]
    eh, el = halves(jnp.concatenate(pieces, axis=0))
    dh, dl = down_ref[0], down_ref[1]
    filtered = mm(dh, eh) + (mm(dh, el) + mm(dl, eh))
    vh, vl = halves(filtered)
    for j in range(4):
        if j:
            lanes = slice(128 * j - 128, 128 * j + 128)
            ah, al = across_ref[:256, :], across_ref[256:, :]
        else:
            lanes = slice(0, 128)
            ah, al = across_ref[128:256, :], across_ref[384:, :]
        done = mm(vh[:, lanes], ah) + (mm(vl[:, lanes], ah) + mm(vh[:, lanes], al))
        here = slice(128 * j, 128 * j + 128)
        place = slice(8 * (j % 2), 8 * (j % 2) + 8)
        for band in range(4):
            part = done[4 * count * (band // 2) : 4 * count * (band // 2) + 4 * count]
            part = part[:, 128 * (band % 2) : 128 * (band % 2) + 128].reshape(4, count, 128)
            blended = dual_ref[band, four, :, here] + part
            blend_ref[band, four, :, here] = blended
            squares = jnp.sum(blended * blended, axis=0)
            for strip in range(count // 8):
                energy_ref[j // 2, 4 * band + first // 8 + strip, place, :] += squares[
                    8 * strip : 8 * strip + 8
                ]


def inner_kernel(
    sky_in,
    dual_in,
    down_in,
    across_in,
    blend_out,
    energy_out,
    sky_ref,
    dual_ref,
    down_ref,
    across_ref,
    blend_ref,
    energy_ref,
    in_sems,
    out_sems,
):
    fours = [slice(4 * k, 4 * k + 4) for k in range(4)]
    down = copy_in(down_in, down_ref, in_sems.at[0])
    sky, dual = [], []
    for k, four in enumerate(fours):
        sky.append(copy_in(sky_in.at[four], sky_ref.at[four], in_sems.at[2 + k]))
        if k == 0:
            across = copy_in(across_in, across_ref, in_sems.at[1])
        dual.append(copy_in(dual_in.at[:, four, 8:], dual_ref.at[:, four], in_sems.at[6 + k]))
    energy_ref[...] = jnp.zeros_like(energy_ref)
    down.wait()
    going = []
    for k, four in enumerate(fours):
        sky[k].wait()
        if k == 0:
            across.wait()
        dual[k].wait()
        pieces = [sky_ref[c] for c in range(4 * k, 4 * k + 4)]
        blend_group(pieces, four, 8, down_ref, across_ref, dual_ref, blend_ref, energy_ref)
        going.append(copy_in(blend_ref.at[:, four], blend_out.at[:4, four, 8:], out_sems.at[k]))
    going.append(copy_in(energy_ref, energy_out, out_sems.at[4]))
    for copy in going:
        copy.wait()


def outer_kernel(
    margins_ref,
    sky_in,
    rim_in,
    dual_in,
    down_in,
    across_in,
    energy_in,
    blend_in,
    blend_out,
    kept_out,
    sent_out,
    sky_ref,
    rim_ref,
    dual_ref,
    down_ref,
    across_ref,
    blend_ref,
    energy_ref,
    in_sems,
    out_sems,
):
    margin = margins_ref[lax.axis_index("facet")]
    half = lax.axis_index("chan") % 2
    row = lax.broadcasted_iota(jnp.int32, (8, 512), 0)
    kept = row >= 8 - margin
    coming = [
        copy_in(source, target, in_sems.at[k])
        for k, (source, target) in enumerate(
            (
                (rim_in, rim_ref),
                (sky_in.at[:, :8], sky_ref),
                (down_in, down_ref),
                (across_in, across_ref),
                (energy_in, energy_ref),
                (dual_in.at[:, :, :8], dual_ref),
            )
        )
    ]
    for copy in coming:
        copy.wait()
    going = []
    for k in range(4):
        four = slice(4 * k, 4 * k + 4)
        pieces = []
        for c in range(4 * k, 4 * k + 4):
            pieces += [jnp.where(kept, rim_ref[c], 0.0), sky_ref[c]]
        blend_group(pieces, four, 0, down_ref, across_ref, dual_ref, blend_ref, energy_ref)
        going.append(copy_in(blend_ref.at[:, four], blend_out.at[:4, four, :8], out_sems.at[k]))
    for number, (which, target) in enumerate(((1 - half, sent_out), (half, kept_out))):
        going.append(copy_in(energy_ref.at[which], target, out_sems.at[4 + number]))
    for copy in going:
        copy.wait()


def blend_inner(sky, dual):
    down, across = (jnp.asarray(t) for t in filter_tables(8, 32))
    hbm = pl.BlockSpec(memory_space=pl.ANY)
    return pl.pallas_call(
        inner_kernel,
        in_specs=[hbm] * 4,
        out_specs=(hbm, hbm),
        out_shape=(
            jax.ShapeDtypeStruct((ROOM, 16, 32, 512), f32),
            jax.ShapeDtypeStruct((2, 16, 16, 128), f32),
        ),
        scratch_shapes=[
            pltpu.VMEM(sky.shape, f32),
            pltpu.VMEM((4, 16, 24, 512), f32),
            pltpu.VMEM(down.shape, bf16),
            pltpu.VMEM(across.shape, bf16),
            pltpu.VMEM((4, 16, 24, 512), f32),
            pltpu.VMEM((2, 16, 16, 128), f32),
            pltpu.SemaphoreType.DMA((10,)),
            pltpu.SemaphoreType.DMA((5,)),
        ],
        compiler_params=params(60),
        cost_estimate=cost(2e9, 8 * MIB),
        name="blend_inner",
    )(sky, dual, down, across)


def blend_outer(margins, sky, rim, dual, energy, blended):
    down, across = (jnp.asarray(t) for t in filter_tables(0, 8))
    hbm = pl.BlockSpec(memory_space=pl.ANY)
    return pl.pallas_call(
        outer_kernel,
        in_specs=[pl.BlockSpec(memory_space=pltpu.SMEM)] + [hbm] * 7,
        out_specs=(hbm, hbm, hbm),
        out_shape=(
            jax.ShapeDtypeStruct(blended.shape, f32),
            jax.ShapeDtypeStruct((16, 16, 128), f32),
            jax.ShapeDtypeStruct((16, 16, 128), f32),
        ),
        input_output_aliases={7: 0},
        scratch_shapes=[
            pltpu.VMEM((16, 8, 512), f32),
            pltpu.VMEM((16, 8, 512), f32),
            pltpu.VMEM((4, 16, 8, 512), f32),
            pltpu.VMEM(down.shape, bf16),
            pltpu.VMEM(across.shape, bf16),
            pltpu.VMEM((4, 16, 8, 512), f32),
            pltpu.VMEM((2, 16, 16, 128), f32),
            pltpu.SemaphoreType.DMA((6,)),
            pltpu.SemaphoreType.DMA((6,)),
        ],
        compiler_params=params(60),
        cost_estimate=cost(1e9, 4 * MIB),
        name="blend_outer",
    )(margins, sky, rim, dual, down, across, energy, blended)


def degrid_tables(side):
    column = np.arange(side, dtype=np.int64)[None, :]
    kx = np.arange(KT, dtype=np.int64)[:, None]
    tile = np.arange(side // KT, dtype=np.int64)[:, None]
    inner = (kx * column % side) * (2.0 * np.pi / side)
    outer = (KT * tile * column % side) * (2.0 * np.pi / side)
    columns = np.concatenate([np.cos(inner), np.sin(inner), np.cos(outer), np.sin(outer)])
    ky, row = np.arange(16)[:, None], np.arange(32)[None, :]
    turn = ky * row * (2.0 * np.pi / side)
    whole = np.zeros((16, 4, 2, 2, 4, 32))
    for ch in range(4):
        whole[:, ch, 0, 0, ch, :] = np.cos(turn)
        whole[:, ch, 0, 1, ch, :] = np.sin(turn)
        whole[:, ch, 1, 0, ch, :] = -np.sin(turn)
        whole[:, ch, 1, 1, ch, :] = np.cos(turn)
    rows = np.concatenate(host_halves(whole.reshape(128, 256)))
    shift = np.arange(32)[:, None] * np.arange(32)[None, :] * (2.0 * np.pi / 32)
    shift = np.concatenate(host_halves(np.concatenate([np.cos(shift), np.sin(shift)])))
    turn = np.arange(16) * (2.0 * np.pi / 16)
    turn = np.stack([np.cos(turn), np.sin(turn)]).astype(np.float32)
    return columns.astype(np.float32), rows, shift, turn


def channel_at(place):
    b0, b3, b1, b2 = ((place >> k) & 1 for k in (3, 2, 1, 0))
    return b0 + 2 * b1 + 4 * b2 + 8 * b3


def degrid_kernel(
    tile_ref,
    turn_ref,
    sky_ref,
    shift_ref,
    column_ref,
    row_ref,
    weight_in,
    out_ref,
    xh_ref,
    xl_ref,
    table_ref,
    t_ref,
    u_ref,
    weight_ref,
    sem,
):
    coming = pltpu.make_async_copy(weight_in, weight_ref, sem.at[0])
    coming.start()
    facet = lax.axis_index("facet")
    inner_cos, inner_sin = column_ref[:KT, :], column_ref[KT : 2 * KT, :]
    block = lax.broadcasted_iota(jnp.int32, (8, 512), 1) // KT
    ty = jnp.zeros((8, 512), jnp.int32)
    for b in range(32):
        tile = tile_ref[0, b]
        ty = jnp.where(block == b, tile // 32, ty)
        outer_cos = column_ref[pl.ds(2 * KT + tile % 32, 1), :]
        outer_sin = column_ref[pl.ds(2 * KT + 32 + tile % 32, 1), :]
        rows = slice(KT * b, KT * b + KT)
        both = (
            inner_cos * outer_cos - inner_sin * outer_sin,
            inner_sin * outer_cos + inner_cos * outer_sin,
        )
        for k, values in enumerate(both):
            upper, lower = halves(values)
            table_ref[2 * k, rows, :] = upper
            table_ref[2 * k + 1, rows, :] = lower
    for place in range(16):
        xh, xl = halves(sky_ref[channel_at(place)])
        xh_ref[32 * place : 32 * place + 32, :] = xh
        xl_ref[32 * place : 32 * place + 32, :] = xl
    wanted = lax.broadcasted_iota(jnp.int32, (32, 512), 0) == ty[:1, :]
    phase = mm(shift_ref[...], wanted.astype(f32).astype(bf16))
    phase = (phase[:64] + phase[64:]).reshape(2, 32, 512)
    cos_h, cos_l, sin_h, sin_l = (table_ref[k] for k in range(4))
    row_h, row_l = row_ref[:128, :], row_ref[128:, :]
    for half in range(4):
        rows = slice(128 * half, 128 * half + 128)
        xh, xl = xh_ref[rows, :], xl_ref[rows, :]
        gc = mm_t(xh, cos_h) + (mm_t(xl, cos_h) + mm_t(xh, cos_l))
        gs = mm_t(xh, sin_h) + (mm_t(xl, sin_h) + mm_t(xh, sin_l))
        gc, gs = gc.reshape(4, 32, 512), gs.reshape(4, 32, 512)
        pc, ps = phase[0][None], phase[1][None]
        pre = (gc * pc - gs * ps).reshape(128, 512)
        pim = (-(gs * pc + gc * ps)).reshape(128, 512)
        both_h, both_l = halves(jnp.concatenate([pre, pim], axis=0))
        t_ref[half] = mm(row_h, both_h) + (mm(row_l, both_h) + mm(row_h, both_l))
    even = lax.broadcasted_iota(jnp.int32, (8, 128), 0) % 2 == 0
    coming.wait()
    for quarter in range(4):
        for four in range(4):
            for high in range(2):
                parts = []
                for low in range(8):
                    ky = 8 * high + low
                    part = t_ref[four, 8 * ky : 8 * ky + 8, 128 * quarter : 128 * quarter + 128]
                    other = jnp.where(even, pltpu.roll(part, 7, 0), -pltpu.roll(part, 1, 0))
                    spot = ky * facet % 16
                    parts.append(part * turn_ref[0, spot] + other * turn_ref[1, spot])
                for b, done in enumerate(swap_chunks(parts, 16)):
                    u_ref[32 * b + 8 * four : 32 * b + 8 * four + 8, 128 * high : 128 * high + 128] = done
        uh, ul = halves(u_ref[...])
        rows = slice(256 * quarter, 256 * quarter + 256)
        sums = []
        for part in range(2):
            weights = weight_ref[rows, 256 * part : 256 * part + 256]
            sums.append(mm_t(uh, weights) + mm_t(ul, weights))
        lane = lax.broadcasted_iota(jnp.int32, (32, 256), 1)
        row = lax.broadcasted_iota(jnp.int32, (32, 256), 0)
        first = jnp.zeros((32, 256), f32)
        second = jnp.zeros((32, 256), f32)
        for b in range(8):
            mine = lane // 32 == b
            first = jnp.where(mine, sums[0][32 * b : 32 * b + 32, :], first)
            second = jnp.where(mine, sums[1][32 * b : 32 * b + 32, :], second)
        other = jnp.where(row % 2 == 0, -pltpu.roll(second, 31, 0), pltpu.roll(second, 1, 0))
        out_ref[:, 256 * quarter : 256 * quarter + 256] = (first + other) * (1.0 / 512.0)


def degrid(sky, weights, tile_ids):
    columns, rows, shift, turn = (jnp.asarray(t) for t in degrid_tables(sky.shape[-1]))
    smem = pl.BlockSpec(memory_space=pltpu.SMEM)
    vmem = pl.BlockSpec(memory_space=pltpu.VMEM)
    return pl.pallas_call(
        degrid_kernel,
        in_specs=[smem, smem] + [vmem] * 4 + [pl.BlockSpec(memory_space=pl.ANY)],
        out_specs=vmem,
        out_shape=jax.ShapeDtypeStruct((32, 1024), f32),
        scratch_shapes=[
            pltpu.VMEM((512, 512), bf16),
            pltpu.VMEM((512, 512), bf16),
            pltpu.VMEM((4, 512, 512), bf16),
            pltpu.VMEM((4, 128, 512), f32),
            pltpu.VMEM((256, 256), f32),
            pltpu.VMEM((1024, 512), bf16),
            pltpu.SemaphoreType.DMA((1,)),
        ],
        compiler_params=params(60),
        cost_estimate=cost(3e9, 6 * MIB),
        name="degrid",
    )(tile_ids, turn, sky, shift, columns, rows, weights)


def split_kernel(values_ref, sent_ref, kept_ref):
    core = lax.axis_index("facet") % 2
    sent_ref[...] = values_ref[pl.ds(pl.multiple_of(16 * (1 - core), 16), 16), :]
    kept_ref[...] = values_ref[pl.ds(pl.multiple_of(16 * core, 16), 16), :]


def split(values):
    return pl.pallas_call(
        split_kernel,
        out_shape=(jax.ShapeDtypeStruct((16, 1024), f32),) * 2,
        compiler_params=params(16),
        cost_estimate=cost(1e6, 16 * MIB),
        name="split",
    )(values)


def data_step(data_dual, forward, visibilities, radius_scale):
    moved = data_dual + forward
    residual = 2.0 * moved - visibilities
    distance = jnp.sqrt(jnp.sum(residual * residual, axis=(1, 2)) + 1e-06)
    radius = radius_scale * math.sqrt(2.0 * visibilities.shape[2])
    shrunk = jnp.minimum(1.0, radius / distance)
    return moved - 0.5 * (visibilities + residual * shrunk[:, None, None])


def trade(values, axis):
    return lax.all_to_all(values, axis, 0, 0, tiled=True)


def facet_pairs(bit):
    return [(i, i ^ (1 << bit)) for i in range(lax.axis_size("facet"))]


def halving_sum(values, bits):
    me = lax.axis_index("facet")
    for bit in bits:
        values = values.reshape(2, values.shape[0] // 2, values.shape[1])
        mine = (me >> bit) & 1
        sent = lax.dynamic_index_in_dim(values, 1 - mine, 0, keepdims=False)
        kept = lax.dynamic_index_in_dim(values, mine, 0, keepdims=False)
        values = kept + lax.ppermute(sent, "facet", facet_pairs(bit))
    return values


def per_device(
    sky_image,
    margins,
    wavelet_dual,
    sparsity_weights,
    lowrank_dual,
    kernel_weights,
    tile_index,
    data_dual,
    visibilities,
    radius_scale,
):
    facet_rows, image_side = sky_image.shape[1:]
    channels = lowrank_dual.shape[0]
    devices = lax.axis_size("facet")

    packed, rim = pack_sky(sky_image)
    packed, sky = lax.optimization_barrier((packed, sky_image))
    got = trade(packed, "chan").reshape(2048, 128)
    rim = lax.ppermute(rim, "facet", [(i, i + 1) for i in range(devices - 1)])
    blended, energy = blend_inner(sky, wavelet_dual)
    blended, kept, sent = blend_outer(margins, sky, rim, wavelet_dual, energy, blended)
    other = lax.ppermute(sent, "chan", [(i, i ^ 1) for i in range(lax.axis_size("chan"))])
    sky, kept = lax.optimization_barrier((sky, kept))
    forward_part = degrid(sky, kernel_weights.reshape(1024, 512), tile_index)
    sent, mine = split(forward_part)
    forward = mine + lax.ppermute(sent, "facet", facet_pairs(0))
    kept, forward = lax.optimization_barrier((kept, forward))

    dual = jnp.transpose(lowrank_dual, (1, 2, 0)).reshape(4, 8, 32, 256)
    y, part = gram_part(got, dual, kept, other)
    part, forward = lax.optimization_barrier((part, forward))
    forward = halving_sum(forward, (3,))
    reduced, forward = lax.optimization_barrier((trade(part, "chan"), forward))
    forward = halving_sum(forward, (1, 2))[None]
    data_next = data_step(data_dual, forward, visibilities, radius_scale)
    total = trade(sum_copies(reduced), "chan")
    wavelet_next, mixed = finish(
        total, sparsity_weights, blended, y.reshape(2 * ROOM, 1024, 256), facet_rows * image_side, channels
    )
    lowrank_next = jnp.transpose(mixed.reshape(32, 32, 256), (2, 0, 1))
    return (wavelet_next, lowrank_next, data_next)


def solution(mesh):
    in_specs = (
        P("chan", "facet", None),
        P(),
        P(None, "chan", "facet", None),
        P(None, "facet", None),
        P(None, "facet", "chan"),
        P("chan", None, None, None),
        P("chan", None),
        P(("chan", "facet"), None, None),
        P(("chan", "facet"), None, None),
        P(("chan", "facet")),
    )
    out_specs = (
        P(None, "chan", "facet", None),
        P(None, "facet", "chan"),
        P(("chan", "facet"), None, None),
    )
    return jax.shard_map(
        per_device, mesh=mesh, in_specs=in_specs, out_specs=out_specs, check_vma=False
    )
```

time: 102 us -> 97.2 us (0.953)
  waiting for transfers between devices: 34.9 us -> 32.1 us
    all_to_all x3, waiting for transfers between devices: 27.1 us -> 16.5 us  [trade(): return lax.all_to_all(values, axis, 0, 0, tiled=True)]
    ppermute x5 -> x6, waiting for transfers between devices: 7.8 us -> 15.5 us  [the longest x3 11.2 us: halving_sum(): values = kept + lax.ppermute(sent, 'facet', facet_pairs(bit))]
    ppermute x5 -> x6, starting transfers between devices: 9.77 us -> 7.31 us  [the longest x1 3.69 us: per_device(): lax.ppermute(sent, 'chan', [(i, i ^ 1) for i in range(lax.axis_size('chan...]
    pallas_call x1, Pallas kernels: 7.94 us -> 5.76 us  [finish(): pl.pallas_call(lambda *refs: finish_kernel(pixels, channels, *refs), in_s...]
    all_to_all x3, starting transfers between devices: 18.8 us -> 20.4 us  [trade(): return lax.all_to_all(values, axis, 0, 0, tiled=True)]
    pallas_call x4 -> x6, Pallas kernels: 15.1 us -> 16.3 us  [the longest x1 5.33 us: blend_outer(): pl.pallas_call(outer_kernel, in_specs=[pl.BlockSpec(memory_space=pltpu.SM...]
    pallas_call x1, Pallas kernels: 7.64 us -> 8.74 us  [degrid(): pl.pallas_call(degrid_kernel, in_specs=[smem, smem] + [vmem] * 4 + [pl.Bl...]
    unnamed x20 -> x14, local copies, waits for them, and re-layouts: 1.53 us -> 2.52 us
  transfers between devices with their start and end apart: 8 -> 9, of which waited for: 7 -> 7; matrix products, arithmetic and copies ran while one was open for 3% -> 1% of each run, Pallas kernels for 15% -> 20%
where the time goes in v3:
time: 97.2 us; the launch traced here: 96.7 us
  waiting for transfers between devices  32.1 us (33%)
  Pallas kernels  30.8 us (32%)
  starting transfers between devices  27.7 us (28%)
  local copies, waits for them, and re-layouts  2.59 us (3%)
  between operations  2.36 us (2%)
  other arithmetic  1.25 us (1%)
    all_to_all x3, starting transfers between devices, trade(): return lax.all_to_all(values, axis, 0, 0, tiled=True)  20.4 us
    all_to_all x3, waiting for transfers between devices, trade(): return lax.all_to_all(values, axis, 0, 0, tiled=True)  16.5 us
    ppermute x3, waiting for transfers between devices, halving_sum(): values = kept + lax.ppermute(sent, 'facet', facet_pairs(bit))  11.2 us
    pallas_call x1, Pallas kernels, degrid(): pl.pallas_call(degrid_kernel, in_specs=[smem, smem] + [vmem] * 4 + [pl.Bl...  8.74 us
    pallas_call x1, Pallas kernels, finish(): pl.pallas_call(lambda *refs: finish_kernel(pixels, channels, *refs), in_s...  5.76 us
    pallas_call x1, Pallas kernels, blend_outer(): pl.pallas_call(outer_kernel, in_specs=[pl.BlockSpec(memory_space=pltpu.SM...  5.33 us
    pallas_call x1, Pallas kernels, blend_inner(): pl.pallas_call(inner_kernel, in_specs=[hbm] * 4, out_specs=(hbm, hbm), ou...  5.31 us
    ppermute x1, starting transfers between devices, per_device(): lax.ppermute(sent, 'chan', [(i, i ^ 1) for i in range(lax.axis_size('chan...  3.69 us
  transfers between devices with their start and end apart: 9, of which 7 were waited for; matrix products, arithmetic and copies ran while one was open for 1% of the time, Pallas kernels for 20%

profile of v3, /device:TPU:8, one launch (start us, length us, event | category | flops | bytes accessed | tf_op | source)
XLA Modules:
  0.0 96.7 jit_solution(14781932415712583108)
XLA Ops:
  0.6 2.9 %pack_sky.1 = (f32[16,16,8,128]{3,2,1,0:T(8,128)}, f32[16,8,512]{2,1,0:T(8,128)}) custom-call(f32[16,32,512]{2,1,0:T(8,128)} %sky_ref), custom_call_target="tpu_custom_call" | custom-call | flops 3000000 | bytes 2097152 | tf_op jit(solution)/shard_map/pack_sky/pallas_call | solution.py:112
  3.6 10.3 %all-to-all-start = ((f32[16,16,8,128]{3,2,1,0:T(8,128)}), f32[16,16,8,128]{3,2,1,0:T(8,128)S(1)}, u32[]{:S(2)}, u32[]{:S(2)}) async-start(f32[16,16,8,128]{3,2,1,0:T(8,128)} %get-tuple-element.27), calls=%async_computation | async-start | bytes 2097152 | tf_op jit(solution)/shard_map/all_to_all | solution.py:706
  13.9 0.0 copy-start
  13.9 2.1 %collective-permute-start = (f32[16,8,512]{2,1,0:T(8,128)}, f32[16,8,512]{2,1,0:T(8,128)S(1)}, u32[]{:S(2)}, u32[]{:S(2)}) collective-permute-start(f32[16,8,512]{2,1,0:T(8,128)} %get-tuple-element.29), channel_id=1, source_target_pairs={{0,16},{16,32},{32,48},{48,64},{64,80},{80,96},{96,112},{112,128},... | collective-permute-start | bytes 786440 | tf_op jit(solution)/shard_map/ppermute | solution.py:743
  16.0 5.3 %blend_inner.1 = (f32[24,16,32,512]{3,2,1,0:T(8,128)}, f32[2,16,16,128]{3,2,1,0:T(8,128)}) custom-call(f32[16,32,512]{2,1,0:T(8,128)} %sky_ref, f32[4,16,32,512]{3,2,1,0:T(8,128)} %dual_in.3, bf16[2,192,128]{2,1,0:T(8,128)(2,1)} %constant.60.clone.down_in, bf16[512,256]{1,0:T(8,128)(2,1)} %constant.61.clone.across_in), custom_call_target="tpu_custom_call" | custom-call | flops 2000000000 | bytes 8388608 | tf_op jit(solution)/shard_map/blend_inner/pallas_call | solution.py:485
  21.3 0.0 copy-start.5
  21.3 0.0 copy-start.6
  21.3 0.0 copy-start.1
  21.3 3.1 %collective-permute-done.rim_in = f32[16,8,512]{2,1,0:T(8,128)S(1)} collective-permute-done((f32[16,8,512]{2,1,0:T(8,128)}, f32[16,8,512]{2,1,0:T(8,128)S(1)}, u32[]{:S(2)}, u32[]{:S(2)}) %collective-permute-start) | collective-permute-done | bytes 262176 | tf_op jit(solution)/shard_map/ppermute | solution.py:743
  24.4 0.0 copy-start.4
  24.4 0.7 copy-done.4
  25.1 5.3 %blend_outer.1 = (f32[24,16,32,512]{3,2,1,0:T(8,128)}, f32[16,16,128]{2,1,0:T(8,128)}, f32[16,16,128]{2,1,0:T(8,128)}) custom-call(s32[16]{0:T(128)} %margins_ref.1, f32[16,32,512]{2,1,0:T(8,128)} %sky_ref, f32[16,8,512]{2,1,0:T(8,128)} %copy-done.4, f32[4,16,32,512]{3,2,1,0:T(8,128)} %dual_in.3, ...), custom_call_target="tpu_custom_call", output_to_operand_aliasing={{0}: (7, {})} | custom-call | flops 1000000000 | bytes 4194304 | tf_op jit(solution)/shard_map/blend_outer/pallas_call | solution.py:512
  30.5 3.7 %collective-permute-start.2 = (f32[16,16,128]{2,1,0:T(8,128)}, f32[16,16,128]{2,1,0:T(8,128)S(1)}, u32[]{:S(2)}, u32[]{:S(2)}) collective-permute-start(f32[16,16,128]{2,1,0:T(8,128)} %get-tuple-element.38), channel_id=1, source_target_pairs={{0,1},{1,0},{2,3},{3,2},{4,5},{5,4},{6,7},{7,6},{8,9},{9,8},{10,11... | collective-permute-start | bytes 393224 | tf_op jit(solution)/shard_map/ppermute | solution.py:746
  34.2 8.7 %degrid.1.values_ref = f32[32,1024]{1,0:T(8,128)} custom-call(s32[1,32]{1,0:T(1,128)} %tile_ref.1, f32[2,16]{1,0:T(2,128)} %constant.66.clone.turn_ref, f32[16,32,512]{2,1,0:T(8,128)} %sky_ref, bf16[128,32]{1,0:T(8,128)(2,1)} %constant.65.clone.shift_ref, f32[96,512]{1,0:T(8,128)} %constant.63.clone.column_ref, bf16[256,256]{1,0:T(8,128)(2,1)} %constant.64.clone.row_ref, ...), custom_call_target="tpu_custom_call" | custom-call | flops 3000000000 | bytes 6291456 | tf_op jit(solution)/shard_map/degrid/pallas_call | solution.py:660
  42.9 0.0 copy-start.3
  42.9 0.9 copy-done.3
  43.8 0.1 collective-permute-start.1
  43.9 1.2 %collective-permute-done.1 = f32[16,1024]{1,0:T(8,128)S(1)} collective-permute-done((f32[16,1024]{1,0:T(8,128)S(1)}, f32[16,1024]{1,0:T(8,128)S(1)}, u32[]{:S(2)}, u32[]{:S(2)}) %collective-permute-start.1) | collective-permute-done | bytes 65568 | tf_op jit(solution)/shard_map/ppermute | solution.py:750
  45.2 0.0 collective-permute-done.2.other_ref
  45.2 0.0 all-to-all-done
  45.2 0.0 copy-done
  45.2 0.0 copy-start.2
  45.2 0.9 copy-done.2
  46.1 1.9 %gram_part.1 = (bf16[48,4,8,32,256]{4,3,2,1,0:T(8,128)(2,1)}, f32[16,40,128]{2,1,0:T(8,128)}) custom-call(f32[2048,128]{1,0:T(8,128)S(1)} %bitcast.30, f32[4,8,32,256]{3,2,1,0:T(8,128)S(1)} %bitcast.31, f32[16,16,128]{2,1,0:T(8,128)S(1)} %copy-done.2, f32[16,16,128]{2,1,0:T(8,128)S(1)} %collective-permute-done.2.other_ref), custom_call_target="tpu_custom_call" | custom-call | flops 400000000 | bytes 3145728 | tf_op jit(solution)/shard_map/gram_part/pallas_call | solution.py:175
  48.0 6.5 %all-to-all-start.1 = ((f32[16,40,128]{2,1,0:T(8,128)}), f32[16,40,128]{2,1,0:T(8,128)S(1)}, u32[]{:S(2)}, u32[]{:S(2)}) async-start(f32[16,40,128]{2,1,0:T(8,128)} %get-tuple-element.41), calls=%async_computation.1 | async-start | bytes 655360 | tf_op jit(solution)/shard_map/all_to_all | solution.py:706
  54.5 0.3 collective-permute-start.3
  54.8 4.0 %collective-permute-done.3 = f32[8,1024]{1,0:T(8,128)S(1)} collective-permute-done((f32[8,1024]{1,0:T(8,128)S(1)}, f32[8,1024]{1,0:T(8,128)S(1)}, u32[]{:S(2)}, u32[]{:S(2)}) %collective-permute-start.3) | collective-permute-done | bytes 32800 | tf_op jit(solution)/shard_map/ppermute | solution.py:720
  58.8 10.8 %all-to-all-done.1.got_ref = f32[16,40,128]{2,1,0:T(8,128)S(1)} async-done(((f32[16,40,128]{2,1,0:T(8,128)}), f32[16,40,128]{2,1,0:T(8,128)S(1)}, u32[]{:S(2)}, u32[]{:S(2)}) %all-to-all-start.1) | async-done | bytes 327712 | tf_op jit(solution)/shard_map/all_to_all | solution.py:706
  69.5 0.8 sum_copies.1
  70.3 3.6 %all-to-all-start.2 = ((f32[16,56,128]{2,1,0:T(8,128)}), f32[16,56,128]{2,1,0:T(8,128)S(1)}, u32[]{:S(2)}, u32[]{:S(2)}) async-start(f32[16,56,128]{2,1,0:T(8,128)} %sum_copies.1), calls=%async_computation.2 | async-start | bytes 917504 | tf_op jit(solution)/shard_map/all_to_all | solution.py:706
  73.9 0.1 collective-permute-start.4
  74.0 3.7 %collective-permute-done.4 = f32[4,1024]{1,0:T(4,128)S(1)} collective-permute-done((f32[4,1024]{1,0:T(4,128)S(1)}, f32[4,1024]{1,0:T(4,128)S(1)}, u32[]{:S(2)}, u32[]{:S(2)}) %collective-permute-start.4) | collective-permute-done | bytes 16416 | tf_op jit(solution)/shard_map/ppermute | solution.py:720
  77.8 1.1 %collective-permute-start.5 = (f32[2,1024]{1,0:T(2,128)S(1)}, f32[2,1024]{1,0:T(2,128)S(1)}, u32[]{:S(2)}, u32[]{:S(2)}) collective-permute-start(f32[2,1024]{1,0:T(2,128)S(1)} %dynamic-slice_bitcast_fusion.2), channel_id=1, source_target_pairs={{0,64},{16,80},{32,96},{48,112},{64,0},{80,16},{96,32},{112,48},{1... | collective-permute-start | bytes 24584 | tf_op jit(solution)/shard_map/ppermute | solution.py:720
  79.6 3.5 %collective-permute-done.5 = f32[2,1024]{1,0:T(2,128)S(1)} collective-permute-done((f32[2,1024]{1,0:T(2,128)S(1)}, f32[2,1024]{1,0:T(2,128)S(1)}, u32[]{:S(2)}, u32[]{:S(2)}) %collective-permute-start.5) | collective-permute-done | bytes 8224 | tf_op jit(solution)/shard_map/ppermute | solution.py:720
  83.1 0.0 copy-done.5
  83.1 0.0 copy-done.6
  83.1 0.6 multiply_reduce_fusion
  84.4 0.6 multiply_subtract_fusion
  85.0 5.8 %all-to-all-done.2.refs_0_ = f32[16,56,128]{2,1,0:T(8,128)S(1)} async-done(((f32[16,56,128]{2,1,0:T(8,128)}), f32[16,56,128]{2,1,0:T(8,128)S(1)}, u32[]{:S(2)}, u32[]{:S(2)}) %all-to-all-start.2) | async-done | bytes 458784 | tf_op jit(solution)/shard_map/all_to_all | solution.py:706
  90.8 0.0 copy-done.1
  90.8 5.8 %finish.1 = (f32[4,16,32,512]{3,2,1,0:T(8,128)}, f32[1024,256]{1,0:T(8,128)}) custom-call(f32[16,56,128]{2,1,0:T(8,128)S(1)} %all-to-all-done.2.refs_0_, f32[4,32,512]{2,1,0:T(8,128)S(1)} %copy-done.1, f32[24,16,32,512]{3,2,1,0:T(8,128)} %get-tuple-element.44.refs_2_, bf16[48,1024,256]{2,1,0:T(8,128)(2,1)} %bitcast.32), custom_call_target="tpu_custom_call" | custom-call | flops 2000000000 | bytes 8388608 | tf_op jit(solution)/shard_map/finish/pallas_call | solution.py:314
  (9 shorter events, 0.1 us)
Async XLA Ops:
  3.6 41.6 %all-to-all-start = ((f32[16,16,8,128]{3,2,1,0:T(8,128)}), f32[16,16,8,128]{3,2,1,0:T(8,128)S(1)}, u32[]{:S(2)}, u32[]{:S(2)}) async-start(f32[16,16,8,128]{3,2,1,0:T(8,128)} %get-tuple-element.27), calls=%async_computation | async-start | bytes 2097152 | tf_op jit(solution)/shard_map/all_to_all | solution.py:706
  13.9 31.3 %copy-start = (f32[256,32,32]{0,2,1:T(8,128)S(1)}, f32[256,32,32]{0,2,1:T(8,128)}, u32[]{:S(2)}) copy-start(f32[256,32,32]{0,2,1:T(8,128)} %param.22) | copy-start | bytes 3145732
  13.9 10.5 %collective-permute-start = (f32[16,8,512]{2,1,0:T(8,128)}, f32[16,8,512]{2,1,0:T(8,128)S(1)}, u32[]{:S(2)}, u32[]{:S(2)}) collective-permute-start(f32[16,8,512]{2,1,0:T(8,128)} %get-tuple-element.29), channel_id=1, source_target_pairs={{0,16},{16,32},{32,48},{48,64},{64,80},{80,96},{96,112},{112,128},... | collective-permute-start | bytes 786440 | tf_op jit(solution)/shard_map/ppermute | solution.py:743
  21.3 61.8 %copy-start.5 = (f32[1,2,1024]{2,1,0:T(2,128)S(1)}, f32[1,2,1024]{2,1,0:T(2,128)}, u32[]{:S(2)}) copy-start(f32[1,2,1024]{2,1,0:T(2,128)} %param.26) | copy-start | bytes 24580
  21.3 61.8 %copy-start.6 = (f32[1,2,1024]{2,1,0:T(2,128)S(1)}, f32[1,2,1024]{2,1,0:T(2,128)}, u32[]{:S(2)}) copy-start(f32[1,2,1024]{2,1,0:T(2,128)} %param.25) | copy-start | bytes 24580
  21.3 69.5 %copy-start.1 = (f32[4,32,512]{2,1,0:T(8,128)S(1)}, f32[4,32,512]{2,1,0:T(8,128)}, u32[]{:S(2)}) copy-start(f32[4,32,512]{2,1,0:T(8,128)} %refs_1_.1) | copy-start | bytes 786436
  24.4 0.7 copy-start.4
  30.5 14.7 %collective-permute-start.2 = (f32[16,16,128]{2,1,0:T(8,128)}, f32[16,16,128]{2,1,0:T(8,128)S(1)}, u32[]{:S(2)}, u32[]{:S(2)}) collective-permute-start(f32[16,16,128]{2,1,0:T(8,128)} %get-tuple-element.38), channel_id=1, source_target_pairs={{0,1},{1,0},{2,3},{3,2},{4,5},{5,4},{6,7},{7,6},{8,9},{9,8},{10,11... | collective-permute-start | bytes 393224 | tf_op jit(solution)/shard_map/ppermute | solution.py:746
  42.9 0.9 copy-start.3
  43.8 1.3 %collective-permute-start.1 = (f32[16,1024]{1,0:T(8,128)S(1)}, f32[16,1024]{1,0:T(8,128)S(1)}, u32[]{:S(2)}, u32[]{:S(2)}) collective-permute-start(f32[16,1024]{1,0:T(8,128)S(1)} %get-tuple-element.36), channel_id=1, source_target_pairs={{0,16},{16,0},{32,48},{48,32},{64,80},{80,64},{96,112},{112,96},{1... | collective-permute-start | bytes 196616 | tf_op jit(solution)/shard_map/ppermute | solution.py:750
  45.2 0.9 copy-start.2
  48.0 21.5 %all-to-all-start.1 = ((f32[16,40,128]{2,1,0:T(8,128)}), f32[16,40,128]{2,1,0:T(8,128)S(1)}, u32[]{:S(2)}, u32[]{:S(2)}) async-start(f32[16,40,128]{2,1,0:T(8,128)} %get-tuple-element.41), calls=%async_computation.1 | async-start | bytes 655360 | tf_op jit(solution)/shard_map/all_to_all | solution.py:706
  54.5 4.2 %collective-permute-start.3 = (f32[8,1024]{1,0:T(8,128)S(1)}, f32[8,1024]{1,0:T(8,128)S(1)}, u32[]{:S(2)}, u32[]{:S(2)}) collective-permute-start(f32[8,1024]{1,0:T(8,128)S(1)} %dynamic-slice_bitcast_fusion), channel_id=1, source_target_pairs={{0,128},{16,144},{32,160},{48,176},{64,192},{80,208},{96,224},{112... | collective-permute-start | bytes 98312 | tf_op jit(solution)/shard_map/ppermute | solution.py:720
  70.3 20.4 %all-to-all-start.2 = ((f32[16,56,128]{2,1,0:T(8,128)}), f32[16,56,128]{2,1,0:T(8,128)S(1)}, u32[]{:S(2)}, u32[]{:S(2)}) async-start(f32[16,56,128]{2,1,0:T(8,128)} %sum_copies.1), calls=%async_computation.2 | async-start | bytes 917504 | tf_op jit(solution)/shard_map/all_to_all | solution.py:706
  73.9 3.9 %collective-permute-start.4 = (f32[4,1024]{1,0:T(4,128)S(1)}, f32[4,1024]{1,0:T(4,128)S(1)}, u32[]{:S(2)}, u32[]{:S(2)}) collective-permute-start(f32[4,1024]{1,0:T(4,128)S(1)} %dynamic-slice_bitcast_fusion.1), channel_id=1, source_target_pairs={{0,32},{16,48},{32,0},{48,16},{64,96},{80,112},{96,64},{112,80},{1... | collective-permute-start | bytes 49160 | tf_op jit(solution)/shard_map/ppermute | solution.py:720
  77.8 5.2 %collective-permute-start.5 = (f32[2,1024]{1,0:T(2,128)S(1)}, f32[2,1024]{1,0:T(2,128)S(1)}, u32[]{:S(2)}, u32[]{:S(2)}) collective-permute-start(f32[2,1024]{1,0:T(2,128)S(1)} %dynamic-slice_bitcast_fusion.2), channel_id=1, source_target_pairs={{0,64},{16,80},{32,96},{48,112},{64,0},{80,16},{96,32},{112,48},{1... | collective-permute-start | bytes 24584 | tf_op jit(solution)/shard_map/ppermute | solution.py:720

commit v4 on v3

--- a/solution.py
+++ b/solution.py
@@ -129,15 +129,21 @@
     )(sky)
 
 
+def turn_rows(block, back):
+    row = lax.broadcasted_iota(jnp.int32, block.shape, 0)
+    for bit in (1, 2, 4, 8):
+        turned = pltpu.roll(block, bit if back else 256 - bit, 1)
+        block = jnp.where((row // bit) % 2 == 1, turned, block)
+    return block
+
+
 def gram_kernel(
-    got_ref, dual_ref, kept_ref, other_ref, y_out, part_out, y_ref, sum_ref, gram_ref, sems
+    got_ref, dual_ref, blend_in, other_ref, y_out, part_out, y_ref, kept_ref, sum_ref, gram_ref, sems
 ):
-    sum_ref[...] = kept_ref[...] + other_ref[...]
-    copies = [pltpu.make_async_copy(sum_ref, part_out.at[:, :16], sems.at[8])]
-    copies[0].start()
+    kept = copy_in(blend_in.at[4, :, :16, :128], kept_ref, sems.at[10])
     total = jnp.zeros((256, 256), f32)
     cross = jnp.zeros((256, 256), f32)
-    held = []
+    held, copies = [], []
     for low in range(8):
         seen = got_ref[pl.ds(low, 256, stride=8), :].T
         right = dual_ref[:, low].reshape(128, 256) + 0.5 * seen
@@ -155,26 +161,30 @@
             total = total + mm(lh, rh)
             cross = cross + mm(lh, rl)
     total = total + (cross + cross.T)
-    gram_ref[:, 16:, :] = jnp.zeros((16, 8, 128), f32)
+    kept.wait()
+    sum_ref[...] = kept_ref[...] + other_ref[...]
+    copies.append(copy_in(sum_ref, part_out.at[:, :16], sems.at[8]))
+    row = lax.broadcasted_iota(jnp.int32, (128, 128), 0)
+    lane = lax.broadcasted_iota(jnp.int32, (128, 128), 1)
+    far = jnp.sum(jnp.where(row == lane, total[:128, 128:], 0.0), axis=0, keepdims=True)
+    gram_ref[:, 16:, :] = jnp.broadcast_to(far[None], (16, 8, 128))
     for peer in range(16):
         turned = total[16 * peer : 16 * peer + 16, :]
         if peer:
             turned = pltpu.roll(turned, 256 - 16 * peer, 1)
-        gram_ref[peer, :16, :] = turned[:, :128]
-        gram_ref[peer, 16:, :16] = turned[:8, 128:144]
-        gram_ref[peer, 16:, 16:32] = turned[8:, 128:144]
+        gram_ref[peer, :16, :] = turn_rows(turned, False)[:, :128]
     copies.append(pltpu.make_async_copy(gram_ref, part_out.at[:, 16:], sems.at[9]))
     copies[-1].start()
     for copy in copies:
         copy.wait()
 
 
-def gram_part(got, dual, kept, other):
+def gram_part(got, dual, blended, other):
     vmem = pl.BlockSpec(memory_space=pltpu.VMEM)
     hbm = pl.BlockSpec(memory_space=pl.ANY)
     return pl.pallas_call(
         gram_kernel,
-        in_specs=[vmem] * 4,
+        in_specs=[vmem, vmem, hbm, vmem],
         out_specs=(hbm, hbm),
         out_shape=(
             jax.ShapeDtypeStruct((2 * ROOM, 4, 8, 32, 256), bf16),
@@ -183,32 +193,37 @@
         scratch_shapes=[
             pltpu.VMEM((2, 4, 8, 32, 256), bf16),
             pltpu.VMEM((16, 16, 128), f32),
+            pltpu.VMEM((16, 16, 128), f32),
             pltpu.VMEM((16, 24, 128), f32),
-            pltpu.SemaphoreType.DMA((10,)),
+            pltpu.SemaphoreType.DMA((11,)),
         ],
         compiler_params=params(40),
         cost_estimate=cost(4e8, 3 * MIB),
         name="gram_part",
-    )(got, dual, kept, other)
-
-
-def sum_kernel(got_ref, out_ref):
+    )(got, dual, blended, other)
+
+
+def sum_kernel(got_ref, out_ref, far_ref):
     halves_of = [got_ref[0, :16], got_ref[1, :16]]
     gram = got_ref[0, 16:]
     for peer in range(1, 16):
         gram = gram + got_ref[peer, 16:]
         if peer > 1:
             halves_of[peer % 2] = halves_of[peer % 2] + got_ref[peer, :16]
+    far_ref[...] = gram[16:]
     for peer in range(16):
         out_ref[peer, :16] = halves_of[0]
         out_ref[peer, 16:32] = halves_of[1]
-        out_ref[peer, 32:] = gram
+        out_ref[peer, 32:] = gram[:16]
 
 
 def sum_copies(got):
     return pl.pallas_call(
         sum_kernel,
-        out_shape=jax.ShapeDtypeStruct((16, 56, 128), f32),
+        out_shape=(
+            jax.ShapeDtypeStruct((16, 48, 128), f32),
+            jax.ShapeDtypeStruct((8, 128), f32),
+        ),
         compiler_params=params(16),
         cost_estimate=cost(1e6, MIB),
         name="sum_copies",
@@ -219,6 +234,7 @@
     pixels,
     channels,
     got_ref,
+    far_ref,
     weight_in,
     blend_in,
     y_in,
@@ -264,15 +280,15 @@
     rows = lax.broadcasted_iota(jnp.int32, (size, size), 0)
     cols = lax.broadcasted_iota(jnp.int32, (size, size), 1)
     blocks = []
+    nothing = jnp.zeros((16, 128), f32)
     for peer in range(16):
-        ninth = jnp.concatenate([got_ref[peer, 48:, :], jnp.zeros((8, 128), f32)], axis=0)
-        second = jnp.concatenate([jnp.zeros((8, 128), f32), pltpu.roll(got_ref[peer, 48:, :], 112, 1)], axis=0)
-        ninth = ninth + second
-        block = jnp.concatenate([got_ref[peer, 32:48, :], ninth], axis=1)
+        block = turn_rows(jnp.concatenate([got_ref[peer, 32:48, :], nothing], axis=1), True)
         blocks.append(pltpu.roll(block, 16 * peer, 1) if peer else block)
     half = jnp.concatenate(blocks, axis=0)
-    known = (cols // 16 - rows // 16) % 16 < 9
-    gram = jnp.where(known, half, half.T)
+    far = far_ref[:1, :]
+    apart = (cols - rows) % 256
+    gram = jnp.where(apart < 128, half, half.T)
+    gram = jnp.where(apart == 128, jnp.concatenate([far, far], axis=1), gram)
     shifted = (rows == cols).astype(f32) + gram * (1.0 / pixels)
     frob = jnp.sqrt(jnp.sum(shifted * shifted, keepdims=True))
 
@@ -308,12 +324,12 @@
         copy.wait()
 
 
-def finish(got, weights, blended, y, pixels, channels):
+def finish(got, far, weights, blended, y, pixels, channels):
     shape = (4, 16, 32, 512)
     hbm = pl.BlockSpec(memory_space=pl.ANY)
     return pl.pallas_call(
         lambda *refs: finish_kernel(pixels, channels, *refs),
-        in_specs=[pl.BlockSpec(memory_space=pltpu.VMEM)] + [hbm] * 3,
+        in_specs=[pl.BlockSpec(memory_space=pltpu.VMEM)] * 2 + [hbm] * 3,
         out_specs=(hbm, hbm),
         out_shape=(
             jax.ShapeDtypeStruct(shape, f32),
@@ -331,7 +347,7 @@
         compiler_params=params(40),
         cost_estimate=cost(2e9, 8 * MIB),
         name="finish",
-    )(got, weights, blended, y)
+    )(got, far, weights, blended, y)
 
 
 def filter_tables(first, last):
@@ -434,7 +450,6 @@
     energy_in,
     blend_in,
     blend_out,
-    kept_out,
     sent_out,
     sky_ref,
     rim_ref,
@@ -473,8 +488,8 @@
             pieces += [jnp.where(kept, rim_ref[c], 0.0), sky_ref[c]]
         blend_group(pieces, four, 0, down_ref, across_ref, dual_ref, blend_ref, energy_ref)
         going.append(copy_in(blend_ref.at[:, four], blend_out.at[:4, four, :8], out_sems.at[k]))
-    for number, (which, target) in enumerate(((1 - half, sent_out), (half, kept_out))):
-        going.append(copy_in(energy_ref.at[which], target, out_sems.at[4 + number]))
+    going.append(copy_in(energy_ref.at[1 - half], sent_out, out_sems.at[4]))
+    going.append(copy_in(energy_ref.at[half], blend_out.at[4, :, :16, :128], out_sems.at[5]))
     for copy in going:
         copy.wait()
 
@@ -512,10 +527,9 @@
     return pl.pallas_call(
         outer_kernel,
         in_specs=[pl.BlockSpec(memory_space=pltpu.SMEM)] + [hbm] * 7,
-        out_specs=(hbm, hbm, hbm),
+        out_specs=(hbm, hbm),
         out_shape=(
             jax.ShapeDtypeStruct(blended.shape, f32),
-            jax.ShapeDtypeStruct((16, 16, 128), f32),
             jax.ShapeDtypeStruct((16, 16, 128), f32),
         ),
         input_output_aliases={7: 0},
@@ -572,6 +586,8 @@
     column_ref,
     row_ref,
     weight_in,
+    sent_out,
+    mine_out,
     out_ref,
     xh_ref,
     xl_ref,
@@ -581,8 +597,7 @@
     weight_ref,
     sem,
 ):
-    coming = pltpu.make_async_copy(weight_in, weight_ref, sem.at[0])
-    coming.start()
+    coming = copy_in(weight_in, weight_ref, sem.at[0])
     facet = lax.axis_index("facet")
     inner_cos, inner_sin = column_ref[:KT, :], column_ref[KT : 2 * KT, :]
     block = lax.broadcasted_iota(jnp.int32, (8, 512), 1) // KT
@@ -651,25 +666,34 @@
             second = jnp.where(mine, sums[1][32 * b : 32 * b + 32, :], second)
         other = jnp.where(row % 2 == 0, -pltpu.roll(second, 31, 0), pltpu.roll(second, 1, 0))
         out_ref[:, 256 * quarter : 256 * quarter + 256] = (first + other) * (1.0 / 512.0)
+    core = facet % 2
+    going = [
+        copy_in(out_ref.at[pl.ds(pl.multiple_of(16 * which, 16), 16)], target, sem.at[k])
+        for k, (which, target) in enumerate(((1 - core, sent_out), (core, mine_out)))
+    ]
+    for copy in going:
+        copy.wait()
 
 
 def degrid(sky, weights, tile_ids):
     columns, rows, shift, turn = (jnp.asarray(t) for t in degrid_tables(sky.shape[-1]))
     smem = pl.BlockSpec(memory_space=pltpu.SMEM)
     vmem = pl.BlockSpec(memory_space=pltpu.VMEM)
+    hbm = pl.BlockSpec(memory_space=pl.ANY)
     return pl.pallas_call(
         degrid_kernel,
-        in_specs=[smem, smem] + [vmem] * 4 + [pl.BlockSpec(memory_space=pl.ANY)],
-        out_specs=vmem,
-        out_shape=jax.ShapeDtypeStruct((32, 1024), f32),
+        in_specs=[smem, smem] + [vmem] * 4 + [hbm],
+        out_specs=(hbm, hbm),
+        out_shape=(jax.ShapeDtypeStruct((16, 1024), f32),) * 2,
         scratch_shapes=[
+            pltpu.VMEM((32, 1024), f32),
             pltpu.VMEM((512, 512), bf16),
             pltpu.VMEM((512, 512), bf16),
             pltpu.VMEM((4, 512, 512), bf16),
             pltpu.VMEM((4, 128, 512), f32),
             pltpu.VMEM((256, 256), f32),
             pltpu.VMEM((1024, 512), bf16),
-            pltpu.SemaphoreType.DMA((1,)),
+            pltpu.SemaphoreType.DMA((2,)),
         ],
         compiler_params=params(60),
         cost_estimate=cost(3e9, 6 * MIB),
@@ -677,29 +701,26 @@
     )(tile_ids, turn, sky, shift, columns, rows, weights)
 
 
-def split_kernel(values_ref, sent_ref, kept_ref):
-    core = lax.axis_index("facet") % 2
-    sent_ref[...] = values_ref[pl.ds(pl.multiple_of(16 * (1 - core), 16), 16), :]
-    kept_ref[...] = values_ref[pl.ds(pl.multiple_of(16 * core, 16), 16), :]
-
-
-def split(values):
+def data_kernel(radius_ref, dual_ref, forward_ref, vis_ref, out_ref):
+    vis = vis_ref[0]
+    moved = dual_ref[0] + forward_ref[...]
+    residual = 2.0 * moved - vis
+    distance = jnp.sqrt(jnp.sum(residual * residual, keepdims=True) + 1e-06)
+    radius = radius_ref[0] * math.sqrt(2.0 * vis.shape[1])
+    out_ref[0] = moved - 0.5 * (vis + residual * jnp.minimum(1.0, radius / distance))
+
+
+def data_step(data_dual, forward, visibilities, radius_scale):
+    vmem = pl.BlockSpec(memory_space=pltpu.VMEM)
     return pl.pallas_call(
-        split_kernel,
-        out_shape=(jax.ShapeDtypeStruct((16, 1024), f32),) * 2,
+        data_kernel,
+        in_specs=[pl.BlockSpec(memory_space=pltpu.SMEM)] + [vmem] * 3,
+        out_specs=vmem,
+        out_shape=jax.ShapeDtypeStruct(data_dual.shape, f32),
         compiler_params=params(16),
-        cost_estimate=cost(1e6, 16 * MIB),
-        name="split",
-    )(values)
-
-
-def data_step(data_dual, forward, visibilities, radius_scale):
-    moved = data_dual + forward
-    residual = 2.0 * moved - visibilities
-    distance = jnp.sqrt(jnp.sum(residual * residual, axis=(1, 2)) + 1e-06)
-    radius = radius_scale * math.sqrt(2.0 * visibilities.shape[2])
-    shrunk = jnp.minimum(1.0, radius / distance)
-    return moved - 0.5 * (visibilities + residual * shrunk[:, None, None])
+        cost_estimate=cost(1e5, 1e5),
+        name="data_step",
+    )(radius_scale, data_dual, forward, visibilities)
 
 
 def trade(values, axis):
@@ -742,24 +763,24 @@
     got = trade(packed, "chan").reshape(2048, 128)
     rim = lax.ppermute(rim, "facet", [(i, i + 1) for i in range(devices - 1)])
     blended, energy = blend_inner(sky, wavelet_dual)
-    blended, kept, sent = blend_outer(margins, sky, rim, wavelet_dual, energy, blended)
+    blended, sent = blend_outer(margins, sky, rim, wavelet_dual, energy, blended)
+    sky, sent = lax.optimization_barrier((sky, sent))
     other = lax.ppermute(sent, "chan", [(i, i ^ 1) for i in range(lax.axis_size("chan"))])
-    sky, kept = lax.optimization_barrier((sky, kept))
-    forward_part = degrid(sky, kernel_weights.reshape(1024, 512), tile_index)
-    sent, mine = split(forward_part)
-    forward = mine + lax.ppermute(sent, "facet", facet_pairs(0))
-    kept, forward = lax.optimization_barrier((kept, forward))
+    sent, mine = degrid(sky, kernel_weights.reshape(1024, 512), tile_index)
+    seen = lax.ppermute(sent, "facet", facet_pairs(0))
+    other, mine, seen = lax.optimization_barrier((other, mine, seen))
 
     dual = jnp.transpose(lowrank_dual, (1, 2, 0)).reshape(4, 8, 32, 256)
-    y, part = gram_part(got, dual, kept, other)
-    part, forward = lax.optimization_barrier((part, forward))
-    forward = halving_sum(forward, (3,))
+    y, part = gram_part(got, dual, blended, other)
+    part, mine, seen = lax.optimization_barrier((part, mine, seen))
+    forward = halving_sum(mine + seen, (3,))
     reduced, forward = lax.optimization_barrier((trade(part, "chan"), forward))
-    forward = halving_sum(forward, (1, 2))[None]
+    forward = halving_sum(forward, (1, 2))
     data_next = data_step(data_dual, forward, visibilities, radius_scale)
-    total = trade(sum_copies(reduced), "chan")
+    summed, far = sum_copies(reduced)
+    total = trade(summed, "chan")
     wavelet_next, mixed = finish(
-        total, sparsity_weights, blended, y.reshape(2 * ROOM, 1024, 256), facet_rows * image_side, channels
+        total, far, sparsity_weights, blended, y.reshape(2 * ROOM, 1024, 256), facet_rows * image_side, channels
     )
     lowrank_next = jnp.transpose(mixed.reshape(32, 32, 256), (2, 0, 1))
     return (wavelet_next, lowrank_next, data_next)

time: 97.2 us -> 94.9 us (0.976)
  local copies, waits for them, and re-layouts: 2.59 us -> 0.81 us
  Pallas kernels: 30.8 us -> 32.3 us
  other arithmetic: 1.25 us -> 0.03 us
    unnamed x14 -> x12, local copies, waits for them, and re-layouts: 2.52 us -> 0.73 us
    pallas_call x4, Pallas kernels: 11.4 us -> 12.6 us  [the longest x1 8.75 us: degrid(): pl.pallas_call(degrid_kernel, in_specs=[smem, smem] + [vmem] * 4 + [hbm],...]
  transfers between devices with their start and end apart: 9 -> 9, of which waited for: 7 -> 7; matrix products, arithmetic and copies ran while one was open for 1% -> 0% of each run, Pallas kernels for 20% -> 21%
where the time goes in v4:
time: 94.9 us; the launch traced here: 94.4 us
  Pallas kernels  32.3 us (34%)
  waiting for transfers between devices  31.7 us (33%)
  starting transfers between devices  27.9 us (29%)
  between operations  1.66 us (2%)
    all_to_all x3, starting transfers between devices, trade(): return lax.all_to_all(values, axis, 0, 0, tiled=True)  20.3 us
    all_to_all x3, waiting for transfers between devices, trade(): return lax.all_to_all(values, axis, 0, 0, tiled=True)  16.2 us
    ppermute x3, waiting for transfers between devices, halving_sum(): values = kept + lax.ppermute(sent, 'facet', facet_pairs(bit))  11 us
    pallas_call x1, Pallas kernels, degrid(): pl.pallas_call(degrid_kernel, in_specs=[smem, smem] + [vmem] * 4 + [hbm],...  8.75 us
    pallas_call x1, Pallas kernels, finish(): pl.pallas_call(lambda *refs: finish_kernel(pixels, channels, *refs), in_s...  6.03 us
    pallas_call x1, Pallas kernels, blend_outer(): pl.pallas_call(outer_kernel, in_specs=[pl.BlockSpec(memory_space=pltpu.SM...  5.37 us
    pallas_call x1, Pallas kernels, blend_inner(): pl.pallas_call(inner_kernel, in_specs=[hbm] * 4, out_specs=(hbm, hbm), ou...  5.33 us
    ppermute x1, starting transfers between devices, per_device(): lax.ppermute(sent, 'chan', [(i, i ^ 1) for i in range(lax.axis_size('chan...  3.69 us
  transfers between devices with their start and end apart: 9, of which 7 were waited for; matrix products, arithmetic and copies ran while one was open for 0% of the time, Pallas kernels for 21%

profile of v4, /device:TPU:8, one launch (start us, length us, event | category | flops | bytes accessed | tf_op | source)
XLA Modules:
  0.0 94.4 jit_solution(4591476048312557511)
XLA Ops:
  0.6 2.9 %pack_sky.1 = (f32[16,16,8,128]{3,2,1,0:T(8,128)}, f32[16,8,512]{2,1,0:T(8,128)}) custom-call(f32[16,32,512]{2,1,0:T(8,128)} %sky_ref), custom_call_target="tpu_custom_call" | custom-call | flops 3000000 | bytes 2097152 | tf_op jit(solution)/shard_map/pack_sky/pallas_call | solution.py:112
  3.6 10.3 %all-to-all-start = ((f32[16,16,8,128]{3,2,1,0:T(8,128)}), f32[16,16,8,128]{3,2,1,0:T(8,128)S(1)}, u32[]{:S(2)}, u32[]{:S(2)}) async-start(f32[16,16,8,128]{3,2,1,0:T(8,128)} %get-tuple-element.30), calls=%async_computation | async-start | bytes 2097152 | tf_op jit(solution)/shard_map/all_to_all | solution.py:727
  13.9 0.0 copy-start
  13.9 2.1 %collective-permute-start = (f32[16,8,512]{2,1,0:T(8,128)}, f32[16,8,512]{2,1,0:T(8,128)S(1)}, u32[]{:S(2)}, u32[]{:S(2)}) collective-permute-start(f32[16,8,512]{2,1,0:T(8,128)} %get-tuple-element.32), channel_id=1, source_target_pairs={{0,16},{16,32},{32,48},{48,64},{64,80},{80,96},{96,112},{112,128},... | collective-permute-start | bytes 786440 | tf_op jit(solution)/shard_map/ppermute | solution.py:764
  16.0 5.3 %blend_inner.1 = (f32[24,16,32,512]{3,2,1,0:T(8,128)}, f32[2,16,16,128]{3,2,1,0:T(8,128)}) custom-call(f32[16,32,512]{2,1,0:T(8,128)} %sky_ref, f32[4,16,32,512]{3,2,1,0:T(8,128)} %dual_in.3, bf16[2,192,128]{2,1,0:T(8,128)(2,1)} %constant.47.clone.down_in, bf16[512,256]{1,0:T(8,128)(2,1)} %constant.48.clone.across_in), custom_call_target="tpu_custom_call" | custom-call | flops 2000000000 | bytes 8388608 | tf_op jit(solution)/shard_map/blend_inner/pallas_call | solution.py:500
  21.3 3.1 %collective-permute-done.rim_in = f32[16,8,512]{2,1,0:T(8,128)S(1)} collective-permute-done((f32[16,8,512]{2,1,0:T(8,128)}, f32[16,8,512]{2,1,0:T(8,128)S(1)}, u32[]{:S(2)}, u32[]{:S(2)}) %collective-permute-start) | collective-permute-done | bytes 262176 | tf_op jit(solution)/shard_map/ppermute | solution.py:764
  24.4 0.0 copy-start.4
  24.4 0.7 copy-done.4
  25.1 5.4 %blend_outer.1 = (f32[24,16,32,512]{3,2,1,0:T(8,128)}, f32[16,16,128]{2,1,0:T(8,128)}) custom-call(s32[16]{0:T(128)} %margins_ref.1, f32[16,32,512]{2,1,0:T(8,128)} %sky_ref, f32[16,8,512]{2,1,0:T(8,128)} %copy-done.4, f32[4,16,32,512]{3,2,1,0:T(8,128)} %dual_in.3, bf16[2,64,64]{2,1,0:T(8,128)(2,1)} %constant.49.clone.down_in, ...), custom_call_target="tpu_custom_call", output_to_operand_aliasing={{0}: (7, {})} | custom-call | flops 1000000000 | bytes 4194304 | tf_op jit(solution)/shard_map/blend_outer/pallas_call | solution.py:527
  30.5 0.0 copy-start.2
  30.5 0.0 copy-start.3
  30.5 0.0 copy-start.1
  30.5 3.7 %collective-permute-start.1 = (f32[16,16,128]{2,1,0:T(8,128)}, f32[16,16,128]{2,1,0:T(8,128)S(1)}, u32[]{:S(2)}, u32[]{:S(2)}) collective-permute-start(f32[16,16,128]{2,1,0:T(8,128)} %get-tuple-element.37), channel_id=1, source_target_pairs={{0,1},{1,0},{2,3},{3,2},{4,5},{5,4},{6,7},{7,6},{8,9},{9,8},{10,11... | collective-permute-start | bytes 393224 | tf_op jit(solution)/shard_map/ppermute | solution.py:768
  34.2 8.7 %degrid.1 = (f32[16,1024]{1,0:T(8,128)}, f32[16,1024]{1,0:T(8,128)}) custom-call(s32[1,32]{1,0:T(1,128)} %tile_ref.1, f32[2,16]{1,0:T(2,128)} %constant.53.clone.turn_ref, f32[16,32,512]{2,1,0:T(8,128)} %sky_ref, bf16[128,32]{1,0:T(8,128)(2,1)} %constant.52.clone.shift_ref, f32[96,512]{1,0:T(8,128)} %constant.50.clone.column_ref, ...), custom_call_target="tpu_custom_call" | custom-call | flops 3000000000 | bytes 6291456 | tf_op jit(solution)/shard_map/degrid/pallas_call | solution.py:683
  43.0 0.0 copy-start.5
  43.0 0.1 collective-permute-start.2
  43.1 1.5 %collective-permute-done.2 = f32[16,1024]{1,0:T(8,128)S(1)} collective-permute-done((f32[16,1024]{1,0:T(8,128)}, f32[16,1024]{1,0:T(8,128)S(1)}, u32[]{:S(2)}, u32[]{:S(2)}) %collective-permute-start.2) | collective-permute-done | bytes 65568 | tf_op jit(solution)/shard_map/ppermute | solution.py:770
  44.5 0.0 collective-permute-done.1.other_ref
  44.6 0.0 all-to-all-done
  44.6 0.0 copy-done
  44.6 2.3 %gram_part.1 = (bf16[48,4,8,32,256]{4,3,2,1,0:T(8,128)(2,1)}, f32[16,40,128]{2,1,0:T(8,128)}) custom-call(f32[2048,128]{1,0:T(8,128)S(1)} %bitcast.23, f32[4,8,32,256]{3,2,1,0:T(8,128)S(1)} %bitcast.24, f32[24,16,32,512]{3,2,1,0:T(8,128)} %get-tuple-element.35.blend_in.refs_3_, f32[16,16,128]{2,1,0:T(8,128)S(1)} %collective-permute-done.1.other_ref), custom_call_target="tpu_custom_call" | custom-call | flops 400000000 | bytes 3145728 | tf_op jit(solution)/shard_map/gram_part/pallas_call | solution.py:185
  46.9 6.5 %all-to-all-start.1 = ((f32[16,40,128]{2,1,0:T(8,128)}), f32[16,40,128]{2,1,0:T(8,128)S(1)}, u32[]{:S(2)}, u32[]{:S(2)}) async-start(f32[16,40,128]{2,1,0:T(8,128)} %get-tuple-element.45), calls=%async_computation.1 | async-start | bytes 655360 | tf_op jit(solution)/shard_map/all_to_all | solution.py:727
  53.4 0.0 copy-done.5
  53.4 0.3 collective-permute-start.3
  53.7 4.0 %collective-permute-done.3 = f32[8,1024]{1,0:T(8,128)S(1)} collective-permute-done((f32[8,1024]{1,0:T(8,128)S(1)}, f32[8,1024]{1,0:T(8,128)S(1)}, u32[]{:S(2)}, u32[]{:S(2)}) %collective-permute-start.3) | collective-permute-done | bytes 32800 | tf_op jit(solution)/shard_map/ppermute | solution.py:741
  57.7 10.7 %all-to-all-done.1.got_ref = f32[16,40,128]{2,1,0:T(8,128)S(1)} async-done(((f32[16,40,128]{2,1,0:T(8,128)}), f32[16,40,128]{2,1,0:T(8,128)S(1)}, u32[]{:S(2)}, u32[]{:S(2)}) %all-to-all-start.1) | async-done | bytes 327712 | tf_op jit(solution)/shard_map/all_to_all | solution.py:727
  68.4 0.8 sum_copies.1
  69.2 3.6 %all-to-all-start.2 = ((f32[16,48,128]{2,1,0:T(8,128)}), f32[16,48,128]{2,1,0:T(8,128)S(1)}, u32[]{:S(2)}, u32[]{:S(2)}) async-start(f32[16,48,128]{2,1,0:T(8,128)} %get-tuple-element.49), calls=%async_computation.2 | async-start | bytes 786432 | tf_op jit(solution)/shard_map/all_to_all | solution.py:727
  72.8 0.1 collective-permute-start.4
  72.9 3.8 %collective-permute-done.4 = f32[4,1024]{1,0:T(4,128)S(1)} collective-permute-done((f32[4,1024]{1,0:T(4,128)S(1)}, f32[4,1024]{1,0:T(4,128)S(1)}, u32[]{:S(2)}, u32[]{:S(2)}) %collective-permute-start.4) | collective-permute-done | bytes 16416 | tf_op jit(solution)/shard_map/ppermute | solution.py:741
  76.7 1.4 %collective-permute-start.5 = (f32[2,1024]{1,0:T(2,128)S(1)}, f32[2,1024]{1,0:T(2,128)S(1)}, u32[]{:S(2)}, u32[]{:S(2)}) collective-permute-start(f32[2,1024]{1,0:T(2,128)S(1)} %dynamic-slice_bitcast_fusion.2), channel_id=1, source_target_pairs={{0,64},{16,80},{32,96},{48,112},{64,0},{80,16},{96,32},{112,48},{1... | collective-permute-start | bytes 24584 | tf_op jit(solution)/shard_map/ppermute | solution.py:741
  78.8 3.2 %collective-permute-done.5 = f32[2,1024]{1,0:T(2,128)S(1)} collective-permute-done((f32[2,1024]{1,0:T(2,128)S(1)}, f32[2,1024]{1,0:T(2,128)S(1)}, u32[]{:S(2)}, u32[]{:S(2)}) %collective-permute-start.5) | collective-permute-done | bytes 8224 | tf_op jit(solution)/shard_map/ppermute | solution.py:741
  82.0 0.0 copy-done.2
  82.0 0.0 copy-done.3
  82.0 0.8 data_step.1
  82.8 5.5 %all-to-all-done.2.refs_0_ = f32[16,48,128]{2,1,0:T(8,128)S(1)} async-done(((f32[16,48,128]{2,1,0:T(8,128)}), f32[16,48,128]{2,1,0:T(8,128)S(1)}, u32[]{:S(2)}, u32[]{:S(2)}) %all-to-all-start.2) | async-done | bytes 393248 | tf_op jit(solution)/shard_map/all_to_all | solution.py:727
  88.2 0.0 copy-done.1
  88.2 6.0 %finish.1 = (f32[4,16,32,512]{3,2,1,0:T(8,128)}, f32[1024,256]{1,0:T(8,128)}) custom-call(f32[16,48,128]{2,1,0:T(8,128)S(1)} %all-to-all-done.2.refs_0_, f32[8,128]{1,0:T(8,128)S(1)} %get-tuple-element.50.refs_1_, f32[4,32,512]{2,1,0:T(8,128)S(1)} %copy-done.1, f32[24,16,32,512]{3,2,1,0:T(8,128)} %get-tuple-element.35.blend_in.refs_3_, ...), custom_call_target="tpu_custom_call" | custom-call | flops 2000000000 | bytes 8388608 | tf_op jit(solution)/shard_map/finish/pallas_call | solution.py:330
  (9 shorter events, 0.1 us)
Async XLA Ops:
  3.6 41.0 %all-to-all-start = ((f32[16,16,8,128]{3,2,1,0:T(8,128)}), f32[16,16,8,128]{3,2,1,0:T(8,128)S(1)}, u32[]{:S(2)}, u32[]{:S(2)}) async-start(f32[16,16,8,128]{3,2,1,0:T(8,128)} %get-tuple-element.30), calls=%async_computation | async-start | bytes 2097152 | tf_op jit(solution)/shard_map/all_to_all | solution.py:727
  13.9 30.7 %copy-start = (f32[256,32,32]{0,2,1:T(8,128)S(1)}, f32[256,32,32]{0,2,1:T(8,128)}, u32[]{:S(2)}) copy-start(f32[256,32,32]{0,2,1:T(8,128)} %param.22) | copy-start | bytes 3145732
  13.9 10.5 %collective-permute-start = (f32[16,8,512]{2,1,0:T(8,128)}, f32[16,8,512]{2,1,0:T(8,128)S(1)}, u32[]{:S(2)}, u32[]{:S(2)}) collective-permute-start(f32[16,8,512]{2,1,0:T(8,128)} %get-tuple-element.32), channel_id=1, source_target_pairs={{0,16},{16,32},{32,48},{48,64},{64,80},{80,96},{96,112},{112,128},... | collective-permute-start | bytes 786440 | tf_op jit(solution)/shard_map/ppermute | solution.py:764
  24.4 0.7 copy-start.4
  30.5 51.5 %copy-start.2 = (f32[1,2,1024]{2,1,0:T(2,128)S(1)}, f32[1,2,1024]{2,1,0:T(2,128)}, u32[]{:S(2)}) copy-start(f32[1,2,1024]{2,1,0:T(2,128)} %dual_ref.1) | copy-start | bytes 24580
  30.5 51.5 %copy-start.3 = (f32[1,2,1024]{2,1,0:T(2,128)S(1)}, f32[1,2,1024]{2,1,0:T(2,128)}, u32[]{:S(2)}) copy-start(f32[1,2,1024]{2,1,0:T(2,128)} %vis_ref.1) | copy-start | bytes 24580
  30.5 57.7 %copy-start.1 = (f32[4,32,512]{2,1,0:T(8,128)S(1)}, f32[4,32,512]{2,1,0:T(8,128)}, u32[]{:S(2)}) copy-start(f32[4,32,512]{2,1,0:T(8,128)} %refs_2_.1) | copy-start | bytes 786436
  30.5 14.0 %collective-permute-start.1 = (f32[16,16,128]{2,1,0:T(8,128)}, f32[16,16,128]{2,1,0:T(8,128)S(1)}, u32[]{:S(2)}, u32[]{:S(2)}) collective-permute-start(f32[16,16,128]{2,1,0:T(8,128)} %get-tuple-element.37), channel_id=1, source_target_pairs={{0,1},{1,0},{2,3},{3,2},{4,5},{5,4},{6,7},{7,6},{8,9},{9,8},{10,11... | collective-permute-start | bytes 393224 | tf_op jit(solution)/shard_map/ppermute | solution.py:768
  43.0 10.4 %copy-start.5 = (f32[16,1024]{1,0:T(8,128)S(1)}, f32[16,1024]{1,0:T(8,128)}, u32[]{:S(2)}) copy-start(f32[16,1024]{1,0:T(8,128)} %get-tuple-element.46) | copy-start | bytes 196612
  43.0 1.6 %collective-permute-start.2 = (f32[16,1024]{1,0:T(8,128)}, f32[16,1024]{1,0:T(8,128)S(1)}, u32[]{:S(2)}, u32[]{:S(2)}) collective-permute-start(f32[16,1024]{1,0:T(8,128)} %get-tuple-element.40), channel_id=1, source_target_pairs={{0,16},{16,0},{32,48},{48,32},{64,80},{80,64},{96,112},{112,96},{1... | collective-permute-start | bytes 196616 | tf_op jit(solution)/shard_map/ppermute | solution.py:770
  46.9 21.5 %all-to-all-start.1 = ((f32[16,40,128]{2,1,0:T(8,128)}), f32[16,40,128]{2,1,0:T(8,128)S(1)}, u32[]{:S(2)}, u32[]{:S(2)}) async-start(f32[16,40,128]{2,1,0:T(8,128)} %get-tuple-element.45), calls=%async_computation.1 | async-start | bytes 655360 | tf_op jit(solution)/shard_map/all_to_all | solution.py:727
  53.4 4.2 %collective-permute-start.3 = (f32[8,1024]{1,0:T(8,128)S(1)}, f32[8,1024]{1,0:T(8,128)S(1)}, u32[]{:S(2)}, u32[]{:S(2)}) collective-permute-start(f32[8,1024]{1,0:T(8,128)S(1)} %dynamic-slice_bitcast_fusion), channel_id=1, source_target_pairs={{0,128},{16,144},{32,160},{48,176},{64,192},{80,208},{96,224},{112... | collective-permute-start | bytes 98312 | tf_op jit(solution)/shard_map/ppermute | solution.py:741
  69.2 19.0 %all-to-all-start.2 = ((f32[16,48,128]{2,1,0:T(8,128)}), f32[16,48,128]{2,1,0:T(8,128)S(1)}, u32[]{:S(2)}, u32[]{:S(2)}) async-start(f32[16,48,128]{2,1,0:T(8,128)} %get-tuple-element.49), calls=%async_computation.2 | async-start | bytes 786432 | tf_op jit(solution)/shard_map/all_to_all | solution.py:727
  72.8 3.9 %collective-permute-start.4 = (f32[4,1024]{1,0:T(4,128)S(1)}, f32[4,1024]{1,0:T(4,128)S(1)}, u32[]{:S(2)}, u32[]{:S(2)}) collective-permute-start(f32[4,1024]{1,0:T(4,128)S(1)} %dynamic-slice_bitcast_fusion.1), channel_id=1, source_target_pairs={{0,32},{16,48},{32,0},{48,16},{64,96},{80,112},{96,64},{112,80},{1... | collective-permute-start | bytes 49160 | tf_op jit(solution)/shard_map/ppermute | solution.py:741
  76.7 5.2 %collective-permute-start.5 = (f32[2,1024]{1,0:T(2,128)S(1)}, f32[2,1024]{1,0:T(2,128)S(1)}, u32[]{:S(2)}, u32[]{:S(2)}) collective-permute-start(f32[2,1024]{1,0:T(2,128)S(1)} %dynamic-slice_bitcast_fusion.2), channel_id=1, source_target_pairs={{0,64},{16,80},{32,96},{48,112},{64,0},{80,16},{96,32},{112,48},{1... | collective-permute-start | bytes 24584 | tf_op jit(solution)/shard_map/ppermute | solution.py:741

commit v5 on v4

--- a/solution.py
+++ b/solution.py
@@ -129,10 +129,10 @@
     )(sky)
 
 
-def turn_rows(block, back):
+def turn_rows(block):
     row = lax.broadcasted_iota(jnp.int32, block.shape, 0)
     for bit in (1, 2, 4, 8):
-        turned = pltpu.roll(block, bit if back else 256 - bit, 1)
+        turned = pltpu.roll(block, 256 - bit, 1)
         block = jnp.where((row // bit) % 2 == 1, turned, block)
     return block
 
@@ -172,7 +172,7 @@
         turned = total[16 * peer : 16 * peer + 16, :]
         if peer:
             turned = pltpu.roll(turned, 256 - 16 * peer, 1)
-        gram_ref[peer, :16, :] = turn_rows(turned, False)[:, :128]
+        gram_ref[peer, :16, :] = turn_rows(turned)[:, :128]
     copies.append(pltpu.make_async_copy(gram_ref, part_out.at[:, 16:], sems.at[9]))
     copies[-1].start()
     for copy in copies:
@@ -282,8 +282,8 @@
     blocks = []
     nothing = jnp.zeros((16, 128), f32)
     for peer in range(16):
-        block = turn_rows(jnp.concatenate([got_ref[peer, 32:48, :], nothing], axis=1), True)
-        blocks.append(pltpu.roll(block, 16 * peer, 1) if peer else block)
+        block = jnp.concatenate([got_ref[peer, 32:48, :], nothing], axis=1)
+        blocks.append(pltpu.roll(block, 16 * peer, 1, stride=1, stride_axis=0))
     half = jnp.concatenate(blocks, axis=0)
     far = far_ref[:1, :]
     apart = (cols - rows) % 256

time: 94.9 us -> 94.6 us (level)
  no operation moved by 1% of the time
where the time goes in v5:
time: 94.6 us; the launch traced here: 94.1 us
  Pallas kernels  32 us (34%)
  waiting for transfers between devices  31.7 us (34%)
  starting transfers between devices  27.9 us (29%)
  between operations  1.66 us (2%)
    all_to_all x3, starting transfers between devices, trade(): return lax.all_to_all(values, axis, 0, 0, tiled=True)  20.3 us
    all_to_all x3, waiting for transfers between devices, trade(): return lax.all_to_all(values, axis, 0, 0, tiled=True)  16.2 us
    ppermute x3, waiting for transfers between devices, halving_sum(): values = kept + lax.ppermute(sent, 'facet', facet_pairs(bit))  11 us
    pallas_call x1, Pallas kernels, degrid(): pl.pallas_call(degrid_kernel, in_specs=[smem, smem] + [vmem] * 4 + [hbm],...  8.75 us
    pallas_call x1, Pallas kernels, finish(): pl.pallas_call(lambda *refs: finish_kernel(pixels, channels, *refs), in_s...  5.73 us
    pallas_call x1, Pallas kernels, blend_outer(): pl.pallas_call(outer_kernel, in_specs=[pl.BlockSpec(memory_space=pltpu.SM...  5.37 us
    pallas_call x1, Pallas kernels, blend_inner(): pl.pallas_call(inner_kernel, in_specs=[hbm] * 4, out_specs=(hbm, hbm), ou...  5.33 us
    ppermute x1, starting transfers between devices, per_device(): lax.ppermute(sent, 'chan', [(i, i ^ 1) for i in range(lax.axis_size('chan...  3.69 us
  transfers between devices with their start and end apart: 9, of which 7 were waited for; matrix products, arithmetic and copies ran while one was open for 0% of the time, Pallas kernels for 21%

profile of v5, /device:TPU:8, one launch (start us, length us, event | category | flops | bytes accessed | tf_op | source)
XLA Modules:
  0.0 94.1 jit_solution(5171325624061643099)
XLA Ops:
  0.6 2.9 %pack_sky.1 = (f32[16,16,8,128]{3,2,1,0:T(8,128)}, f32[16,8,512]{2,1,0:T(8,128)}) custom-call(f32[16,32,512]{2,1,0:T(8,128)} %sky_ref), custom_call_target="tpu_custom_call" | custom-call | flops 3000000 | bytes 2097152 | tf_op jit(solution)/shard_map/pack_sky/pallas_call | solution.py:112
  3.6 10.3 %all-to-all-start = ((f32[16,16,8,128]{3,2,1,0:T(8,128)}), f32[16,16,8,128]{3,2,1,0:T(8,128)S(1)}, u32[]{:S(2)}, u32[]{:S(2)}) async-start(f32[16,16,8,128]{3,2,1,0:T(8,128)} %get-tuple-element.30), calls=%async_computation | async-start | bytes 2097152 | tf_op jit(solution)/shard_map/all_to_all | solution.py:727
  13.9 0.0 copy-start
  13.9 2.1 %collective-permute-start = (f32[16,8,512]{2,1,0:T(8,128)}, f32[16,8,512]{2,1,0:T(8,128)S(1)}, u32[]{:S(2)}, u32[]{:S(2)}) collective-permute-start(f32[16,8,512]{2,1,0:T(8,128)} %get-tuple-element.32), channel_id=1, source_target_pairs={{0,16},{16,32},{32,48},{48,64},{64,80},{80,96},{96,112},{112,128},... | collective-permute-start | bytes 786440 | tf_op jit(solution)/shard_map/ppermute | solution.py:764
  16.0 5.3 %blend_inner.1 = (f32[24,16,32,512]{3,2,1,0:T(8,128)}, f32[2,16,16,128]{3,2,1,0:T(8,128)}) custom-call(f32[16,32,512]{2,1,0:T(8,128)} %sky_ref, f32[4,16,32,512]{3,2,1,0:T(8,128)} %dual_in.3, bf16[2,192,128]{2,1,0:T(8,128)(2,1)} %constant.47.clone.down_in, bf16[512,256]{1,0:T(8,128)(2,1)} %constant.48.clone.across_in), custom_call_target="tpu_custom_call" | custom-call | flops 2000000000 | bytes 8388608 | tf_op jit(solution)/shard_map/blend_inner/pallas_call | solution.py:500
  21.3 3.1 %collective-permute-done.rim_in = f32[16,8,512]{2,1,0:T(8,128)S(1)} collective-permute-done((f32[16,8,512]{2,1,0:T(8,128)}, f32[16,8,512]{2,1,0:T(8,128)S(1)}, u32[]{:S(2)}, u32[]{:S(2)}) %collective-permute-start) | collective-permute-done | bytes 262176 | tf_op jit(solution)/shard_map/ppermute | solution.py:764
  24.4 0.0 copy-start.4
  24.4 0.7 copy-done.4
  25.1 5.4 %blend_outer.1 = (f32[24,16,32,512]{3,2,1,0:T(8,128)}, f32[16,16,128]{2,1,0:T(8,128)}) custom-call(s32[16]{0:T(128)} %margins_ref.1, f32[16,32,512]{2,1,0:T(8,128)} %sky_ref, f32[16,8,512]{2,1,0:T(8,128)} %copy-done.4, f32[4,16,32,512]{3,2,1,0:T(8,128)} %dual_in.3, bf16[2,64,64]{2,1,0:T(8,128)(2,1)} %constant.49.clone.down_in, ...), custom_call_target="tpu_custom_call", output_to_operand_aliasing={{0}: (7, {})} | custom-call | flops 1000000000 | bytes 4194304 | tf_op jit(solution)/shard_map/blend_outer/pallas_call | solution.py:527
  30.5 0.0 copy-start.2
  30.5 0.0 copy-start.3
  30.5 0.0 copy-start.1
  30.5 3.7 %collective-permute-start.1 = (f32[16,16,128]{2,1,0:T(8,128)}, f32[16,16,128]{2,1,0:T(8,128)S(1)}, u32[]{:S(2)}, u32[]{:S(2)}) collective-permute-start(f32[16,16,128]{2,1,0:T(8,128)} %get-tuple-element.37), channel_id=1, source_target_pairs={{0,1},{1,0},{2,3},{3,2},{4,5},{5,4},{6,7},{7,6},{8,9},{9,8},{10,11... | collective-permute-start | bytes 393224 | tf_op jit(solution)/shard_map/ppermute | solution.py:768
  34.2 8.7 %degrid.1 = (f32[16,1024]{1,0:T(8,128)}, f32[16,1024]{1,0:T(8,128)}) custom-call(s32[1,32]{1,0:T(1,128)} %tile_ref.1, f32[2,16]{1,0:T(2,128)} %constant.53.clone.turn_ref, f32[16,32,512]{2,1,0:T(8,128)} %sky_ref, bf16[128,32]{1,0:T(8,128)(2,1)} %constant.52.clone.shift_ref, f32[96,512]{1,0:T(8,128)} %constant.50.clone.column_ref, ...), custom_call_target="tpu_custom_call" | custom-call | flops 3000000000 | bytes 6291456 | tf_op jit(solution)/shard_map/degrid/pallas_call | solution.py:683
  43.0 0.0 copy-start.5
  43.0 0.1 collective-permute-start.2
  43.1 1.5 %collective-permute-done.2 = f32[16,1024]{1,0:T(8,128)S(1)} collective-permute-done((f32[16,1024]{1,0:T(8,128)}, f32[16,1024]{1,0:T(8,128)S(1)}, u32[]{:S(2)}, u32[]{:S(2)}) %collective-permute-start.2) | collective-permute-done | bytes 65568 | tf_op jit(solution)/shard_map/ppermute | solution.py:770
  44.5 0.0 collective-permute-done.1.other_ref
  44.6 0.0 all-to-all-done
  44.6 0.0 copy-done
  44.6 2.3 %gram_part.1 = (bf16[48,4,8,32,256]{4,3,2,1,0:T(8,128)(2,1)}, f32[16,40,128]{2,1,0:T(8,128)}) custom-call(f32[2048,128]{1,0:T(8,128)S(1)} %bitcast.23, f32[4,8,32,256]{3,2,1,0:T(8,128)S(1)} %bitcast.24, f32[24,16,32,512]{3,2,1,0:T(8,128)} %get-tuple-element.35.blend_in.refs_3_, f32[16,16,128]{2,1,0:T(8,128)S(1)} %collective-permute-done.1.other_ref), custom_call_target="tpu_custom_call" | custom-call | flops 400000000 | bytes 3145728 | tf_op jit(solution)/shard_map/gram_part/pallas_call | solution.py:185
  46.9 6.5 %all-to-all-start.1 = ((f32[16,40,128]{2,1,0:T(8,128)}), f32[16,40,128]{2,1,0:T(8,128)S(1)}, u32[]{:S(2)}, u32[]{:S(2)}) async-start(f32[16,40,128]{2,1,0:T(8,128)} %get-tuple-element.45), calls=%async_computation.1 | async-start | bytes 655360 | tf_op jit(solution)/shard_map/all_to_all | solution.py:727
  53.4 0.0 copy-done.5
  53.4 0.3 collective-permute-start.3
  53.7 4.0 %collective-permute-done.3 = f32[8,1024]{1,0:T(8,128)S(1)} collective-permute-done((f32[8,1024]{1,0:T(8,128)S(1)}, f32[8,1024]{1,0:T(8,128)S(1)}, u32[]{:S(2)}, u32[]{:S(2)}) %collective-permute-start.3) | collective-permute-done | bytes 32800 | tf_op jit(solution)/shard_map/ppermute | solution.py:741
  57.7 10.7 %all-to-all-done.1.got_ref = f32[16,40,128]{2,1,0:T(8,128)S(1)} async-done(((f32[16,40,128]{2,1,0:T(8,128)}), f32[16,40,128]{2,1,0:T(8,128)S(1)}, u32[]{:S(2)}, u32[]{:S(2)}) %all-to-all-start.1) | async-done | bytes 327712 | tf_op jit(solution)/shard_map/all_to_all | solution.py:727
  68.4 0.8 sum_copies.1
  69.2 3.6 %all-to-all-start.2 = ((f32[16,48,128]{2,1,0:T(8,128)}), f32[16,48,128]{2,1,0:T(8,128)S(1)}, u32[]{:S(2)}, u32[]{:S(2)}) async-start(f32[16,48,128]{2,1,0:T(8,128)} %get-tuple-element.49), calls=%async_computation.2 | async-start | bytes 786432 | tf_op jit(solution)/shard_map/all_to_all | solution.py:727
  72.8 0.1 collective-permute-start.4
  72.9 3.8 %collective-permute-done.4 = f32[4,1024]{1,0:T(4,128)S(1)} collective-permute-done((f32[4,1024]{1,0:T(4,128)S(1)}, f32[4,1024]{1,0:T(4,128)S(1)}, u32[]{:S(2)}, u32[]{:S(2)}) %collective-permute-start.4) | collective-permute-done | bytes 16416 | tf_op jit(solution)/shard_map/ppermute | solution.py:741
  76.7 1.4 %collective-permute-start.5 = (f32[2,1024]{1,0:T(2,128)S(1)}, f32[2,1024]{1,0:T(2,128)S(1)}, u32[]{:S(2)}, u32[]{:S(2)}) collective-permute-start(f32[2,1024]{1,0:T(2,128)S(1)} %dynamic-slice_bitcast_fusion.2), channel_id=1, source_target_pairs={{0,64},{16,80},{32,96},{48,112},{64,0},{80,16},{96,32},{112,48},{1... | collective-permute-start | bytes 24584 | tf_op jit(solution)/shard_map/ppermute | solution.py:741
  78.8 3.2 %collective-permute-done.5 = f32[2,1024]{1,0:T(2,128)S(1)} collective-permute-done((f32[2,1024]{1,0:T(2,128)S(1)}, f32[2,1024]{1,0:T(2,128)S(1)}, u32[]{:S(2)}, u32[]{:S(2)}) %collective-permute-start.5) | collective-permute-done | bytes 8224 | tf_op jit(solution)/shard_map/ppermute | solution.py:741
  82.0 0.0 copy-done.2
  82.0 0.0 copy-done.3
  82.0 0.8 data_step.1
  82.8 5.5 %all-to-all-done.2.refs_0_ = f32[16,48,128]{2,1,0:T(8,128)S(1)} async-done(((f32[16,48,128]{2,1,0:T(8,128)}), f32[16,48,128]{2,1,0:T(8,128)S(1)}, u32[]{:S(2)}, u32[]{:S(2)}) %all-to-all-start.2) | async-done | bytes 393248 | tf_op jit(solution)/shard_map/all_to_all | solution.py:727
  88.2 0.0 copy-done.1
  88.2 5.7 %finish.1 = (f32[4,16,32,512]{3,2,1,0:T(8,128)}, f32[1024,256]{1,0:T(8,128)}) custom-call(f32[16,48,128]{2,1,0:T(8,128)S(1)} %all-to-all-done.2.refs_0_, f32[8,128]{1,0:T(8,128)S(1)} %get-tuple-element.50.refs_1_, f32[4,32,512]{2,1,0:T(8,128)S(1)} %copy-done.1, f32[24,16,32,512]{3,2,1,0:T(8,128)} %get-tuple-element.35.blend_in.refs_3_, ...), custom_call_target="tpu_custom_call" | custom-call | flops 2000000000 | bytes 8388608 | tf_op jit(solution)/shard_map/finish/pallas_call | solution.py:330
  (9 shorter events, 0.1 us)
Async XLA Ops:
  3.6 41.0 %all-to-all-start = ((f32[16,16,8,128]{3,2,1,0:T(8,128)}), f32[16,16,8,128]{3,2,1,0:T(8,128)S(1)}, u32[]{:S(2)}, u32[]{:S(2)}) async-start(f32[16,16,8,128]{3,2,1,0:T(8,128)} %get-tuple-element.30), calls=%async_computation | async-start | bytes 2097152 | tf_op jit(solution)/shard_map/all_to_all | solution.py:727
  13.9 30.7 %copy-start = (f32[256,32,32]{0,2,1:T(8,128)S(1)}, f32[256,32,32]{0,2,1:T(8,128)}, u32[]{:S(2)}) copy-start(f32[256,32,32]{0,2,1:T(8,128)} %param.22) | copy-start | bytes 3145732
  13.9 10.5 %collective-permute-start = (f32[16,8,512]{2,1,0:T(8,128)}, f32[16,8,512]{2,1,0:T(8,128)S(1)}, u32[]{:S(2)}, u32[]{:S(2)}) collective-permute-start(f32[16,8,512]{2,1,0:T(8,128)} %get-tuple-element.32), channel_id=1, source_target_pairs={{0,16},{16,32},{32,48},{48,64},{64,80},{80,96},{96,112},{112,128},... | collective-permute-start | bytes 786440 | tf_op jit(solution)/shard_map/ppermute | solution.py:764
  24.4 0.7 copy-start.4
  30.5 51.5 %copy-start.2 = (f32[1,2,1024]{2,1,0:T(2,128)S(1)}, f32[1,2,1024]{2,1,0:T(2,128)}, u32[]{:S(2)}) copy-start(f32[1,2,1024]{2,1,0:T(2,128)} %dual_ref.1) | copy-start | bytes 24580
  30.5 51.5 %copy-start.3 = (f32[1,2,1024]{2,1,0:T(2,128)S(1)}, f32[1,2,1024]{2,1,0:T(2,128)}, u32[]{:S(2)}) copy-start(f32[1,2,1024]{2,1,0:T(2,128)} %vis_ref.1) | copy-start | bytes 24580
  30.5 57.7 %copy-start.1 = (f32[4,32,512]{2,1,0:T(8,128)S(1)}, f32[4,32,512]{2,1,0:T(8,128)}, u32[]{:S(2)}) copy-start(f32[4,32,512]{2,1,0:T(8,128)} %refs_2_.1) | copy-start | bytes 786436
  30.5 14.0 %collective-permute-start.1 = (f32[16,16,128]{2,1,0:T(8,128)}, f32[16,16,128]{2,1,0:T(8,128)S(1)}, u32[]{:S(2)}, u32[]{:S(2)}) collective-permute-start(f32[16,16,128]{2,1,0:T(8,128)} %get-tuple-element.37), channel_id=1, source_target_pairs={{0,1},{1,0},{2,3},{3,2},{4,5},{5,4},{6,7},{7,6},{8,9},{9,8},{10,11... | collective-permute-start | bytes 393224 | tf_op jit(solution)/shard_map/ppermute | solution.py:768
  43.0 10.4 %copy-start.5 = (f32[16,1024]{1,0:T(8,128)S(1)}, f32[16,1024]{1,0:T(8,128)}, u32[]{:S(2)}) copy-start(f32[16,1024]{1,0:T(8,128)} %get-tuple-element.46) | copy-start | bytes 196612
  43.0 1.6 %collective-permute-start.2 = (f32[16,1024]{1,0:T(8,128)}, f32[16,1024]{1,0:T(8,128)S(1)}, u32[]{:S(2)}, u32[]{:S(2)}) collective-permute-start(f32[16,1024]{1,0:T(8,128)} %get-tuple-element.40), channel_id=1, source_target_pairs={{0,16},{16,0},{32,48},{48,32},{64,80},{80,64},{96,112},{112,96},{1... | collective-permute-start | bytes 196616 | tf_op jit(solution)/shard_map/ppermute | solution.py:770
  46.9 21.5 %all-to-all-start.1 = ((f32[16,40,128]{2,1,0:T(8,128)}), f32[16,40,128]{2,1,0:T(8,128)S(1)}, u32[]{:S(2)}, u32[]{:S(2)}) async-start(f32[16,40,128]{2,1,0:T(8,128)} %get-tuple-element.45), calls=%async_computation.1 | async-start | bytes 655360 | tf_op jit(solution)/shard_map/all_to_all | solution.py:727
  53.4 4.2 %collective-permute-start.3 = (f32[8,1024]{1,0:T(8,128)S(1)}, f32[8,1024]{1,0:T(8,128)S(1)}, u32[]{:S(2)}, u32[]{:S(2)}) collective-permute-start(f32[8,1024]{1,0:T(8,128)S(1)} %dynamic-slice_bitcast_fusion), channel_id=1, source_target_pairs={{0,128},{16,144},{32,160},{48,176},{64,192},{80,208},{96,224},{112... | collective-permute-start | bytes 98312 | tf_op jit(solution)/shard_map/ppermute | solution.py:741
  69.2 19.0 %all-to-all-start.2 = ((f32[16,48,128]{2,1,0:T(8,128)}), f32[16,48,128]{2,1,0:T(8,128)S(1)}, u32[]{:S(2)}, u32[]{:S(2)}) async-start(f32[16,48,128]{2,1,0:T(8,128)} %get-tuple-element.49), calls=%async_computation.2 | async-start | bytes 786432 | tf_op jit(solution)/shard_map/all_to_all | solution.py:727
  72.8 3.9 %collective-permute-start.4 = (f32[4,1024]{1,0:T(4,128)S(1)}, f32[4,1024]{1,0:T(4,128)S(1)}, u32[]{:S(2)}, u32[]{:S(2)}) collective-permute-start(f32[4,1024]{1,0:T(4,128)S(1)} %dynamic-slice_bitcast_fusion.1), channel_id=1, source_target_pairs={{0,32},{16,48},{32,0},{48,16},{64,96},{80,112},{96,64},{112,80},{1... | collective-permute-start | bytes 49160 | tf_op jit(solution)/shard_map/ppermute | solution.py:741
  76.7 5.2 %collective-permute-start.5 = (f32[2,1024]{1,0:T(2,128)S(1)}, f32[2,1024]{1,0:T(2,128)S(1)}, u32[]{:S(2)}, u32[]{:S(2)}) collective-permute-start(f32[2,1024]{1,0:T(2,128)S(1)} %dynamic-slice_bitcast_fusion.2), channel_id=1, source_target_pairs={{0,64},{16,80},{32,96},{48,112},{64,0},{80,16},{96,32},{112,48},{1... | collective-permute-start | bytes 24584 | tf_op jit(solution)/shard_map/ppermute | solution.py:741
